TPU v7x, 32 devices: a whole 2x2x4 slice. The times are simulated.
32 devices in a mesh: section: 2 (over core), seq: 4 (over z), wshard: 4 (over y, x).
Axes of the slice: x: 2, y: 2, z: 4, core: 2. Of those that a mesh axis runs over, the one named last changes fastest.
Arguments:
- inputs: bfloat16 [4, 4, 1024, 1024], P(None, 'wshard', 'seq'), may hold values from -6 to 6
- seq_lengths: int32 [4, 4], replicated, may hold values from 128 to 1024, as said below
- cotangent: bfloat16 [4, 4, 1024, 1024], P(None, 'wshard', 'seq'), may hold values from -6 to 6
- norm_gain: float32 [2, 1024], P('section'), may hold values from 0.5 to 1.5
- in_weight: bfloat16 [2, 1024, 4384], P('section', ('seq', 'wshard')), may hold values from -0.1875 to 0.1875
- conv_weight: float32 [2, 4, 2304], P('section'), may hold values from -3 to 3
- conv_bias: float32 [2, 2304], P('section'), may hold values from -3 to 3
- dt_bias: float32 [2, 32], P('section'), may hold values from -7 to -2.5
- a_log: float32 [2, 32], P('section'), may hold values from -2.5 to 1.2
- d_skip: float32 [2, 32], P('section'), may hold values from 0.5 to 1.5
- gated_gain: float32 [2, 2048], P('section'), may hold values from 0.5 to 1.5
- out_weight: bfloat16 [2, 2048, 1024], P('section', ('seq', 'wshard')), may hold values from -0.125 to 0.125
Outputs:
- acts: bfloat16 [2, 4, 4, 1024, 1024], P('section', None, 'wshard', 'seq')
- grad_in: bfloat16 [2, 4, 4, 1024, 1024], P('section', None, 'wshard', 'seq')
- grad_norm_gain: float32 [2, 1024], P('section')
- grad_in_weight: float32 [2, 1024, 4384], P('section', ('seq', 'wshard'))
- grad_conv_weight: float32 [2, 4, 2304], P('section')
- grad_conv_bias: float32 [2, 2304], P('section')
- grad_dt_bias: float32 [2, 32], P('section')
- grad_a_log: float32 [2, 32], P('section')
- grad_d_skip: float32 [2, 32], P('section')
- grad_gated_gain: float32 [2, 2048], P('section')
- grad_out_weight: float32 [2, 2048, 1024], P('section', ('seq', 'wshard'))
Inputs may be any that keep to these rules, and one draw needn't show every extreme that they name: `seq_lengths`: in each column one entry equals 1024, which row is drawn; the others are at least 128.
All inputs are finite; a program needn't handle non-finite values.
Results may differ from a plain program's by a relative error of at most 0.015.
Values may be sent and summed in bfloat16 or wider, within the bound.
No kernel may reach another device: no remote copies, remote signals or barrier semaphores. Data moves between devices by JAX's collectives and lax.ppermute only.
A program may use at most 384 MiB of HBM per device.

v0:
```python
import jax
import jax.numpy as jnp
from jax import lax
from jax.sharding import PartitionSpec as P

SPAN = 256


epsilon = 1e-05
highest = lax.Precision.HIGHEST


def passed_along(array, axis, by):
    size = lax.axis_size(axis)
    pairs = [(i, i + by) for i in range(size) if 0 <= i + by < size]
    return lax.ppermute(array, axis, pairs)


def norm_rows(values, gain_vec):
    return (
        values * lax.rsqrt(jnp.mean(values * values, axis=-1, keepdims=True) + epsilon) * gain_vec
    )


def causal_conv(signal, kernel, offset):
    taps = kernel.shape[0]
    seq_total = signal.shape[0]
    padded = jnp.pad(signal, ((taps - 1, 0), (0, 0)))
    total = jnp.zeros_like(signal) + offset[None, :]
    for tap_index in range(taps):
        total = total + kernel[tap_index][None, :] * padded[tap_index : tap_index + seq_total]
    return total


def scan_heads(x_heads, dt_heads, decay_rate, b_rows, c_rows, skip_gain):
    seq_total, head_local, head_size = x_heads.shape
    state_width = b_rows.shape[1]
    span_count = seq_total // SPAN
    x_blocks = x_heads.reshape(span_count, SPAN, head_local, head_size)
    b_blocks = b_rows.reshape(span_count, SPAN, state_width)
    c_blocks = c_rows.reshape(span_count, SPAN, state_width)
    dt_blocks = jnp.transpose(dt_heads.reshape(span_count, SPAN, head_local), (0, 2, 1))
    cumulated = jnp.cumsum(dt_blocks * decay_rate[None, :, None], axis=2)
    scores_cb = jnp.einsum("cin,cjn->cij", c_blocks, b_blocks, precision=highest)
    positions = jnp.arange(SPAN)
    lower_mask = (positions[:, None] >= positions[None, :])[None, None]
    diff_decay = cumulated[:, :, :, None] - cumulated[:, :, None, :]
    weighted = jnp.where(lower_mask, jnp.exp(jnp.where(lower_mask, diff_decay, 0.0)), 0.0)
    weighted = weighted * scores_cb[:, None] * dt_blocks[:, :, None, :]
    intra_out = jnp.einsum("chij,cjhp->cihp", weighted, x_blocks, precision=highest)
    last_rate = cumulated[:, :, -1]
    tail_weight = jnp.exp(last_rate[:, :, None] - cumulated) * dt_blocks
    span_states = jnp.einsum(
        "chj,cjn,cjhp->chnp", tail_weight, b_blocks, x_blocks, precision=highest
    )
    totals_run = jnp.cumsum(last_rate, axis=0)
    start_run = totals_run - last_rate
    span_ids = jnp.arange(span_count)
    before_mask = (span_ids[:, None] > span_ids[None, :])[:, :, None]
    gap_decay = start_run[:, None, :] - totals_run[None, :, :]
    carry_decay = jnp.where(before_mask, jnp.exp(jnp.where(before_mask, gap_decay, 0.0)), 0.0)
    entering = jnp.einsum("ckh,khnp->chnp", carry_decay, span_states, precision=highest)
    inter_out = jnp.einsum(
        "cin,chnp,chi->cihp", c_blocks, entering, jnp.exp(cumulated), precision=highest
    )
    result = (intra_out + inter_out).reshape(seq_total, head_local, head_size)
    return result + skip_gain[None, :, None] * x_heads


def head_piece(
    x_local,
    dt_local,
    bc_whole,
    kernel_x,
    offset_x,
    kernel_bc,
    offset_bc,
    dt_offset,
    a_local,
    skip_local,
):
    seq_total = x_local.shape[0]
    head_local = dt_local.shape[1]
    head_size = x_local.shape[1] // head_local
    state_width = bc_whole.shape[1] // 2
    x_conv = jax.nn.silu(causal_conv(x_local, kernel_x, offset_x))
    bc_conv = jax.nn.silu(causal_conv(bc_whole, kernel_bc, offset_bc))
    dt_heads = jax.nn.softplus(dt_local + dt_offset)
    scanned = scan_heads(
        x_conv.reshape(seq_total, head_local, head_size),
        dt_heads,
        -jnp.exp(a_local),
        bc_conv[:, :state_width],
        bc_conv[:, state_width:],
        skip_local,
    )
    return scanned.reshape(seq_total, head_local * head_size)


def gate_norm(scanned, gate_z, gain_vec):
    return norm_rows(scanned * jax.nn.silu(gate_z), gain_vec)


def fetch_weights(in_weight, out_weight):
    whole_in, whole_out = (
        lax.all_gather(in_weight, ("seq", "wshard"), axis=1, tiled=True),
        lax.all_gather(out_weight, ("seq", "wshard"), axis=1, tiled=True),
    )
    return (whole_in[0], whole_out[0])


def send_forward(layer_out):
    return passed_along(layer_out, "section", 1)


def send_back(grad_rows):
    return passed_along(grad_rows, "section", -1)


def forward_tick(hidden_bf, valid_rows, whole_in, whole_out, gain_in, gain_out, head_params):
    kernel_x, offset_x, kernel_bc, offset_bc, dt_offset, a_local, skip_local = head_params
    inner_width = gain_out.shape[0]
    bc_end = 2 * inner_width + kernel_bc.shape[1]
    hidden = hidden_bf.astype(jnp.float32)
    normed_in = norm_rows(hidden, gain_in).astype(jnp.bfloat16)
    projected = jnp.dot(normed_in, whole_in, preferred_element_type=jnp.float32)
    gate_z = projected[:, :inner_width]
    x_part = projected[:, inner_width : 2 * inner_width].astype(jnp.bfloat16)
    bc_part = projected[:, 2 * inner_width : bc_end].astype(jnp.bfloat16)
    dt_part = projected[:, bc_end:].astype(jnp.bfloat16)
    x_local, dt_local = (
        lax.all_to_all(x_part, "seq", split_axis=1, concat_axis=0, tiled=True),
        lax.all_to_all(dt_part, "seq", split_axis=1, concat_axis=0, tiled=True),
    )
    bc_whole = lax.all_gather(bc_part, "seq", axis=0, tiled=True)
    scanned = head_piece(
        x_local.astype(jnp.float32),
        dt_local.astype(jnp.float32),
        bc_whole.astype(jnp.float32),
        kernel_x,
        offset_x,
        kernel_bc,
        offset_bc,
        dt_offset,
        a_local,
        skip_local,
    )
    scanned_rows = lax.all_to_all(
        scanned.astype(jnp.bfloat16), "seq", split_axis=0, concat_axis=1, tiled=True
    )
    normed_out = gate_norm(scanned_rows.astype(jnp.float32), gate_z, gain_out).astype(jnp.bfloat16)
    branch = jnp.dot(normed_out, whole_out, preferred_element_type=jnp.float32)
    layer_out = (valid_rows * (hidden + branch)).astype(jnp.bfloat16)
    return (
        layer_out,
        (hidden, normed_in, gate_z, x_local, dt_local, bc_whole, scanned_rows, normed_out),
    )


def backward_tick(
    grad_rows,
    saved,
    valid_rows,
    whole_in,
    whole_out,
    gain_in,
    gain_out,
    head_params,
    chan_start,
    head_start,
    head_count,
):
    hidden, normed_in, gate_z, x_local, dt_local, bc_whole, scanned_rows, normed_out = saved
    kernel_x, offset_x, kernel_bc, offset_bc, dt_offset, a_local, skip_local = head_params
    inner_width = gain_out.shape[0]
    masked = grad_rows * valid_rows
    grad_branch = masked.astype(jnp.bfloat16)
    grad_wout = jnp.einsum("td,te->de", normed_out, grad_branch, preferred_element_type=jnp.float32)
    grad_normed = jnp.einsum(
        "te,de->td", grad_branch, whole_out, preferred_element_type=jnp.float32
    )
    _, pull_gate = jax.vjp(gate_norm, scanned_rows.astype(jnp.float32), gate_z, gain_out)
    grad_scanned, grad_gate, grad_gain_out = pull_gate(grad_normed)
    grad_heads = lax.all_to_all(
        grad_scanned.astype(jnp.bfloat16), "seq", split_axis=1, concat_axis=0, tiled=True
    )
    _, pull_head = jax.vjp(
        head_piece,
        x_local.astype(jnp.float32),
        dt_local.astype(jnp.float32),
        bc_whole.astype(jnp.float32),
        kernel_x,
        offset_x,
        kernel_bc,
        offset_bc,
        dt_offset,
        a_local,
        skip_local,
    )
    (
        grad_x,
        grad_dt,
        grad_bc,
        grad_kx,
        grad_ox,
        grad_kbc,
        grad_obc,
        grad_dto,
        grad_alog,
        grad_skip,
    ) = pull_head(grad_heads.astype(jnp.float32))
    x_back, dt_back = (
        lax.all_to_all(grad_x.astype(jnp.bfloat16), "seq", split_axis=0, concat_axis=1, tiled=True),
        lax.all_to_all(
            grad_dt.astype(jnp.bfloat16), "seq", split_axis=0, concat_axis=1, tiled=True
        ),
    )
    bc_back = lax.psum_scatter(grad_bc.astype(jnp.bfloat16), "seq", scatter_dimension=0, tiled=True)
    grad_proj = jnp.concatenate([grad_gate.astype(jnp.bfloat16), x_back, bc_back, dt_back], axis=1)
    grad_win = jnp.einsum("td,tp->dp", normed_in, grad_proj, preferred_element_type=jnp.float32)
    grad_normed_in = jnp.einsum(
        "tp,dp->td", grad_proj, whole_in, preferred_element_type=jnp.float32
    )
    _, pull_norm = jax.vjp(norm_rows, hidden, gain_in)
    grad_hidden, grad_gain_in = pull_norm(grad_normed_in)
    grad_total = masked + grad_hidden
    kernel_full = jnp.concatenate(
        [
            lax.dynamic_update_slice_in_dim(
                jnp.zeros((kernel_x.shape[0], inner_width), jnp.float32), grad_kx, chan_start, 1
            ),
            grad_kbc,
        ],
        axis=1,
    )
    offset_full = jnp.concatenate(
        [
            lax.dynamic_update_slice_in_dim(
                jnp.zeros((inner_width,), jnp.float32), grad_ox, chan_start, 0
            ),
            grad_obc,
        ],
        axis=0,
    )
    head_zeros = jnp.zeros((head_count,), jnp.float32)
    dto_full = lax.dynamic_update_slice_in_dim(head_zeros, grad_dto, head_start, 0)
    alog_full = lax.dynamic_update_slice_in_dim(head_zeros, grad_alog, head_start, 0)
    skip_full = lax.dynamic_update_slice_in_dim(head_zeros, grad_skip, head_start, 0)
    return (
        grad_total,
        (
            grad_win,
            grad_wout,
            kernel_full,
            offset_full,
            dto_full,
            alog_full,
            skip_full,
            grad_gain_in,
            grad_gain_out,
        ),
    )


def local(
    inputs,
    seq_lengths,
    cotangent,
    norm_gain,
    in_weight,
    conv_weight,
    conv_bias,
    dt_bias,
    a_log,
    d_skip,
    gated_gain,
    out_weight,
):
    section = lax.axis_index("section")
    seat = lax.axis_index("seq")
    lane_index = lax.axis_index("wshard")
    groups = lax.axis_size("seq")
    micro_count = inputs.shape[0]
    tok_rows = inputs.shape[2]
    model_width = inputs.shape[3]
    inner_width = gated_gain.shape[1]
    head_count = dt_bias.shape[1]
    head_local = head_count // groups
    chan_local = inner_width // groups
    chan_start = seat * chan_local
    head_start = seat * head_local
    gain_in = norm_gain[0]
    gain_out = gated_gain[0]
    kernel_all = conv_weight[0]
    offset_all = conv_bias[0]
    head_params = (
        lax.dynamic_slice_in_dim(kernel_all[:, :inner_width], chan_start, chan_local, 1),
        lax.dynamic_slice_in_dim(offset_all[:inner_width], chan_start, chan_local, 0),
        kernel_all[:, inner_width:],
        offset_all[inner_width:],
        lax.dynamic_slice_in_dim(dt_bias[0], head_start, head_local, 0),
        lax.dynamic_slice_in_dim(a_log[0], head_start, head_local, 0),
        lax.dynamic_slice_in_dim(d_skip[0], head_start, head_local, 0),
    )
    my_lengths = lax.dynamic_index_in_dim(seq_lengths, lane_index, 1, keepdims=False)
    positions = seat * tok_rows + jnp.arange(tok_rows)
    valid_all = (positions[None, :] < my_lengths[:, None]).astype(jnp.float32)
    first_rows = inputs[:, 0]
    cot_rows = cotangent[:, 0]
    whole_in, whole_out = fetch_weights(in_weight, out_weight)
    received = jnp.zeros((tok_rows, model_width), jnp.bfloat16)
    kept_list = []
    produced = []
    for tick_index in range(micro_count + 1):
        current = jnp.clip(tick_index - section, 0, micro_count - 1)
        feed = jnp.where(
            section == 0, lax.dynamic_index_in_dim(first_rows, current, 0, keepdims=False), received
        )
        valid_rows = lax.dynamic_index_in_dim(valid_all, current, 0, keepdims=False)[:, None]
        layer_out, saved = forward_tick(
            feed, valid_rows, whole_in, whole_out, gain_in, gain_out, head_params
        )
        received = send_forward(layer_out)
        kept_list.append(saved)
        produced.append(layer_out)
    acts = lax.dynamic_slice_in_dim(jnp.stack(produced), section, micro_count, 0)
    grad_recv = jnp.zeros((tok_rows, model_width), jnp.bfloat16)
    acc_in = jnp.zeros(whole_in.shape, jnp.float32)
    acc_out = jnp.zeros(whole_out.shape, jnp.float32)
    small_acc = None
    returned = []
    for back_index in range(micro_count + 1):
        fwd_tick = micro_count - back_index
        current_raw = micro_count - back_index - section
        live_flag = ((current_raw >= 0) & (current_raw < micro_count)).astype(jnp.float32)
        current = jnp.clip(current_raw, 0, micro_count - 1)
        valid_rows = lax.dynamic_index_in_dim(valid_all, current, 0, keepdims=False)[:, None]
        cot_here = lax.dynamic_index_in_dim(cot_rows, current, 0, keepdims=False).astype(
            jnp.float32
        )
        grad_rows = jnp.where(section == 1, cot_here, grad_recv.astype(jnp.float32)) * live_flag
        saved = kept_list[fwd_tick]
        grad_total, grads = backward_tick(
            grad_rows,
            saved,
            valid_rows,
            whole_in,
            whole_out,
            gain_in,
            gain_out,
            head_params,
            chan_start,
            head_start,
            head_count,
        )
        grad_bf = grad_total.astype(jnp.bfloat16)
        grad_recv = send_back(grad_bf)
        returned.append(grad_bf)
        acc_in = acc_in + grads[0]
        acc_out = acc_out + grads[1]
        if small_acc is None:
            small_acc = grads[2:]
        else:
            small_acc = tuple(
                (total_part + new_part for total_part, new_part in zip(small_acc, grads[2:]))
            )
    shard_in, shard_out = (
        lax.psum_scatter(acc_in[None], ("seq", "wshard"), scatter_dimension=1, tiled=True),
        lax.psum_scatter(acc_out[None], ("seq", "wshard"), scatter_dimension=1, tiled=True),
    )
    kernel_sum, offset_sum, dto_sum, alog_sum, skip_sum, gain_in_sum, gain_out_sum = lax.psum(
        (
            small_acc[0],
            small_acc[1],
            small_acc[2],
            small_acc[3],
            small_acc[4],
            small_acc[5],
            small_acc[6],
        ),
        ("seq", "wshard"),
    )
    grad_rows_all = lax.dynamic_slice_in_dim(jnp.stack(returned[::-1]), section, micro_count, 0)
    return (
        acts[None, :, None],
        grad_rows_all[None, :, None],
        gain_in_sum[None],
        shard_in,
        kernel_sum[None],
        offset_sum[None],
        dto_sum[None],
        alog_sum[None],
        skip_sum[None],
        gain_out_sum[None],
        shard_out,
    )


def solution(mesh):
    return jax.shard_map(
        local,
        mesh=mesh,
        in_specs=(
            P(None, "wshard", "seq", None),
            P(),
            P(None, "wshard", "seq", None),
            P("section", None),
            P("section", ("seq", "wshard"), None),
            P("section", None, None),
            P("section", None),
            P("section", None),
            P("section", None),
            P("section", None),
            P("section", None),
            P("section", ("seq", "wshard"), None),
        ),
        out_specs=(
            P("section", None, "wshard", "seq", None),
            P("section", None, "wshard", "seq", None),
            P("section", None),
            P("section", ("seq", "wshard"), None),
            P("section", None, None),
            P("section", None),
            P("section", None),
            P("section", None),
            P("section", None),
            P("section", None),
            P("section", ("seq", "wshard"), None),
        ),
        check_vma=False,
    )
```

profile of v0, /device:TPU:0, one launch (start us, length us, event | category | flops | bytes accessed | tf_op | source)
XLA Modules:
  0.0 2566.8 jit_solution(16803684065987407807)
XLA Ops:
  16.6 116.9 %all-gather.3.cloned.1.call-done = bf16[1,1024,4384]{2,1,0:T(8,128)(2,1)} async-done(((bf16[1,64,4384]{2,1,0:T(8,128)(2,1)}), bf16[1,1024,4384]{2,1,0:T(8,128)(2,1)}) %all-gather.3.cloned.1.call-update) | async-done | bytes 8978448 | tf_op jit(solution)/shard_map/all_gather | solution.py:106
  143.0 18.2 all_gather.22
  186.0 37.2 %all-to-all-done = bf16[256,4,512]{2,0,1:T(8,128)(2,1)S(1)} async-done(((bf16[256,4,512]{2,0,1:T(8,128)(2,1)}), bf16[256,4,512]{2,0,1:T(8,128)(2,1)S(1)}, u32[]{:S(2)}, u32[]{:S(2)}) %all-to-all-start) | async-done | bytes 1048608 | tf_op jit(solution)/shard_map/all_to_all | solution.py:132
  263.3 13.6 all-to-all-start.2
  277.8 21.7 all-to-all-done.2
  325.1 16.2 all_gather.24
  420.1 27.4 %all_to_all.465 = bf16[4,256,512]{2,1,0:T(8,128)(2,1)S(1)} all-to-all(bf16[4,256,512]{2,1,0:T(8,128)(2,1)S(1)} %bitcast.1469), channel_id=1, replica_groups=mesh['section'=2,'seq'=4,'wshard'=4] {'seq'}, dimensions={0} | all-to-all | bytes 2097152 | tf_op jit(solution)/shard_map/all_to_all | solution.py:148
  471.7 16.2 all_gather.25
  566.8 27.4 %all_to_all.466 = bf16[4,256,512]{2,1,0:T(8,128)(2,1)S(1)} all-to-all(bf16[4,256,512]{2,1,0:T(8,128)(2,1)S(1)} %bitcast.1471), channel_id=1, replica_groups=mesh['section'=2,'seq'=4,'wshard'=4] {'seq'}, dimensions={0} | all-to-all | bytes 2097152 | tf_op jit(solution)/shard_map/all_to_all | solution.py:148
  618.3 16.2 all_gather.26
  660.2 12.8 all-to-all-done.9
  713.5 27.4 %all_to_all.467 = bf16[4,256,512]{2,1,0:T(8,128)(2,1)S(1)} all-to-all(bf16[4,256,512]{2,1,0:T(8,128)(2,1)S(1)} %bitcast.1473), channel_id=1, replica_groups=mesh['section'=2,'seq'=4,'wshard'=4] {'seq'}, dimensions={0} | all-to-all | bytes 2097152 | tf_op jit(solution)/shard_map/all_to_all | solution.py:148
  765.9 16.2 all_gather.27
  868.5 24.8 all-to-all-done.14
  918.8 20.2 all-to-all-done.15
  1051.8 13.0 all-to-all-done.16
  1105.8 21.3 all-to-all-done.18
  1228.6 15.2 all-to-all-done.19
  1283.3 23.1 all-to-all-done.21
  1406.7 15.2 all-to-all-done.22
  1461.4 23.1 all-to-all-done.24
  1586.2 14.3 all-to-all-done.25
  1650.0 13.8 fusion.644
  1663.8 13.9 fusion.643
  1776.8 22.3 all-to-all-done.28
  1802.5 13.9 fusion.642
  1818.0 31.4 %add_bitcast_fusion = f32[1,1024,4384]{1,2,0:T(8,128)} fusion(f32[1024,4384]{0,1:T(8,128)} %fusion.642, f32[1024,4384]{0,1:T(8,128)} %fusion.643, f32[1024,4384]{0,1:T(8,128)} %fusion.645, f32[1024,4384]{0,1:T(8,128)} %fusion.644, f32[256]{0:T(256)S(1)} %copy-done.232, f32[1024]{0:T(1024)S(1)} %bitcast.1532, bf16[256,32]{0,1:T(8,128)(2,1)S(1)} %bitcast.1678, ...), kind=kOutput, calls=%fused_computation | convolution fusion | flops 2326724608 | bytes 92558344 | tf_op jit(solution)/shard_map/td,tp->dp/dot_general | solution.py:220
  1849.5 37.5 %copy.1318 = f32[1,1024,4384]{2,0,1:T(1,128)} copy(f32[1,1024,4384]{1,2,0:T(8,128)} %add_bitcast_fusion) | data formatting | bytes 35913728 | tf_op jit(solution)/shard_map/broadcast_in_dim | solution.py:368
  1910.2 15.8 add_bitcast_fusion.1
  1958.8 79.9 %all-reduce.106 = (f32[1,1024]{1,0:T(1,128)}, f32[1,4,2304]{2,1,0:T(4,128)}, f32[1,2304]{1,0:T(1,128)}, f32[1,32]{1,0:T(1,128)}, f32[1,32]{1,0:T(1,128)}, /*index=5*/f32[1,32]{1,0:T(1,128)}, f32[1,2048]{1,0:T(1,128)}) all-reduce(f32[1,1024]{1,0:T(1,128)S(1)} %bitcast.1688, ...), channel_id=1, replica_groups=mesh['section'=2,'seq'=4,'wshard'=4] {'seq','wshard'}, use_global_device_ids=true, to_apply=%region_110.112 | all-reduce | flops 14688 | bytes 117504 | tf_op jit(solution)/shard_map/psum | solution.py:371
  2045.6 334.3 %all-reduce.109.cloned.1.call-done = f32[1,1024,4384]{2,0,1:T(1,128)} async-done(((f32[1,1024,4384]{2,0,1:T(1,128)}), f32[1,1024,4384]{2,0,1:T(1,128)}) %all-reduce.109.cloned.1.call-update) | async-done | bytes 17956880
  2382.4 177.5 %reduce-scatter.17.cloned.1.call-done = f32[1,128,1024]{2,1,0:T(8,128)} async-done(((f32[1,2048,1024]{2,1,0:T(8,128)}), f32[1,128,1024]{2,1,0:T(8,128)}) %reduce-scatter.17.cloned.1.call-update) | async-done | bytes 524304 | tf_op jit(solution)/shard_map/reduce_scatter | solution.py:369
  (1388 shorter events, 1269.2 us)
Async XLA Ops:
  7.2 126.2 %all-gather.3.cloned.1.call-start = ((), (), s32[]{:S(2)}) async-start(), calls=%async_computation.36 | async-start | bytes 9748480 | tf_op jit(solution)/shard_map/all_gather | solution.py:106
  7.9 296.7 %all-gather.5.cloned.1.call-start = ((), (), s32[]{:S(2)}) async-start(), calls=%async_computation.37 | async-start | bytes 4456448 | tf_op jit(solution)/shard_map/all_gather | solution.py:107
  162.8 10.4 all-to-all-start.1
  173.2 50.0 %all-to-all-start = ((bf16[256,4,512]{2,0,1:T(8,128)(2,1)}), bf16[256,4,512]{2,0,1:T(8,128)(2,1)S(1)}, u32[]{:S(2)}, u32[]{:S(2)}) async-start(bf16[256,4,512]{2,0,1:T(8,128)(2,1)} %copy.1043), calls=%async_computation | async-start | bytes 2097152 | tf_op jit(solution)/shard_map/all_to_all | solution.py:132
  263.3 36.2 %all-to-all-start.2 = ((bf16[4,256,512]{2,1,0:T(8,128)(2,1)}), bf16[4,256,512]{2,1,0:T(8,128)(2,1)S(1)}, u32[]{:S(2)}, u32[]{:S(2)}) async-start(bf16[4,256,512]{2,1,0:T(8,128)(2,1)} %bitcast.1460), calls=%async_computation.2 | async-start | bytes 2097152 | tf_op jit(solution)/shard_map/all_to_all | solution.py:148
  341.3 10.4 all-to-all-start.4
  351.8 28.0 %all-to-all-start.3 = ((bf16[256,4,512]{2,0,1:T(8,128)(2,1)}), bf16[256,4,512]{2,0,1:T(8,128)(2,1)S(1)}, u32[]{:S(2)}, u32[]{:S(2)}) async-start(bf16[256,4,512]{2,0,1:T(8,128)(2,1)} %copy.1061), calls=%async_computation.3 | async-start | bytes 2097152 | tf_op jit(solution)/shard_map/all_to_all | solution.py:132
  488.0 10.5 all-to-all-start.7
  498.5 28.0 %all-to-all-start.6 = ((bf16[256,4,512]{2,0,1:T(8,128)(2,1)}), bf16[256,4,512]{2,0,1:T(8,128)(2,1)S(1)}, u32[]{:S(2)}, u32[]{:S(2)}) async-start(bf16[256,4,512]{2,0,1:T(8,128)(2,1)} %copy.1079), calls=%async_computation.6 | async-start | bytes 2097152 | tf_op jit(solution)/shard_map/all_to_all | solution.py:132
  634.5 10.4 all-to-all-start.10
  645.0 28.0 %all-to-all-start.9 = ((bf16[256,4,512]{2,0,1:T(8,128)(2,1)}), bf16[256,4,512]{2,0,1:T(8,128)(2,1)S(1)}, u32[]{:S(2)}, u32[]{:S(2)}) async-start(bf16[256,4,512]{2,0,1:T(8,128)(2,1)} %copy.1097), calls=%async_computation.9 | async-start | bytes 2097152 | tf_op jit(solution)/shard_map/all_to_all | solution.py:132
  783.0 10.5 all-to-all-start.13
  793.5 28.0 %all-to-all-start.12 = ((bf16[256,4,512]{2,0,1:T(8,128)(2,1)}), bf16[256,4,512]{2,0,1:T(8,128)(2,1)S(1)}, u32[]{:S(2)}, u32[]{:S(2)}) async-start(bf16[256,4,512]{2,0,1:T(8,128)(2,1)} %copy.1115), calls=%async_computation.12 | async-start | bytes 2097152 | tf_op jit(solution)/shard_map/all_to_all | solution.py:132
  864.8 28.5 %all-to-all-start.14 = ((bf16[4,256,512]{2,1,0:T(8,128)(2,1)}), bf16[4,256,512]{2,1,0:T(8,128)(2,1)S(1)}, u32[]{:S(2)}, u32[]{:S(2)}) async-start(bf16[4,256,512]{2,1,0:T(8,128)(2,1)} %bitcast.1461), calls=%async_computation.14 | async-start | bytes 2097152 | tf_op jit(solution)/shard_map/all_to_all | solution.py:148
  910.3 28.7 %all-to-all-start.15 = ((bf16[256,4,512]{2,0,1:T(8,128)(2,1)}), bf16[256,4,512]{2,0,1:T(8,128)(2,1)S(1)}, u32[]{:S(2)}, u32[]{:S(2)}) async-start(bf16[256,4,512]{2,0,1:T(8,128)(2,1)} %copy.1134), calls=%async_computation.15 | async-start | bytes 2097152 | tf_op jit(solution)/shard_map/all_to_all | solution.py:184
  1026.8 38.0 %all-to-all-start.16 = ((bf16[4,256,512]{2,1,0:T(8,128)(2,1)}), bf16[4,256,512]{2,1,0:T(8,128)(2,1)}, u32[]{:S(2)}, u32[]{:S(2)}) async-start(bf16[4,256,512]{2,1,0:T(8,128)(2,1)} %bitcast.1459), calls=%async_computation.16 | async-start | bytes 2097152 | tf_op jit(solution)/shard_map/all_to_all | solution.py:213
  1031.1 42.5 %reduce-scatter.7.cloned.1.call-start = ((), (), s32[]{:S(2)}) async-start(), calls=%async_computation.38 | async-start | bytes 655360 | tf_op jit(solution)/shard_map/reduce_scatter | solution.py:218
  1097.3 29.8 %all-to-all-start.18 = ((bf16[256,4,512]{2,0,1:T(8,128)(2,1)}), bf16[256,4,512]{2,0,1:T(8,128)(2,1)S(1)}, u32[]{:S(2)}, u32[]{:S(2)}) async-start(bf16[256,4,512]{2,0,1:T(8,128)(2,1)} %copy.1171), calls=%async_computation.19 | async-start | bytes 2097152 | tf_op jit(solution)/shard_map/all_to_all | solution.py:184
  1205.6 38.2 %all-to-all-start.19 = ((bf16[4,256,512]{2,1,0:T(8,128)(2,1)}), bf16[4,256,512]{2,1,0:T(8,128)(2,1)}, u32[]{:S(2)}, u32[]{:S(2)}) async-start(bf16[4,256,512]{2,1,0:T(8,128)(2,1)} %bitcast.252), calls=%async_computation.20 | async-start | bytes 2097152 | tf_op jit(solution)/shard_map/all_to_all | solution.py:213
  1209.9 42.8 %reduce-scatter.9.cloned.1.call-start = ((), (), s32[]{:S(2)}) async-start(), calls=%async_computation.39 | async-start | bytes 655360 | tf_op jit(solution)/shard_map/reduce_scatter | solution.py:218
  1276.5 29.9 %all-to-all-start.21 = ((bf16[256,4,512]{2,0,1:T(8,128)(2,1)}), bf16[256,4,512]{2,0,1:T(8,128)(2,1)S(1)}, u32[]{:S(2)}, u32[]{:S(2)}) async-start(bf16[256,4,512]{2,0,1:T(8,128)(2,1)} %copy.1208), calls=%async_computation.23 | async-start | bytes 2097152 | tf_op jit(solution)/shard_map/all_to_all | solution.py:184
  1383.7 38.2 %all-to-all-start.22 = ((bf16[4,256,512]{2,1,0:T(8,128)(2,1)}), bf16[4,256,512]{2,1,0:T(8,128)(2,1)}, u32[]{:S(2)}, u32[]{:S(2)}) async-start(bf16[4,256,512]{2,1,0:T(8,128)(2,1)} %bitcast.306), calls=%async_computation.24 | async-start | bytes 2097152 | tf_op jit(solution)/shard_map/all_to_all | solution.py:213
  1388.0 42.8 %reduce-scatter.11.cloned.1.call-start = ((), (), s32[]{:S(2)}) async-start(), calls=%async_computation.40 | async-start | bytes 655360 | tf_op jit(solution)/shard_map/reduce_scatter | solution.py:218
  1454.6 29.9 %all-to-all-start.24 = ((bf16[256,4,512]{2,0,1:T(8,128)(2,1)}), bf16[256,4,512]{2,0,1:T(8,128)(2,1)S(1)}, u32[]{:S(2)}, u32[]{:S(2)}) async-start(bf16[256,4,512]{2,0,1:T(8,128)(2,1)} %copy.1245), calls=%async_computation.27 | async-start | bytes 2097152 | tf_op jit(solution)/shard_map/all_to_all | solution.py:184
  1562.3 38.2 %all-to-all-start.25 = ((bf16[4,256,512]{2,1,0:T(8,128)(2,1)}), bf16[4,256,512]{2,1,0:T(8,128)(2,1)}, u32[]{:S(2)}, u32[]{:S(2)}) async-start(bf16[4,256,512]{2,1,0:T(8,128)(2,1)} %bitcast.360), calls=%async_computation.28 | async-start | bytes 2097152 | tf_op jit(solution)/shard_map/all_to_all | solution.py:213
  1566.5 43.0 %reduce-scatter.13.cloned.1.call-start = ((), (), s32[]{:S(2)}) async-start(), calls=%async_computation.41 | async-start | bytes 655360 | tf_op jit(solution)/shard_map/reduce_scatter | solution.py:218
  1634.5 43.2 %all-to-all-start.27 = ((bf16[256,4,512]{2,0,1:T(8,128)(2,1)}), bf16[256,4,512]{2,0,1:T(8,128)(2,1)S(1)}, u32[]{:S(2)}, u32[]{:S(2)}) async-start(bf16[256,4,512]{2,0,1:T(8,128)(2,1)} %copy.1282), calls=%async_computation.31 | async-start | bytes 2097152 | tf_op jit(solution)/shard_map/all_to_all | solution.py:184
  1759.9 39.2 %all-to-all-start.28 = ((bf16[4,256,512]{2,1,0:T(8,128)(2,1)}), bf16[4,256,512]{2,1,0:T(8,128)(2,1)}, u32[]{:S(2)}, u32[]{:S(2)}) async-start(bf16[4,256,512]{2,1,0:T(8,128)(2,1)} %bitcast.414), calls=%async_computation.32 | async-start | bytes 2097152 | tf_op jit(solution)/shard_map/all_to_all | solution.py:213
  1765.1 52.9 %reduce-scatter.15.cloned.1.call-start = ((), (), s32[]{:S(2)}) async-start(), calls=%async_computation.42 | async-start | bytes 655360 | tf_op jit(solution)/shard_map/reduce_scatter | solution.py:218
  1799.1 18.9 all-to-all-start.29
  1802.4 577.6 %all-reduce.109.cloned.1.call-start = ((), (), s32[]{:S(2)}) async-start(), calls=%async_computation.44 | async-start | bytes 36700160
  1887.0 672.8 %reduce-scatter.17.cloned.1.call-start = ((), (), s32[]{:S(2)}) async-start(), calls=%async_computation.43 | async-start | bytes 8912896 | tf_op jit(solution)/shard_map/reduce_scatter | solution.py:369
  (345 other events, 5339.1 us)
Sparse Core Ops, SparseCore 0:
  10.8 122.5 all-gather.2
  136.2 90.4 all-gather.4
  1035.5 27.7 reduce-scatter.6
  1214.4 27.7 reduce-scatter.8
  1392.6 27.7 reduce-scatter.10
  1571.1 27.7 reduce-scatter.12
  1774.9 23.9 reduce-scatter.14
  1887.1 492.7 all-reduce.108
  2382.9 176.8 reduce-scatter.16
where the time goes:
time: 2580 us; the launch traced here: 2570 us
  waiting for transfers between devices  950 us (37%)
  matrix products  613 us (24%)
  local copies, waits for them, and re-layouts  307 us (12%)
  other arithmetic  303 us (12%)
  blocking collectives  245 us (9%)
  starting transfers between devices  129 us (5%)
    unnamed x10, waiting for transfers between devices  336 us
    reduce_scatter x1, waiting for transfers between devices, local(): lax.psum_scatter(acc_out[None], ('seq', 'wshard'), scatter_dimension=1, t...  177 us
    dot_general x15, matrix products, scan_heads(): jnp.einsum('chij,cjhp->cihp', weighted, x_blocks, precision=highest)  148 us
    all_gather x1, waiting for transfers between devices, fetch_weights(): lax.all_gather(in_weight, ('seq', 'wshard'), axis=1, tiled=True)  117 us
    another operation x45, other arithmetic  102 us
    all_to_all x5, waiting for transfers between devices, backward_tick(): lax.all_to_all(grad_scanned.astype(jnp.bfloat16), 'seq', split_axis=1, co...  87.6 us
    dot_general x5, matrix products, backward_tick(): jnp.einsum('td,tp->dp', normed_in, grad_proj, preferred_element_type=jnp....  83.5 us
    all_gather x5, blocking collectives, forward_tick(): bc_whole = lax.all_gather(bc_part, 'seq', axis=0, tiled=True)  82.9 us
  transfers between devices with their start and end apart: 44, of which 31 were waited for; matrix products, arithmetic and copies ran while one was open for 16% of the time, Pallas kernels for 0%

commit v1 on v0

v1 whole, which is shorter than its diff:
```python
import jax
import jax.numpy as jnp
from jax import lax
from jax.sharding import PartitionSpec as P

LANES = 128
EPSILON = 1e-05
BOTH = ("seq", "wshard")
SWAP = [(0, 1), (1, 0)]
HIGHEST = lax.Precision.HIGHEST


def swapped(array):
    return lax.ppermute(array, "section", SWAP)


def norm_rows(values, gain_vec):
    return (
        values * lax.rsqrt(jnp.mean(values * values, axis=-1, keepdims=True) + EPSILON) * gain_vec
    )


def gate_norm(scanned, gate_z, gain_vec):
    return norm_rows(scanned * jax.nn.silu(gate_z), gain_vec)


def seat_groups(n_seq, micro):
    return [list(range(start, start + micro)) for start in range(0, n_seq, micro)]


def to_sequences(rows, section, micro, n_seq):
    _, t, d = rows.shape
    half = t // 2
    mine = lax.dynamic_slice_in_dim(rows, section * half, half, 1)
    got = lax.all_to_all(
        mine, "seq", 0, 0, axis_index_groups=seat_groups(n_seq, micro), tiled=True
    )
    pairs = got.reshape(2, micro // 2, half, d)
    keep = lax.dynamic_index_in_dim(pairs, section, 0, keepdims=False)
    give = lax.dynamic_index_in_dim(pairs, 1 - section, 0, keepdims=False)
    other = swapped(give)
    first = jnp.where(section == 0, keep, other)
    second = jnp.where(section == 0, other, keep)
    return jnp.stack([first, second], axis=1).reshape(micro * half, d)


def to_pieces(first_rows, second_rows, section, micro, n_seq):
    rows, d = first_rows.shape
    keep = jnp.where(section == 0, first_rows, second_rows)
    give = jnp.where(section == 0, second_rows, first_rows)
    other = swapped(give)
    lo = jnp.where(section == 0, keep, other)
    hi = jnp.where(section == 0, other, keep)
    whole = jnp.concatenate([lo, hi]).reshape(micro, 2 * rows // micro, d)
    return lax.all_to_all(
        whole, "seq", 0, 0, axis_index_groups=seat_groups(n_seq, micro), tiled=True
    )


class Halves:
    def __init__(self, own, other):
        self.own = own
        self.other = other


def fetch(weight, section):
    width = weight.shape[1] // 2
    keep = lax.dynamic_slice_in_dim(weight, section * width, width, 1)
    give = lax.dynamic_slice_in_dim(weight, (1 - section) * width, width, 1)
    got = swapped(give)
    layers = []
    for layer in range(2):
        piece = jnp.where(section == layer, keep, got)
        own = lax.all_gather(piece, BOTH, axis=0, tiled=True)
        layers.append(Halves(own, swapped(own)))
    return layers


def in_order(own, other, section, axis):
    lo = jnp.where(section == 0, own, other)
    hi = jnp.where(section == 0, other, own)
    return jnp.concatenate([lo, hi], axis=axis)


def times(rows, weight, section):
    own = jnp.dot(rows, weight.own, preferred_element_type=jnp.float32)
    other = jnp.dot(rows, weight.other, preferred_element_type=jnp.float32)
    return in_order(own, other, section, 1)


def halves_of(array, section):
    width = array.shape[1] // 2
    return (
        lax.dynamic_slice_in_dim(array, section * width, width, 1),
        lax.dynamic_slice_in_dim(array, (1 - section) * width, width, 1),
    )


def times_back(grad, weight, section):
    own, other = halves_of(grad, section)
    return jnp.einsum(
        "tp,dp->td", own, weight.own, preferred_element_type=jnp.float32
    ) + jnp.einsum("tp,dp->td", other, weight.other, preferred_element_type=jnp.float32)


def bits_of(size):
    return size.bit_length() - 1


def hop_list():
    hops = []
    for axis in BOTH:
        for bit in reversed(range(bits_of(lax.axis_size(axis)))):
            hops.append((axis, 1 << bit))
    return hops


def exchanged(array, axis, distance):
    pairs = [(i, i ^ distance) for i in range(lax.axis_size(axis))]
    return lax.ppermute(array, axis, pairs)


def side_of(axis, distance):
    return (lax.axis_index(axis) // distance) % 2


def add_low(one, two):
    return (one.astype(jnp.float32) + two.astype(jnp.float32)).astype(jnp.bfloat16)


def scatter_sum(array, turned):
    hops = hop_list()
    seat_bits = bits_of(lax.axis_size("seq"))
    order = list(range(seat_bits, len(hops)))
    order = (order if turned else order[::-1]) + list(range(seat_bits))[::-1]
    rows = array.shape[0] >> len(hops)
    array = array.reshape((2,) * len(hops) + (rows, array.shape[1]))
    left = list(range(len(hops)))
    for dim in order:
        axis, distance = hops[dim]
        at = left.index(dim)
        side = side_of(axis, distance)
        give = lax.dynamic_index_in_dim(array, 1 - side, at, keepdims=False)
        keep = lax.dynamic_index_in_dim(array, side, at, keepdims=False)
        array = add_low(keep, exchanged(give, axis, distance))
        left.remove(dim)
    return array


def sum_everywhere(array):
    for axis, distance in hop_list():
        array = array + exchanged(array, axis, distance)
    return array


def weight_sum(rows, grad, section, turned):
    own, other = halves_of(grad, section)
    give = jnp.einsum("td,te->de", rows, other, preferred_element_type=jnp.float32)
    got = swapped(give.astype(jnp.bfloat16))
    keep = jnp.einsum("td,te->de", rows, own, preferred_element_type=jnp.float32)
    return scatter_sum(add_low(keep, got), turned)


def place(first, second, section):
    keep = jnp.where(section == 0, first, second)
    give = jnp.where(section == 0, second, first)
    other = swapped(give)
    return in_order(keep, other, section, 1).astype(jnp.float32)


def mixer(
    conv_in, dt_raw, kernel, offset, dt_offset, a_log, skip, heads, state_width, seat, run, whole_run
):
    tokens = conv_in.shape[0]
    taps = kernel.shape[0]
    inner = conv_in.shape[1] - 2 * state_width
    size = inner // heads
    span = min(256, tokens)
    n_span = tokens // span
    tail = conv_in[tokens - (taps - 1) :]
    halo = before(tail, run, seat, whole_run)
    padded = jnp.concatenate([halo, conv_in], axis=0)
    total = jnp.zeros_like(conv_in) + offset[None, :]
    for tap in range(taps):
        total = total + kernel[tap][None, :] * padded[tap : tap + tokens]
    conv = jax.nn.silu(total)
    x = conv[:, :inner].reshape(n_span, span, heads, size)
    b = conv[:, inner : inner + state_width].reshape(n_span, span, state_width)
    c = conv[:, inner + state_width :].reshape(n_span, span, state_width)
    dt = jax.nn.softplus(dt_raw + dt_offset)
    rate = -jnp.exp(a_log)
    dt_b = jnp.transpose(dt.reshape(n_span, span, heads), (0, 2, 1))
    cum = jnp.cumsum(dt_b * rate[None, :, None], axis=2)
    scores = jnp.einsum("cin,cjn->cij", c, b, precision=HIGHEST)
    ids = jnp.arange(span)
    lower = (ids[:, None] >= ids[None, :])[None, None]
    diff = cum[:, :, :, None] - cum[:, :, None, :]
    weighted = jnp.where(lower, jnp.exp(jnp.where(lower, diff, 0.0)), 0.0)
    weighted = weighted * scores[:, None] * dt_b[:, :, None, :]
    intra = jnp.einsum(
        "chij,cjhp->cihp", weighted.astype(jnp.bfloat16), x.astype(jnp.bfloat16),
        preferred_element_type=jnp.float32,
    )
    last = cum[:, :, -1]
    tail_weight = jnp.exp(last[:, :, None] - cum) * dt_b
    xw = x * jnp.transpose(tail_weight, (0, 2, 1))[..., None]
    states = jnp.einsum(
        "cjn,cjhp->chnp", b.astype(jnp.bfloat16), xw.astype(jnp.bfloat16),
        preferred_element_type=jnp.float32,
    )
    state = jnp.zeros_like(states[0])
    entering = []
    for k in range(n_span):
        entering.append(state)
        state = jnp.exp(last[k])[:, None, None] * state + states[k]
    enter_run = carried(state, jnp.sum(last, axis=0), run, seat, whole_run)
    gone = jnp.zeros_like(last[0])
    shifted = []
    for k in range(n_span):
        shifted.append(entering[k] + jnp.exp(gone)[:, None, None] * enter_run)
        gone = gone + last[k]
    entering = jnp.stack(shifted)
    inter = jnp.einsum(
        "cin,chnp->cihp", c.astype(jnp.bfloat16), entering.astype(jnp.bfloat16),
        preferred_element_type=jnp.float32,
    ) * jnp.transpose(jnp.exp(cum), (0, 2, 1))[..., None]
    out = (intra + inter + skip[None, None, :, None] * x).reshape(tokens, inner)
    return out


def before(tail, run, seat, whole_run):
    n_seq, micro = whole_run
    if n_seq == micro:
        return lax.ppermute(tail, "section", [(0, 1)])
    every = lax.all_gather(tail, ("seq", "section"), axis=0)
    every = every.reshape((n_seq // micro, micro, 2) + tail.shape)
    mine = lax.dynamic_index_in_dim(every, seat % micro, 1, keepdims=False)
    mine = mine.reshape((-1,) + tail.shape)
    past = lax.dynamic_index_in_dim(mine, jnp.maximum(run - 1, 0), 0, keepdims=False)
    return jnp.where(run > 0, past, 0.0)


def carried(state, total, run, seat, whole_run):
    n_seq, micro = whole_run
    if n_seq == micro:
        return lax.ppermute(state.astype(jnp.bfloat16), "section", [(0, 1)]).astype(jnp.float32)
    every = lax.all_gather(state, ("seq", "section"), axis=0)
    totals = lax.all_gather(total, ("seq", "section"), axis=0)
    every = every.reshape((n_seq // micro, micro, 2) + state.shape)
    totals = totals.reshape((n_seq // micro, micro, 2) + total.shape)
    mine = lax.dynamic_index_in_dim(every, seat % micro, 1, keepdims=False)
    mine = mine.reshape((-1,) + state.shape)
    gone = lax.dynamic_index_in_dim(totals, seat % micro, 1, keepdims=False)
    gone = jnp.cumsum(gone.reshape((-1,) + total.shape), axis=0)
    upto = lax.dynamic_index_in_dim(gone, jnp.maximum(run - 1, 0), 0, keepdims=False)
    early = (jnp.arange(mine.shape[0]) < run)[:, None]
    decay = jnp.where(early, jnp.exp(jnp.where(early, upto[None] - gone, 0.0)), 0.0)
    return jnp.einsum("kh,khnp->hnp", decay, mine, precision=HIGHEST)


def local(
    inputs,
    seq_lengths,
    cotangent,
    norm_gain,
    in_weight,
    conv_weight,
    conv_bias,
    dt_bias,
    a_log,
    d_skip,
    gated_gain,
    out_weight,
):
    section = lax.axis_index("section")
    seat = lax.axis_index("seq")
    lane = lax.axis_index("wshard")
    n_seq = lax.axis_size("seq")
    micro, _, piece, width = inputs.shape
    tokens = micro * piece // 2
    inner = gated_gain.shape[1]
    heads = dt_bias.shape[1]
    channels = conv_weight.shape[2]
    state_width = (channels - inner) // 2
    proj = in_weight.shape[2]
    mixed = proj - inner
    padded = -(-mixed // (2 * LANES)) * 2 * LANES
    run = (seat // micro) * 2 + section
    whole_run = (n_seq, micro)

    mix_layers = fetch(
        jnp.pad(in_weight[0, :, inner:], ((0, 0), (0, padded - mixed))), section
    )
    gate_layers = fetch(in_weight[0, :, :inner], section)
    out_layers = fetch(out_weight[0], section)
    hidden_bf = to_sequences(inputs[:, 0], section, micro, n_seq)
    cot = to_sequences(cotangent[:, 0], section, micro, n_seq)

    def both_layers(array):
        other = swapped(array)
        lo = jnp.where(section == 0, array, other)
        hi = jnp.where(section == 0, other, array)
        return (lo[0], hi[0])

    sizes = [norm_gain, conv_weight.reshape(1, -1), conv_bias, dt_bias, a_log, d_skip, gated_gain]
    packed = jnp.concatenate(sizes, axis=1)
    splits = [int(s.shape[1]) for s in sizes]

    def unpack(flat):
        parts, at = [], 0
        for count in splits:
            parts.append(flat[at : at + count])
            at += count
        parts[1] = parts[1].reshape(conv_weight.shape[1:])
        return parts

    params = [unpack(flat) for flat in both_layers(packed)]
    length = lax.dynamic_index_in_dim(
        lax.dynamic_index_in_dim(seq_lengths, seat % micro, 0, keepdims=False), lane, 0,
        keepdims=False,
    )
    positions = run * tokens + jnp.arange(tokens)
    valid = (positions < length).astype(jnp.float32)[:, None]

    kept = []
    layer_outs = []
    for layer in range(2):
        gain_in, kernel, offset, dt_offset, alog, skip, gain_out = params[layer]
        hidden = hidden_bf.astype(jnp.float32)
        normed_in = norm_rows(hidden, gain_in).astype(jnp.bfloat16)
        projected = times(normed_in, mix_layers[layer], section).astype(jnp.bfloat16)
        gate_z = times(normed_in, gate_layers[layer], section)
        conv_in = projected[:, :channels]
        dt_raw = projected[:, channels:mixed]

        def run_mixer(*args):
            return mixer(*args, heads, state_width, seat, run, whole_run)

        mix_args = (
            conv_in.astype(jnp.float32), dt_raw.astype(jnp.float32), kernel, offset, dt_offset,
            alog, skip,
        )
        scanned = run_mixer(*mix_args).astype(jnp.bfloat16)
        normed_out = gate_norm(scanned.astype(jnp.float32), gate_z, gain_out).astype(jnp.bfloat16)
        branch = times(normed_out, out_layers[layer], section)
        layer_out = (valid * (hidden + branch)).astype(jnp.bfloat16)
        kept.append((hidden_bf, normed_in, gate_z, mix_args, run_mixer, scanned, normed_out))
        layer_outs.append(layer_out)
        hidden_bf = layer_out
    acts = to_pieces(layer_outs[0], layer_outs[1], section, micro, n_seq)

    grad_bf = cot
    shard_gate, shard_mix, shard_out = [None] * 2, [None] * 2, [None] * 2
    small, grad_outs = [None] * 2, [None] * 2
    for layer in (1, 0):
        gain_in, kernel, offset, dt_offset, alog, skip, gain_out = params[layer]
        hid, normed_in, gate_z, mix_args, run_mixer, scanned, normed_out = kept[layer]
        masked = grad_bf.astype(jnp.float32) * valid
        grad_branch = masked.astype(jnp.bfloat16)
        shard_out[layer] = weight_sum(normed_out, grad_branch, section, False)
        grad_normed = times_back(grad_branch, out_layers[layer], section)
        _, pull_gate = jax.vjp(gate_norm, scanned.astype(jnp.float32), gate_z, gain_out)
        grad_scanned, grad_gate, grad_gain_out = pull_gate(grad_normed)
        grad_y = grad_scanned.astype(jnp.bfloat16).astype(jnp.float32)
        _, pull_mixer = jax.vjp(run_mixer, *mix_args)
        g_conv, g_dt, g_kernel, g_offset, g_dto, g_alog, g_skip = pull_mixer(grad_y)
        grad_gate = grad_gate.astype(jnp.bfloat16)
        shard_gate[layer] = weight_sum(normed_in, grad_gate, section, True)
        grad_mix = jnp.concatenate(
            [
                g_conv.astype(jnp.bfloat16),
                g_dt.astype(jnp.bfloat16),
                jnp.zeros((tokens, padded - mixed), jnp.bfloat16),
            ],
            axis=1,
        )
        grad_normed_in = times_back(grad_gate, gate_layers[layer], section) + times_back(
            grad_mix, mix_layers[layer], section
        )
        _, pull_norm = jax.vjp(norm_rows, hid.astype(jnp.float32), gain_in)
        grad_hidden, grad_gain_in = pull_norm(grad_normed_in)
        grad_bf = (masked + grad_hidden).astype(jnp.bfloat16)
        shard_mix[layer] = weight_sum(normed_in, grad_mix, section, False)
        grad_outs[layer] = grad_bf
        small[layer] = jnp.concatenate(
            [grad_gain_in, g_kernel.reshape(-1), g_offset, g_dto, g_alog, g_skip, grad_gain_out]
        )
    grads = to_pieces(grad_outs[0], grad_outs[1], section, micro, n_seq)
    mine = jnp.where(section == 0, small[0], small[1])
    others = jnp.where(section == 0, small[1], small[0])
    g = unpack(sum_everywhere(mine + swapped(others)))
    grad_in_weight = jnp.concatenate(
        [
            place(shard_gate[0], shard_gate[1], section),
            place(shard_mix[0], shard_mix[1], section)[:, :mixed],
        ],
        axis=1,
    )
    return (
        acts[None, :, None],
        grads[None, :, None],
        g[0][None],
        grad_in_weight[None],
        g[1][None],
        g[2][None],
        g[3][None],
        g[4][None],
        g[5][None],
        g[6][None],
        place(shard_out[0], shard_out[1], section)[None],
    )


def solution(mesh):
    return jax.shard_map(
        local,
        mesh=mesh,
        in_specs=(
            P(None, "wshard", "seq", None),
            P(),
            P(None, "wshard", "seq", None),
            P("section", None),
            P("section", ("seq", "wshard"), None),
            P("section", None, None),
            P("section", None),
            P("section", None),
            P("section", None),
            P("section", None),
            P("section", None),
            P("section", ("seq", "wshard"), None),
        ),
        out_specs=(
            P("section", None, "wshard", "seq", None),
            P("section", None, "wshard", "seq", None),
            P("section", None),
            P("section", ("seq", "wshard"), None),
            P("section", None, None),
            P("section", None),
            P("section", None),
            P("section", None),
            P("section", None),
            P("section", None),
            P("section", ("seq", "wshard"), None),
        ),
        check_vma=False,
    )
```

time: 2580 us -> 1270 us (0.49)
  waiting for transfers between devices: 950 us -> 530 us
  matrix products: 613 us -> 215 us
  blocking collectives: 245 us -> 0 us
  other arithmetic: 303 us -> 185 us
  local copies, waits for them, and re-layouts: 307 us -> 237 us
  starting transfers between devices: 129 us -> 77.7 us
    dot_general x115 -> x60, matrix products: 604 us -> 207 us  [the longest x6 61.7 us: mixer(): jnp.einsum('chij,cjhp->cihp', weighted.astype(jnp.bfloat16), x.astype(jnp...]
    unnamed x10 -> x6, waiting for transfers between devices: 336 us -> 1.12 us
    all_to_all x27 -> x4, waiting for transfers between devices: 304 us -> 25.9 us  [the longest x2 25.9 us: to_sequences(): lax.all_to_all(mine, 'seq', 0, 0, axis_index_groups=seat_groups(n_seq, mi...]
    all_gather x2 -> x6, waiting for transfers between devices: 117 us -> 340 us  [fetch(): own = lax.all_gather(piece, BOTH, axis=0, tiled=True)]
    reduce_scatter x6 -> x0, waiting for transfers between devices: 177 us -> none  [the longest x1 177 us: local(): lax.psum_scatter(acc_out[None], ('seq', 'wshard'), scatter_dimension=1, t...]
    ppermute x8 -> x62, waiting for transfers between devices: 16 us -> 162 us  [the longest x28 157 us: exchanged(): return lax.ppermute(array, axis, pairs)]
    all_to_all x27 -> x4, starting transfers between devices: 118 us -> 18.9 us  [the longest x2 9.74 us: to_sequences(): lax.all_to_all(mine, 'seq', 0, 0, axis_index_groups=seat_groups(n_seq, mi...]
    all_gather x5 -> x0, blocking collectives: 82.9 us -> none  [forward_tick(): bc_whole = lax.all_gather(bc_part, 'seq', axis=0, tiled=True)]
  transfers between devices with their start and end apart: 44 -> 72, of which waited for: 31 -> 32; matrix products, arithmetic and copies ran while one was open for 16% -> 47% of each run, Pallas kernels for 0% -> 0%
where the time goes in v1:
time: 1270 us; the launch traced here: 1260 us
  waiting for transfers between devices  530 us (42%)
  local copies, waits for them, and re-layouts  237 us (19%)
  matrix products  215 us (17%)
  other arithmetic  185 us (15%)
  starting transfers between devices  77.7 us (6%)
  between operations  18.2 us (1%)
    all_gather x6, waiting for transfers between devices, fetch(): own = lax.all_gather(piece, BOTH, axis=0, tiled=True)  340 us
    ppermute x28, waiting for transfers between devices, exchanged(): return lax.ppermute(array, axis, pairs)  157 us
    dot_general x6, matrix products, mixer(): jnp.einsum('chij,cjhp->cihp', weighted.astype(jnp.bfloat16), x.astype(jnp...  61.7 us
    reshape x6, local copies, waits for them, and re-layouts, mixer(): x = conv[:, :inner].reshape(n_span, span, heads, size)  45.7 us
    unnamed x497, local copies, waits for them, and re-layouts  35.1 us
    convert_element_type x4, local copies, waits for them, and re-layouts, local(): scanned.astype(jnp.float32)  34 us
    ppermute x28, starting transfers between devices, exchanged(): return lax.ppermute(array, axis, pairs)  33.9 us
    concatenate x4, local copies, waits for them, and re-layouts, in_order(): return jnp.concatenate([lo, hi], axis=axis)  31.3 us
  transfers between devices with their start and end apart: 72, of which 32 were waited for; matrix products, arithmetic and copies ran while one was open for 47% of the time, Pallas kernels for 0%

profile of v1, /device:TPU:0, one launch (start us, length us, event | category | flops | bytes accessed | tf_op | source)
XLA Modules:
  0.0 1261.7 jit_solution(7143128948236520200)
XLA Ops:
  33.8 25.9 %all-to-all-done = bf16[4,128,1024]{2,1,0:T(8,128)(2,1)S(1)} async-done(((bf16[4,128,1024]{2,1,0:T(8,128)(2,1)}), bf16[4,128,1024]{2,1,0:T(8,128)(2,1)S(1)}, u32[]{:S(2)}, u32[]{:S(2)}) %all-to-all-start) | async-done | bytes 1048608 | tf_op jit(solution)/shard_map/all_to_all | solution.py:35
  64.0 32.2 %all-gather.9.cloned.1.call-done = bf16[1024,1024]{1,0:T(8,128)(2,1)} async-done(((bf16[64,1024]{1,0:T(8,128)(2,1)}), bf16[1024,1024]{1,0:T(8,128)(2,1)}) %all-gather.9.cloned.1.call-update) | async-done | bytes 2097168 | tf_op jit(solution)/shard_map/all_gather | solution.py:74
  99.6 63.4 %all-gather.7.cloned.1.call-done = bf16[1024,1280]{1,0:T(8,128)(2,1)} async-done(((bf16[64,1280]{1,0:T(8,128)(2,1)}), bf16[1024,1280]{1,0:T(8,128)(2,1)}) %all-gather.7.cloned.1.call-update) | async-done | bytes 2621456 | tf_op jit(solution)/shard_map/all_gather | solution.py:74
  170.9 54.7 %all-gather.11.cloned.1.call-done = bf16[2048,512]{1,0:T(8,128)(2,1)} async-done(((bf16[128,512]{1,0:T(8,128)(2,1)}), bf16[2048,512]{1,0:T(8,128)(2,1)}) %all-gather.11.cloned.1.call-update) | async-done | bytes 2097168 | tf_op jit(solution)/shard_map/all_gather | solution.py:74
  225.5 62.0 %all-gather.15.cloned.1.call-done = bf16[1024,1024]{1,0:T(8,128)(2,1)} async-done(((bf16[64,1024]{1,0:T(8,128)(2,1)}), bf16[1024,1024]{1,0:T(8,128)(2,1)}) %all-gather.15.cloned.1.call-update) | async-done | bytes 2097168 | tf_op jit(solution)/shard_map/all_gather | solution.py:74
  287.6 62.0 %all-gather.17.cloned.1.call-done = bf16[2048,512]{1,0:T(8,128)(2,1)} async-done(((bf16[128,512]{1,0:T(8,128)(2,1)}), bf16[2048,512]{1,0:T(8,128)(2,1)}) %all-gather.17.cloned.1.call-update) | async-done | bytes 2097168 | tf_op jit(solution)/shard_map/all_gather | solution.py:74
  349.6 65.8 %all-gather.13.cloned.1.call-done = bf16[1024,1280]{1,0:T(8,128)(2,1)} async-done(((bf16[64,1280]{1,0:T(8,128)(2,1)}), bf16[1024,1280]{1,0:T(8,128)(2,1)}) %all-gather.13.cloned.1.call-update) | async-done | bytes 2621456 | tf_op jit(solution)/shard_map/all_gather | solution.py:74
  479.7 7.8 copy.378
  496.6 8.3 multiply_reduce_fusion.17
  504.9 9.1 copy.467
  514.1 7.8 reshape.974
  561.6 7.9 copy.391
  569.5 10.0 fusion.36
  615.5 8.3 multiply_reduce_fusion.16
  623.8 9.1 copy.470
  632.9 7.9 reshape.976
  682.2 15.0 %fusion.19 = (f32[2,32,256]{2,1,0:T(8,128)}, f32[2,32,256]{2,1,0:T(8,128)}, f32[2,32,256]{2,1,0:T(8,128)}, f32[2,256,256]{2,1,0:T(8,128)S(1)}) fusion(f32[2,32,256]{2,1,0:T(8,128)S(1)} %bitcast.896, f32[2,256,256]{2,1,0:T(8,128)S(1)} %copy-done.120, f32[2,32,256]{2,1,0:T(8,128)S(1)} %copy_bitcast_fusion.12, pred[256,256]{1,0:T(8,128)(4,1)S(1)} %copy-done.170, ...), kind=kOutput, calls=%fused_computation.27 | convolution fusion | flops 607993856 | bytes 7733248 | tf_op jit(solution)/shard_map/transpose(jvp(chij,cjhp->cihp))/dot_general | solution.py:200
  740.8 9.2 copy.465
  757.8 13.8 %multiply_reduce_fusion.2 = (f32[2304]{0:T(1024)S(1)}, f32[2304]{0:T(1024)S(1)}, f32[2304]{0:T(1024)S(1)}, f32[2304]{0:T(1024)}, f32[2304]{0:T(1024)S(1)}, /*index=5*/f32[512,2304]{1,0:T(8,128)}) fusion(f32[512,2304]{1,0:T(8,128)} %copy-done.8, f32[3,2304]{1,0:T(4,128)S(1)} %copy-done.138, bf16[512,1280]{1,0:T(8,128)(2,1)} %copy-done.60, ...), kind=kLoop, calls=%fused_computation.70 | loop fusion | flops 31838976 | bytes 21569536 | tf_op jit(solution)/shard_map/transpose(jvp())/reduce_sum | solution.py:185
  861.0 15.1 %fusion.21 = (f32[2,32,256]{2,1,0:T(8,128)}, f32[2,32,256]{2,1,0:T(8,128)}, f32[2,32,256]{2,1,0:T(8,128)}, f32[2,256,256]{2,1,0:T(8,128)}) fusion(f32[2,32,256]{2,1,0:T(8,128)S(1)} %bitcast.893, f32[2,256,256]{2,1,0:T(8,128)} %copy-done.117, f32[2,32,256]{2,1,0:T(8,128)S(1)} %copy-done.128, pred[256,256]{1,0:T(8,128)(4,1)} %iota_compare_fusion, ...), kind=kOutput, calls=%fused_computation.29 | convolution fusion | flops 607993856 | bytes 7733248 | tf_op jit(solution)/shard_map/transpose(jvp(chij,cjhp->cihp))/dot_general | solution.py:200
  905.7 9.1 copy.466
  914.8 7.9 reshape.973
  922.7 12.9 %multiply_reduce_fusion.6 = (f32[2304]{0:T(1024)}, f32[2304]{0:T(1024)S(1)}, f32[2304]{0:T(1024)S(1)}, f32[2304]{0:T(1024)}, f32[2304]{0:T(1024)}, /*index=5*/f32[512,2304]{1,0:T(8,128)}) fusion(f32[512,2304]{1,0:T(8,128)} %copy-done.7, f32[3,2304]{1,0:T(4,128)S(1)} %copy-done.136, bf16[512,1280]{1,0:T(8,128)(2,1)S(1)} %copy-done.59, ...), kind=kLoop, calls=%fused_computation.74 | loop fusion | flops 31838976 | bytes 21569536 | tf_op jit(solution)/shard_map/transpose(jvp())/reduce_sum | solution.py:185
  1051.1 14.4 %collective-permute-done.57 = bf16[2,2,2,128,512]{4,3,0,1,2:T(8,128)(2,1)S(1)} collective-permute-done((bf16[2,2,2,128,512]{4,3,0,1,2:T(8,128)(2,1)S(1)}, bf16[2,2,2,128,512]{4,3,0,1,2:T(8,128)(2,1)S(1)}, u32[]{:S(2)}, u32[]{:S(2)}) %collective-permute-start.57) | collective-permute-done | bytes 1048608 | tf_op jit(solution)/shard_map/ppermute | solution.py:120
  1067.2 20.0 %collective-permute-done.52 = bf16[2,2,2,128,512]{4,3,0,1,2:T(8,128)(2,1)S(1)} collective-permute-done((bf16[2,2,2,128,512]{4,3,0,1,2:T(8,128)(2,1)S(1)}, bf16[2,2,2,128,512]{4,3,0,1,2:T(8,128)(2,1)S(1)}, u32[]{:S(2)}, u32[]{:S(2)}) %collective-permute-start.52) | collective-permute-done | bytes 1048608 | tf_op jit(solution)/shard_map/ppermute | solution.py:120
  1106.7 8.5 collective-permute-done.53
  1146.5 8.1 collective-permute-done.55
  1161.3 8.2 collective-permute-done.41
  1183.1 8.2 collective-permute-done.42
  1191.6 9.2 collective-permute-done.48
  1201.9 25.8 %collective-permute-done.43 = bf16[2,64,1280]{2,1,0:T(8,128)(2,1)S(1)} collective-permute-done((bf16[2,64,1280]{2,1,0:T(8,128)(2,1)S(1)}, bf16[2,64,1280]{2,1,0:T(8,128)(2,1)S(1)}, u32[]{:S(2)}, u32[]{:S(2)}) %collective-permute-start.43) | collective-permute-done | bytes 327712 | tf_op jit(solution)/shard_map/ppermute | solution.py:120
  1231.1 11.7 collective-permute-done.49
  (944 shorter events, 604.0 us)
Async XLA Ops:
  7.2 89.0 %all-gather.9.cloned.1.call-start = ((), (), s32[]{:S(2)}) async-start(), calls=%async_computation.5 | async-start | bytes 2228224 | tf_op jit(solution)/shard_map/all_gather | solution.py:74
  10.8 152.3 %all-gather.7.cloned.1.call-start = ((), (), s32[]{:S(2)}) async-start(), calls=%async_computation.4 | async-start | bytes 2785280 | tf_op jit(solution)/shard_map/all_gather | solution.py:74
  14.2 211.4 %all-gather.11.cloned.1.call-start = ((), (), s32[]{:S(2)}) async-start(), calls=%async_computation.6 | async-start | bytes 2228224 | tf_op jit(solution)/shard_map/all_gather | solution.py:74
  18.2 269.3 %all-gather.15.cloned.1.call-start = ((), (), s32[]{:S(2)}) async-start(), calls=%async_computation.8 | async-start | bytes 2228224 | tf_op jit(solution)/shard_map/all_gather | solution.py:74
  18.8 330.8 %all-gather.17.cloned.1.call-start = ((), (), s32[]{:S(2)}) async-start(), calls=%async_computation.9 | async-start | bytes 2228224 | tf_op jit(solution)/shard_map/all_gather | solution.py:74
  26.7 388.7 %all-gather.13.cloned.1.call-start = ((), (), s32[]{:S(2)}) async-start(), calls=%async_computation.7 | async-start | bytes 2785280 | tf_op jit(solution)/shard_map/all_gather | solution.py:74
  59.7 104.6 %all-to-all-start.2 = ((bf16[4,128,1024]{2,1,0:T(8,128)(2,1)}), bf16[4,128,1024]{2,1,0:T(8,128)(2,1)S(1)}, u32[]{:S(2)}, u32[]{:S(2)}) async-start(bf16[4,128,1024]{2,1,0:T(8,128)(2,1)} %dynamic-slice_bitcast_fusion), calls=%async_computation.2 | async-start | bytes 2097152 | tf_op jit(solution)/shard_map/all_to_all | solution.py:35
  96.2 319.2 %collective-permute-start.7 = (bf16[1024,1024]{1,0:T(8,128)(2,1)}, bf16[1024,1024]{1,0:T(8,128)(2,1)}, u32[]{:S(2)}, u32[]{:S(2)}) collective-permute-start(bf16[1024,1024]{1,0:T(8,128)(2,1)} %all-gather.9.cloned.1.call-done), channel_id=1, source_target_pairs={{0,16},{16,0},{1,17},{17,1},{2,18},{18,2},{3,19},{19,3},{4,20},{20... | collective-permute-start | bytes 6291464 | tf_op jit(solution)/shard_map/ppermute | solution.py:14
  99.1 65.8 %collective-permute-start = (bf16[2,128,1024]{2,1,0:T(8,128)(2,1)S(1)}, bf16[2,128,1024]{2,1,0:T(8,128)(2,1)}, u32[]{:S(2)}, u32[]{:S(2)}) collective-permute-start(bf16[2,128,1024]{2,1,0:T(8,128)(2,1)S(1)} %dynamic-slice_bitcast_fusion.9), channel_id=1, source_target_pairs={{0,16},{16,0},{1,17},{17,1},{2,18},{18,2},{3,19},{19,3},{4,20},{20... | collective-permute-start | bytes 1572872 | tf_op jit(solution)/shard_map/ppermute | solution.py:14
  163.1 259.2 %collective-permute-start.3 = (bf16[1024,1280]{1,0:T(8,128)(2,1)}, bf16[1024,1280]{1,0:T(8,128)(2,1)}, u32[]{:S(2)}, u32[]{:S(2)}) collective-permute-start(bf16[1024,1280]{1,0:T(8,128)(2,1)} %all-gather.7.cloned.1.call-done), channel_id=1, source_target_pairs={{0,16},{16,0},{1,17},{17,1},{2,18},{18,2},{3,19},{19,3},{4,20},{20... | collective-permute-start | bytes 7864328 | tf_op jit(solution)/shard_map/ppermute | solution.py:14
  225.5 300.1 %collective-permute-start.9 = (bf16[2048,512]{1,0:T(8,128)(2,1)}, bf16[2048,512]{1,0:T(8,128)(2,1)}, u32[]{:S(2)}, u32[]{:S(2)}) collective-permute-start(bf16[2048,512]{1,0:T(8,128)(2,1)} %all-gather.11.cloned.1.call-done), channel_id=1, source_target_pairs={{0,16},{16,0},{1,17},{17,1},{2,18},{18,2},{3,19},{19,3},{4,20},{20... | collective-permute-start | bytes 6291464 | tf_op jit(solution)/shard_map/ppermute | solution.py:14
  287.6 257.0 %collective-permute-start.13 = (bf16[1024,1024]{1,0:T(8,128)(2,1)}, bf16[1024,1024]{1,0:T(8,128)(2,1)}, u32[]{:S(2)}, u32[]{:S(2)}) collective-permute-start(bf16[1024,1024]{1,0:T(8,128)(2,1)} %all-gather.15.cloned.1.call-done), channel_id=1, source_target_pairs={{0,16},{16,0},{1,17},{17,1},{2,18},{18,2},{3,19},{19,3},{4,20},{20... | collective-permute-start | bytes 6291464 | tf_op jit(solution)/shard_map/ppermute | solution.py:14
  349.6 255.9 %collective-permute-start.14 = (bf16[2048,512]{1,0:T(8,128)(2,1)}, bf16[2048,512]{1,0:T(8,128)(2,1)}, u32[]{:S(2)}, u32[]{:S(2)}) collective-permute-start(bf16[2048,512]{1,0:T(8,128)(2,1)} %all-gather.17.cloned.1.call-done), channel_id=1, source_target_pairs={{0,16},{16,0},{1,17},{17,1},{2,18},{18,2},{3,19},{19,3},{4,20},{20... | collective-permute-start | bytes 6291464 | tf_op jit(solution)/shard_map/ppermute | solution.py:14
  415.4 117.2 %collective-permute-start.10 = (bf16[1024,1280]{1,0:T(8,128)(2,1)}, bf16[1024,1280]{1,0:T(8,128)(2,1)}, u32[]{:S(2)}, u32[]{:S(2)}) collective-permute-start(bf16[1024,1280]{1,0:T(8,128)(2,1)} %all-gather.13.cloned.1.call-done), channel_id=1, source_target_pairs={{0,16},{16,0},{1,17},{17,1},{2,18},{18,2},{3,19},{19,3},{4,20},{20... | collective-permute-start | bytes 7864328 | tf_op jit(solution)/shard_map/ppermute | solution.py:14
  489.8 395.6 %collective-permute-start.20 = (bf16[32,128,64]{1,2,0:T(8,128)(2,1)}, bf16[32,128,64]{1,2,0:T(8,128)(2,1)}, u32[]{:S(2)}, u32[]{:S(2)}) collective-permute-start(bf16[32,128,64]{1,2,0:T(8,128)(2,1)} %get-tuple-element.175), channel_id=1, source_target_pairs={{0,16},{1,17},{2,18},{3,19},{4,20},{5,21},{6,22},{7,23},{8,24},{9,... | collective-permute-start | bytes 1572872 | tf_op jit(solution)/shard_map/jvp()/ppermute | solution.py:246
  610.4 110.6 %collective-permute-start.17 = (bf16[32,128,64]{1,2,0:T(8,128)(2,1)}, bf16[32,128,64]{1,2,0:T(8,128)(2,1)}, u32[]{:S(2)}, u32[]{:S(2)}) collective-permute-start(bf16[32,128,64]{1,2,0:T(8,128)(2,1)} %get-tuple-element.177), channel_id=1, source_target_pairs={{0,16},{1,17},{2,18},{3,19},{4,20},{5,21},{6,22},{7,23},{8,24},{9,... | collective-permute-start | bytes 1572872 | tf_op jit(solution)/shard_map/jvp()/ppermute | solution.py:246
  676.8 44.2 %collective-permute-start.18 = (bf16[32,128,64]{1,2,0:T(8,128)(2,1)}, bf16[32,128,64]{1,2,0:T(8,128)(2,1)S(1)}, u32[]{:S(2)}, u32[]{:S(2)}) collective-permute-start(bf16[32,128,64]{1,2,0:T(8,128)(2,1)} %fusion.211), channel_id=1, source_target_pairs={{16,0},{17,1},{18,2},{19,3},{20,4},{21,5},{22,6},{23,7},{24,8},{25... | collective-permute-start | bytes 1572872 | tf_op jit(solution)/shard_map/transpose(jvp())/ppermute | solution.py:246
  701.7 312.7 %collective-permute-start.56 = (bf16[2048,512]{1,0:T(8,128)(2,1)}, bf16[2048,512]{1,0:T(8,128)(2,1)}, u32[]{:S(2)}, u32[]{:S(2)}) collective-permute-start(bf16[2048,512]{1,0:T(8,128)(2,1)} %convolution_convert_fusion.4), channel_id=1, source_target_pairs={{0,16},{16,0},{1,17},{17,1},{2,18},{18,2},{3,19},{19,3},{4,20},{20... | collective-permute-start | bytes 6291464 | tf_op jit(solution)/shard_map/ppermute | solution.py:14
  705.5 314.3 %collective-permute-start.34 = (bf16[1024,1024]{1,0:T(8,128)(2,1)}, bf16[1024,1024]{1,0:T(8,128)(2,1)}, u32[]{:S(2)}, u32[]{:S(2)}) collective-permute-start(bf16[1024,1024]{1,0:T(8,128)(2,1)} %convolution_convert_fusion.6), channel_id=1, source_target_pairs={{0,16},{16,0},{1,17},{17,1},{2,18},{18,2},{3,19},{19,3},{4,20},{20... | collective-permute-start | bytes 6291464 | tf_op jit(solution)/shard_map/ppermute | solution.py:14
  997.5 44.3 %collective-permute-start.29 = (bf16[1024,1024]{1,0:T(8,128)(2,1)}, bf16[1024,1024]{1,0:T(8,128)(2,1)}, u32[]{:S(2)}, u32[]{:S(2)}) collective-permute-start(bf16[1024,1024]{1,0:T(8,128)(2,1)} %convolution_convert_fusion.7), channel_id=1, source_target_pairs={{0,16},{16,0},{1,17},{17,1},{2,18},{18,2},{3,19},{19,3},{4,20},{20... | collective-permute-start | bytes 6291464 | tf_op jit(solution)/shard_map/ppermute | solution.py:14
  1024.3 71.5 %collective-permute-start.40 = (bf16[1024,1280]{1,0:T(8,128)(2,1)}, bf16[1024,1280]{1,0:T(8,128)(2,1)}, u32[]{:S(2)}, u32[]{:S(2)}) collective-permute-start(bf16[1024,1280]{1,0:T(8,128)(2,1)} %convolution_convert_fusion.3), channel_id=1, source_target_pairs={{0,16},{16,0},{1,17},{17,1},{2,18},{18,2},{3,19},{19,3},{4,20},{20... | collective-permute-start | bytes 7864328 | tf_op jit(solution)/shard_map/ppermute | solution.py:14
  1027.5 151.0 %all-to-all-start.3 = ((bf16[4,256,1024]{2,1,0:T(8,128)(2,1)}), bf16[4,256,1024]{2,1,0:T(8,128)(2,1)}, u32[]{:S(2)}, u32[]{:S(2)}) async-start(bf16[4,256,1024]{2,1,0:T(8,128)(2,1)} %bitcast.877), calls=%async_computation.3 | async-start | bytes 4194304 | tf_op jit(solution)/shard_map/all_to_all | solution.py:55
  1040.8 46.3 %collective-permute-start.52 = (bf16[2,2,2,128,512]{4,3,0,1,2:T(8,128)(2,1)S(1)}, bf16[2,2,2,128,512]{4,3,0,1,2:T(8,128)(2,1)S(1)}, u32[]{:S(2)}, u32[]{:S(2)}) collective-permute-start(bf16[2,2,2,128,512]{4,3,0,1,2:T(8,128)(2,1)S(1)} %bitcast.915), channel_id=1, source_target_pairs={{0,1},{1,0},{2,3},{3,2},{4,5},{5,4},{6,7},{7,6},{8,9},{9,8},{10,11... | collective-permute-start | bytes 3145736 | tf_op jit(solution)/shard_map/ppermute | solution.py:120
  1045.5 43.3 %collective-permute-start.35 = (bf16[2,2,2,64,1024]{4,3,0,1,2:T(8,128)(2,1)S(1)}, bf16[2,2,2,64,1024]{4,3,0,1,2:T(8,128)(2,1)S(1)}, u32[]{:S(2)}, u32[]{:S(2)}) collective-permute-start(bf16[2,2,2,64,1024]{4,3,0,1,2:T(8,128)(2,1)S(1)} %bitcast.918), channel_id=1, source_target_pairs={{0,2},{1,3},{2,0},{3,1},{4,6},{5,7},{6,4},{7,5},{8,10},{9,11},{10,... | collective-permute-start | bytes 3145736 | tf_op jit(solution)/shard_map/ppermute | solution.py:120
  1046.8 47.3 %collective-permute-start.30 = (bf16[2,2,2,64,1024]{4,3,0,1,2:T(8,128)(2,1)S(1)}, bf16[2,2,2,64,1024]{4,3,0,1,2:T(8,128)(2,1)S(1)}, u32[]{:S(2)}, u32[]{:S(2)}) collective-permute-start(bf16[2,2,2,64,1024]{4,3,0,1,2:T(8,128)(2,1)S(1)} %bitcast.916), channel_id=1, source_target_pairs={{0,2},{1,3},{2,0},{3,1},{4,6},{5,7},{6,4},{7,5},{8,10},{9,11},{10,... | collective-permute-start | bytes 3145736 | tf_op jit(solution)/shard_map/ppermute | solution.py:120
  1065.9 39.4 %collective-permute-start.58 = (bf16[2,2,128,512]{3,2,0,1:T(8,128)(2,1)S(1)}, bf16[2,2,128,512]{3,2,0,1:T(8,128)(2,1)S(1)}, u32[]{:S(2)}, u32[]{:S(2)}) collective-permute-start(bf16[2,2,128,512]{3,2,0,1:T(8,128)(2,1)S(1)} %dynamic-slice_bitcast_fusion.4), channel_id=1, source_target_pairs={{0,2},{1,3},{2,0},{3,1},{4,6},{5,7},{6,4},{7,5},{8,10},{9,11},{10,... | collective-permute-start | bytes 1572872 | tf_op jit(solution)/shard_map/ppermute | solution.py:120
  1099.8 59.9 %collective-permute-start.46 = (bf16[2,2,2,64,1280]{4,3,0,1,2:T(8,128)(2,1)S(1)}, bf16[2,2,2,64,1280]{4,3,0,1,2:T(8,128)(2,1)S(1)}, u32[]{:S(2)}, u32[]{:S(2)}) collective-permute-start(bf16[2,2,2,64,1280]{4,3,0,1,2:T(8,128)(2,1)S(1)} %bitcast.908), channel_id=1, source_target_pairs={{0,1},{1,0},{2,3},{3,2},{4,5},{5,4},{6,7},{7,6},{8,9},{9,8},{10,11... | collective-permute-start | bytes 3932168 | tf_op jit(solution)/shard_map/ppermute | solution.py:120
  1105.3 64.2 %collective-permute-start.41 = (bf16[2,2,2,64,1280]{4,3,0,1,2:T(8,128)(2,1)S(1)}, bf16[2,2,2,64,1280]{4,3,0,1,2:T(8,128)(2,1)S(1)}, u32[]{:S(2)}, u32[]{:S(2)}) collective-permute-start(bf16[2,2,2,64,1280]{4,3,0,1,2:T(8,128)(2,1)S(1)} %bitcast.907), channel_id=1, source_target_pairs={{0,1},{1,0},{2,3},{3,2},{4,5},{5,4},{6,7},{7,6},{8,9},{9,8},{10,11... | collective-permute-start | bytes 3932168 | tf_op jit(solution)/shard_map/ppermute | solution.py:120
  1155.4 74.8 %collective-permute-start.61 = (bf16[128,512]{1,0:T(8,128)(2,1)}, bf16[128,512]{1,0:T(8,128)(2,1)}, u32[]{:S(2)}, u32[]{:S(2)}) collective-permute-start(bf16[128,512]{1,0:T(8,128)(2,1)} %get-tuple-element.65), channel_id=1, source_target_pairs={{0,16},{16,0},{1,17},{17,1},{2,18},{18,2},{3,19},{19,3},{4,20},{20... | collective-permute-start | bytes 393224 | tf_op jit(solution)/shard_map/ppermute | solution.py:14
  1159.7 85.5 %collective-permute-start.39 = (bf16[64,1024]{1,0:T(8,128)(2,1)}, bf16[64,1024]{1,0:T(8,128)(2,1)}, u32[]{:S(2)}, u32[]{:S(2)}) collective-permute-start(bf16[64,1024]{1,0:T(8,128)(2,1)} %get-tuple-element.68), channel_id=1, source_target_pairs={{0,16},{16,0},{1,17},{17,1},{2,18},{18,2},{3,19},{19,3},{4,20},{20... | collective-permute-start | bytes 393224 | tf_op jit(solution)/shard_map/ppermute | solution.py:14
  1178.6 68.4 %all-to-all-start.1 = ((bf16[4,256,1024]{2,1,0:T(8,128)(2,1)}), bf16[4,256,1024]{2,1,0:T(8,128)(2,1)}, u32[]{:S(2)}, u32[]{:S(2)}) async-start(bf16[4,256,1024]{2,1,0:T(8,128)(2,1)} %bitcast.62), calls=%async_computation.1 | async-start | bytes 4194304 | tf_op jit(solution)/shard_map/all_to_all | solution.py:55
  1201.8 41.0 %collective-permute-start.49 = (bf16[64,1280]{1,0:T(8,128)(2,1)S(1)}, bf16[64,1280]{1,0:T(8,128)(2,1)S(1)}, u32[]{:S(2)}, u32[]{:S(2)}) collective-permute-start(bf16[64,1280]{1,0:T(8,128)(2,1)S(1)} %dynamic-slice_bitcast_fusion.16), channel_id=1, source_target_pairs={{0,8},{4,12},{8,0},{12,4},{1,9},{5,13},{9,1},{13,5},{2,10},{6,14},... | collective-permute-start | bytes 491528 | tf_op jit(solution)/shard_map/ppermute | solution.py:120
  (286 other events, 5272.8 us)
Sparse Core Ops, SparseCore 0:
  10.9 85.2 all-gather.8
  99.5 63.5 all-gather.6
  165.8 59.6 all-gather.10
  228.2 59.3 all-gather.14
  290.2 59.3 all-gather.16
  352.7 62.6 all-gather.12

commit v2 on v1

--- a/solution.py
+++ b/solution.py
@@ -1,6 +1,10 @@
+import functools
+
 import jax
 import jax.numpy as jnp
 from jax import lax
+from jax.experimental import pallas as pl
+from jax.experimental.pallas import tpu as pltpu
 from jax.sharding import PartitionSpec as P
 
 LANES = 128
@@ -18,10 +22,6 @@
     return (
         values * lax.rsqrt(jnp.mean(values * values, axis=-1, keepdims=True) + EPSILON) * gain_vec
     )
-
-
-def gate_norm(scanned, gate_z, gain_vec):
-    return norm_rows(scanned * jax.nn.silu(gate_z), gain_vec)
 
 
 def seat_groups(n_seq, micro):
@@ -82,9 +82,9 @@
     return jnp.concatenate([lo, hi], axis=axis)
 
 
-def times(rows, weight, section):
-    own = jnp.dot(rows, weight.own, preferred_element_type=jnp.float32)
-    other = jnp.dot(rows, weight.other, preferred_element_type=jnp.float32)
+def times(rows, weight, section, kind):
+    own = jnp.dot(rows, weight.own, preferred_element_type=jnp.float32).astype(kind)
+    other = jnp.dot(rows, weight.other, preferred_element_type=jnp.float32).astype(kind)
     return in_order(own, other, section, 1)
 
 
@@ -168,94 +168,520 @@
     return in_order(keep, other, section, 1).astype(jnp.float32)
 
 
-def mixer(
-    conv_in, dt_raw, kernel, offset, dt_offset, a_log, skip, heads, state_width, seat, run, whole_run
+BLOCK = 128
+LIMIT = 48 * 1024 * 1024
+F32 = jnp.float32
+BF16 = jnp.bfloat16
+
+
+def mm(one, two, dims=((1,), (0,)), precision=None):
+    return lax.dot_general(
+        one, two, (dims, ((), ())), preferred_element_type=F32, precision=precision
+    )
+
+
+def low(value):
+    return value.astype(BF16)
+
+
+def sigmoid(value):
+    return 1.0 / (1.0 + jnp.exp(-value))
+
+
+def triangle(lower, kind):
+    rows = lax.broadcasted_iota(jnp.int32, (BLOCK, BLOCK), 0)
+    cols = lax.broadcasted_iota(jnp.int32, (BLOCK, BLOCK), 1)
+    return jnp.where(rows >= cols if lower else rows <= cols, 1.0, 0.0).astype(kind)
+
+
+def first_lanes(rows, size):
+    return lax.broadcasted_iota(jnp.int32, (rows, LANES), 1) < size
+
+
+def spread(table, pair, first):
+    rows = first.shape[0]
+    one = jnp.broadcast_to(table[:, 2 * pair : 2 * pair + 1], (rows, LANES))
+    two = jnp.broadcast_to(table[:, 2 * pair + 1 : 2 * pair + 2], (rows, LANES))
+    return jnp.where(first, one, two)
+
+
+def step_sizes(dt_raw, head_ref):
+    raw = dt_raw.astype(F32) + head_ref[0:1, :]
+    dt = jnp.maximum(raw, 0.0) + jnp.log1p(jnp.exp(-jnp.abs(raw)))
+    rate = -jnp.exp(head_ref[1:2, :])
+    cum = mm(triangle(True, F32), dt * rate, precision=HIGHEST)
+    return raw, dt, rate, cum
+
+
+def conv_block(xm_ref, prev, taps_ref, at):
+    lanes = slice(at, at + LANES)
+    whole = jnp.concatenate([prev[8:16, lanes].astype(F32), xm_ref[:, lanes].astype(F32)], axis=0)
+    total = jnp.broadcast_to(taps_ref[4:5, lanes], (BLOCK, LANES))
+    shifted = []
+    for tap in range(4):
+        back = 3 - tap
+        piece = whole if back == 0 else pltpu.roll(whole, back, 0)
+        piece = piece[8:]
+        shifted.append(piece)
+        total = total + taps_ref[tap : tap + 1, lanes] * piece
+    return shifted, total
+
+
+def states_kernel(
+    inner, size, xm_ref, prev_ref, halo_ref, taps_ref, head_ref, conv_ref, enter_ref, out_ref,
+    total_ref, state_ref,
 ):
-    tokens = conv_in.shape[0]
-    taps = kernel.shape[0]
-    inner = conv_in.shape[1] - 2 * state_width
-    size = inner // heads
-    span = min(256, tokens)
-    n_span = tokens // span
-    tail = conv_in[tokens - (taps - 1) :]
-    halo = before(tail, run, seat, whole_run)
-    padded = jnp.concatenate([halo, conv_in], axis=0)
-    total = jnp.zeros_like(conv_in) + offset[None, :]
-    for tap in range(taps):
-        total = total + kernel[tap][None, :] * padded[tap : tap + tokens]
-    conv = jax.nn.silu(total)
-    x = conv[:, :inner].reshape(n_span, span, heads, size)
-    b = conv[:, inner : inner + state_width].reshape(n_span, span, state_width)
-    c = conv[:, inner + state_width :].reshape(n_span, span, state_width)
-    dt = jax.nn.softplus(dt_raw + dt_offset)
-    rate = -jnp.exp(a_log)
-    dt_b = jnp.transpose(dt.reshape(n_span, span, heads), (0, 2, 1))
-    cum = jnp.cumsum(dt_b * rate[None, :, None], axis=2)
-    scores = jnp.einsum("cin,cjn->cij", c, b, precision=HIGHEST)
-    ids = jnp.arange(span)
-    lower = (ids[:, None] >= ids[None, :])[None, None]
-    diff = cum[:, :, :, None] - cum[:, :, None, :]
-    weighted = jnp.where(lower, jnp.exp(jnp.where(lower, diff, 0.0)), 0.0)
-    weighted = weighted * scores[:, None] * dt_b[:, :, None, :]
-    intra = jnp.einsum(
-        "chij,cjhp->cihp", weighted.astype(jnp.bfloat16), x.astype(jnp.bfloat16),
-        preferred_element_type=jnp.float32,
-    )
-    last = cum[:, :, -1]
-    tail_weight = jnp.exp(last[:, :, None] - cum) * dt_b
-    xw = x * jnp.transpose(tail_weight, (0, 2, 1))[..., None]
-    states = jnp.einsum(
-        "cjn,cjhp->chnp", b.astype(jnp.bfloat16), xw.astype(jnp.bfloat16),
-        preferred_element_type=jnp.float32,
-    )
-    state = jnp.zeros_like(states[0])
-    entering = []
-    for k in range(n_span):
-        entering.append(state)
-        state = jnp.exp(last[k])[:, None, None] * state + states[k]
-    enter_run = carried(state, jnp.sum(last, axis=0), run, seat, whole_run)
-    gone = jnp.zeros_like(last[0])
-    shifted = []
-    for k in range(n_span):
-        shifted.append(entering[k] + jnp.exp(gone)[:, None, None] * enter_run)
-        gone = gone + last[k]
-    entering = jnp.stack(shifted)
-    inter = jnp.einsum(
-        "cin,chnp->cihp", c.astype(jnp.bfloat16), entering.astype(jnp.bfloat16),
-        preferred_element_type=jnp.float32,
-    ) * jnp.transpose(jnp.exp(cum), (0, 2, 1))[..., None]
-    out = (intra + inter + skip[None, None, :, None] * x).reshape(tokens, inner)
-    return out
-
-
-def before(tail, run, seat, whole_run):
+    step = pl.program_id(0)
+
+    @pl.when(step == 0)
+    def _():
+        state_ref[...] = jnp.zeros_like(state_ref)
+        total_ref[...] = jnp.zeros_like(total_ref)
+
+    prev = jnp.where(step == 0, halo_ref[...].astype(F32), prev_ref[...].astype(F32))
+    channels = conv_ref.shape[1]
+    for at in range(0, channels, LANES):
+        _, total = conv_block(xm_ref, prev, taps_ref, at)
+        conv_ref[:, at : at + LANES] = low(total * sigmoid(total))
+    _, dt, _, cum = step_sizes(xm_ref[:, channels : channels + LANES], head_ref)
+    last = cum[BLOCK - 1 : BLOCK, :]
+    tail = jnp.exp(last - cum) * dt
+    gone = jnp.exp(last)
+    total_ref[...] = total_ref[...] + last
+    first = first_lanes(BLOCK, size)
+    first_row = first_lanes(1, size)
+    b_turned = conv_ref[:, inner : inner + LANES].astype(F32).T.astype(BF16)
+    for pair in range(inner // LANES):
+        lanes = slice(pair * LANES, (pair + 1) * LANES)
+        state = state_ref[:, lanes]
+        enter_ref[:, lanes] = low(state)
+        weighted = conv_ref[:, lanes].astype(F32) * spread(tail, pair, first)
+        state = state * spread(gone, pair, first_row) + mm(b_turned, low(weighted))
+        state_ref[:, lanes] = state
+        out_ref[:, lanes] = low(state)
+
+
+def scan_kernel(
+    inner, size, conv_ref, raw_ref, enter_ref, into_ref, gate_ref, head_ref, gain_ref, whole_ref,
+    y_ref, n_ref, total_ref, gated_ref,
+):
+    step = pl.program_id(0)
+
+    @pl.when(step == 0)
+    def _():
+        total_ref[...] = jnp.zeros_like(total_ref)
+
+    _, dt, _, cum = step_sizes(raw_ref[...], head_ref)
+    cum_turned = cum.T
+    before_block = jnp.exp(total_ref[0:1, :])
+    total_ref[...] = total_ref[...] + cum[BLOCK - 1 : BLOCK, :]
+    first = first_lanes(BLOCK, size)
+    first_row = first_lanes(1, size)
+    b = conv_ref[:, inner : inner + LANES]
+    c = conv_ref[:, inner + LANES : inner + 2 * LANES]
+    scores = mm(c, b, ((1,), (1,))) * triangle(True, F32)
+    squares = jnp.zeros((BLOCK, LANES), F32)
+    for pair in range(inner // LANES):
+        lanes = slice(pair * LANES, (pair + 1) * LANES)
+        x = conv_ref[:, lanes].astype(F32)
+        entering = low(
+            enter_ref[:, lanes].astype(F32)
+            + into_ref[:, lanes].astype(F32) * spread(before_block, pair, first_row)
+        )
+        whole_ref[:, lanes] = entering
+        xd = x * spread(dt, pair, first)
+        weights = []
+        for head in (2 * pair, 2 * pair + 1):
+            diff = jnp.minimum(cum[:, head : head + 1] - cum_turned[head : head + 1, :], 0.0)
+            weights.append(low(jnp.exp(diff) * scores))
+        halves = jnp.concatenate([jnp.where(first, xd, 0.0), jnp.where(first, 0.0, xd)], axis=0)
+        y = mm(jnp.concatenate(weights, axis=1), low(halves))
+        y = y + mm(c, entering) * jnp.exp(spread(cum, pair, first))
+        y = low(y + x * spread(head_ref[2:3, :], pair, first_row))
+        y_ref[:, lanes] = y
+        z = gate_ref[:, lanes].astype(F32)
+        g = y.astype(F32) * z * sigmoid(z)
+        gated_ref[:, lanes] = g
+        squares = squares + g * g
+    scale = lax.rsqrt(jnp.sum(squares, axis=1, keepdims=True) / inner + EPSILON)
+    for at in range(0, inner, LANES):
+        lanes = slice(at, at + LANES)
+        n_ref[:, lanes] = low(gated_ref[:, lanes] * scale * gain_ref[0:1, lanes])
+
+
+def gate_kernel(
+    inner, size, gn_ref, y_ref, gate_ref, c_ref, raw_ref, head_ref, gain_ref, gy_ref, gz_ref,
+    gain_sum_ref, into_ref, total_ref, acc_ref,
+):
+    step = pl.program_id(0)
+
+    @pl.when(step == 0)
+    def _():
+        total_ref[...] = jnp.zeros_like(total_ref)
+        gain_sum_ref[...] = jnp.zeros_like(gain_sum_ref)
+        acc_ref[...] = jnp.zeros_like(acc_ref)
+
+    _, _, _, cum = step_sizes(raw_ref[...], head_ref)
+    whole = cum + total_ref[0:1, :]
+    total_ref[...] = total_ref[...] + cum[BLOCK - 1 : BLOCK, :]
+    decay = jnp.exp(whole)
+    squares = jnp.zeros((BLOCK, LANES), F32)
+    products = jnp.zeros((BLOCK, LANES), F32)
+    for at in range(0, inner, LANES):
+        lanes = slice(at, at + LANES)
+        z = gate_ref[:, lanes].astype(F32)
+        g = y_ref[:, lanes].astype(F32) * z * sigmoid(z)
+        squares = squares + g * g
+        products = products + g * gn_ref[:, lanes].astype(F32) * gain_ref[0:1, lanes]
+    scale = lax.rsqrt(jnp.sum(squares, axis=1, keepdims=True) / inner + EPSILON)
+    pull = jnp.sum(products, axis=1, keepdims=True) / inner * scale * scale
+    c_turned = c_ref[...].astype(F32).T.astype(BF16)
+    first = first_lanes(BLOCK, size)
+    for pair in range(inner // LANES):
+        lanes = slice(pair * LANES, (pair + 1) * LANES)
+        z = gate_ref[:, lanes].astype(F32)
+        y = y_ref[:, lanes].astype(F32)
+        gn = gn_ref[:, lanes].astype(F32)
+        sig = sigmoid(z)
+        open_z = z * sig
+        g = y * open_z
+        gain_sum_ref[:, lanes] = gain_sum_ref[:, lanes] + jnp.sum(
+            gn * g * scale, axis=0, keepdims=True
+        )
+        grad = scale * (gn * gain_ref[0:1, lanes] - g * pull)
+        gy = low(grad * open_z)
+        gy_ref[:, lanes] = gy
+        gz_ref[:, lanes] = low(grad * y * sig * (1.0 + z * (1.0 - sig)))
+        acc = acc_ref[:, lanes] + mm(c_turned, low(gy.astype(F32) * spread(decay, pair, first)))
+        acc_ref[:, lanes] = acc
+        into_ref[:, lanes] = low(acc)
+
+
+def back_kernel(
+    inner, size, steps, gy_ref, conv_ref, xm_ref, prev_ref, halo_ref, whole_ref, after_ref,
+    taps_ref, head_ref, heads_map_ref, gxm_ref, tap_sum_ref, head_sum_ref, edge_ref, state_ref,
+    cum_grad_ref, dt_grad_ref, next_ref,
+):
+    step = pl.program_id(0)
+    channels = conv_ref.shape[1]
+
+    @pl.when(step == 0)
+    def _():
+        state_ref[...] = after_ref[...].astype(F32)
+        tap_sum_ref[...] = jnp.zeros_like(tap_sum_ref)
+        head_sum_ref[...] = jnp.zeros_like(head_sum_ref)
+        next_ref[...] = jnp.zeros_like(next_ref)
+
+    raw, dt, rate, cum = step_sizes(xm_ref[:, channels : channels + LANES], head_ref)
+    cum_turned = cum.T
+    last = cum[BLOCK - 1 : BLOCK, :]
+    tail = jnp.exp(last - cum)
+    gone = jnp.exp(last)
+    lower = triangle(True, F32)
+    first = first_lanes(BLOCK, size)
+    first_row = first_lanes(1, size)
+    b = conv_ref[:, inner : inner + LANES]
+    c = conv_ref[:, inner + LANES : inner + 2 * LANES]
+    c_turned = c.astype(F32).T.astype(BF16)
+    scores = mm(c, b, ((1,), (1,))) * lower
+    grad_scores = jnp.zeros((BLOCK, BLOCK), F32)
+    grad_b = jnp.zeros((BLOCK, LANES), F32)
+    grad_c = jnp.zeros((BLOCK, LANES), F32)
+    end_rows = []
+    skip_rows = []
+    prev = jnp.where(step == steps - 1, halo_ref[...].astype(F32), prev_ref[...].astype(F32))
+
+    def conv_back(at, grad_conv):
+        lanes = slice(at, at + LANES)
+        shifted, total = conv_block(xm_ref, prev, taps_ref, at)
+        sig = sigmoid(total)
+        g = grad_conv * sig * (1.0 + total * (1.0 - sig))
+        rows = [jnp.sum(g * piece, axis=0, keepdims=True) for piece in shifted]
+        rows.append(jnp.sum(g, axis=0, keepdims=True))
+        rows.append(jnp.zeros((3, LANES), F32))
+        tap_sum_ref[:, lanes] = tap_sum_ref[:, lanes] + jnp.concatenate(rows, axis=0)
+        long = jnp.concatenate([g, next_ref[:, lanes]], axis=0)
+        out = taps_ref[3:4, lanes] * g
+        for ahead in (1, 2, 3):
+            out = out + taps_ref[3 - ahead : 4 - ahead, lanes] * pltpu.roll(
+                long, BLOCK + 8 - ahead, 0
+            )[:BLOCK]
+        gxm_ref[:, lanes] = low(out)
+        next_ref[:, lanes] = g[0:8]
+
+    for pair in range(inner // LANES):
+        lanes = slice(pair * LANES, (pair + 1) * LANES)
+        x = conv_ref[:, lanes].astype(F32)
+        gy_low = gy_ref[:, lanes]
+        gy = gy_low.astype(F32)
+        dt_here = spread(dt, pair, first)
+        cum_here = spread(cum, pair, first)
+        tail_here = spread(tail, pair, first)
+        xd_low = low(x * dt_here)
+        xd = xd_low.astype(F32)
+        grad_state = state_ref[:, lanes]
+        state_low = low(grad_state)
+        entering = whole_ref[:, lanes]
+        decays = []
+        weights = []
+        for head in (2 * pair, 2 * pair + 1):
+            diff = jnp.minimum(cum[:, head : head + 1] - cum_turned[head : head + 1, :], 0.0)
+            decay = jnp.exp(diff)
+            decays.append(decay)
+            weights.append(decay * scores)
+        xd_halves = low(jnp.concatenate([jnp.where(first, xd, 0.0), jnp.where(first, 0.0, xd)], 0))
+        gy_halves = low(jnp.concatenate([jnp.where(first, gy, 0.0), jnp.where(first, 0.0, gy)], 0))
+        y = mm(low(jnp.concatenate(weights, axis=1)), xd_halves)
+        grad_weights = mm(gy_halves, xd_low, ((1,), (1,)))
+        grad_scores = (
+            grad_scores + decays[0] * grad_weights[:BLOCK] + decays[1] * grad_weights[BLOCK:]
+        )
+        turned = low(jnp.concatenate([weights[0].T, weights[1].T], axis=1))
+        grad_xd = mm(turned, gy_halves)
+        grown = jnp.exp(cum_here)
+        y = y + mm(c, entering) * grown
+        from_state = mm(b, state_low) * tail_here
+        grad_xd = grad_xd + from_state
+        gy_grown = low(gy * grown)
+        grad_c = grad_c + mm(gy_grown, entering, ((1,), (1,)))
+        grad_b = grad_b + mm(low(xd * tail_here), state_low, ((1,), (1,)))
+        gone_here = spread(gone, pair, first_row)
+        end_rows.append(
+            jnp.sum(xd * from_state, axis=0, keepdims=True)
+            + gone_here * jnp.sum(entering.astype(F32) * grad_state, axis=0, keepdims=True)
+        )
+        skip_rows.append(jnp.sum(x * gy, axis=0, keepdims=True))
+        state_ref[:, lanes] = grad_state * gone_here + mm(c_turned, gy_grown)
+        cum_grad_ref[:, lanes] = gy * y - xd * grad_xd
+        dt_grad_ref[:, lanes] = low(x * grad_xd)
+        conv_back(pair * LANES, grad_xd * dt_here + gy * spread(head_ref[2:3, :], pair, first_row))
+    grad_scores = grad_scores * lower
+    grad_c = grad_c + mm(low(grad_scores), b)
+    grad_b = grad_b + mm(low(grad_scores.T), c)
+    conv_back(inner, grad_b)
+    conv_back(inner + LANES, grad_c)
+    heads_map = heads_map_ref[...]
+    rough = low(cum_grad_ref[...])
+    fine = low(cum_grad_ref[...] - rough.astype(F32))
+    grad_cum = mm(rough, heads_map) + mm(fine, heads_map)
+    rows = jnp.concatenate(
+        [jnp.concatenate(end_rows, axis=1), jnp.concatenate(skip_rows, axis=1),
+         jnp.zeros((6, inner), F32)], axis=0)
+    rows = mm(rows, heads_map.astype(F32), precision=HIGHEST)
+    row_ids = lax.broadcasted_iota(jnp.int32, (BLOCK, LANES), 0)
+    grad_cum = grad_cum + jnp.where(row_ids == BLOCK - 1, rows[0:1], 0.0)
+    grad_log = mm(triangle(False, F32), grad_cum, precision=HIGHEST)
+    grad_dt = mm(dt_grad_ref[...], heads_map) + rate * grad_log
+    grad_raw = grad_dt * sigmoid(raw)
+    gxm_ref[:, channels : channels + LANES] = low(grad_raw)
+    if gxm_ref.shape[1] > channels + LANES:
+        rest = gxm_ref.shape[1] - channels - LANES
+        gxm_ref[:, channels + LANES :] = jnp.zeros((BLOCK, rest), BF16)
+    sums = [
+        jnp.sum(grad_raw, axis=0, keepdims=True),
+        jnp.sum(dt * grad_log, axis=0, keepdims=True) * rate,
+        rows[1:2],
+        jnp.zeros((5, LANES), F32),
+    ]
+    head_sum_ref[...] = head_sum_ref[...] + jnp.concatenate(sums, axis=0)
+
+    @pl.when(step == steps - 1)
+    def _():
+        for at in range(0, channels, LANES):
+            lanes = slice(at, at + LANES)
+            long = jnp.concatenate([jnp.zeros((8, LANES), F32), next_ref[:, lanes]], axis=0)
+            out = jnp.zeros((8, LANES), F32)
+            for ahead in (1, 2, 3):
+                out = out + taps_ref[3 - ahead : 4 - ahead, lanes] * pltpu.roll(
+                    long, 16 - ahead, 0
+                )[:8]
+            edge_ref[:, lanes] = out
+
+
+def call(kernel, steps, operands, outs, scratch, flops, turned=False):
+    at = (lambda i: steps - 1 - i) if turned else (lambda i: i)
+
+    def spec(block, index):
+        return pl.BlockSpec(block, lambda i: index(at(i)))
+
+    moved = sum(a.size * a.dtype.itemsize for a, _, _ in operands)
+    return pl.pallas_call(
+        kernel,
+        grid=(steps,),
+        in_specs=[spec(block, index) for _, block, index in operands],
+        out_specs=[spec(block, index) for _, _, block, index in outs],
+        out_shape=[jax.ShapeDtypeStruct(shape, kind) for shape, kind, _, _ in outs],
+        scratch_shapes=[pltpu.VMEM(shape, kind) for shape, kind in scratch],
+        compiler_params=pltpu.CompilerParams(
+            vmem_limit_bytes=LIMIT, dimension_semantics=("arbitrary",)
+        ),
+        cost_estimate=pl.CostEstimate(flops=flops, bytes_accessed=moved, transcendentals=0),
+    )(*[a for a, _, _ in operands])
+
+
+def rowwise(i):
+    return (i, 0)
+
+
+def fixed(i):
+    return (0, 0)
+
+
+def run_states(xm, halo, taps, head, inner, size):
+    tokens, wide = xm.shape
+    channels = taps.shape[1]
+    steps = tokens // BLOCK
+    per = BLOCK // 16
+    return call(
+        functools.partial(states_kernel, inner, size),
+        steps,
+        [
+            (xm, (BLOCK, wide), rowwise),
+            (xm, (16, wide), lambda i: (jnp.maximum(i * per - 1, 0), 0)),
+            (halo, (16, wide), fixed),
+            (taps, (8, channels), fixed),
+            (head, (8, LANES), fixed),
+        ],
+        [
+            ((tokens, channels), BF16, (BLOCK, channels), rowwise),
+            ((steps * LANES, inner), BF16, (LANES, inner), rowwise),
+            ((LANES, inner), BF16, (LANES, inner), fixed),
+            ((8, LANES), F32, (8, LANES), fixed),
+        ],
+        [((LANES, inner), F32)],
+        2 * tokens * LANES * inner * 4,
+    )
+
+
+def run_scan(conv, xm, enter, into, gate, head, gain, inner, size):
+    tokens, channels = conv.shape
+    steps = tokens // BLOCK
+    at = channels // LANES
+    return call(
+        functools.partial(scan_kernel, inner, size),
+        steps,
+        [
+            (conv, (BLOCK, channels), rowwise),
+            (xm, (BLOCK, LANES), lambda i: (i, at)),
+            (enter, (LANES, inner), rowwise),
+            (into, (LANES, inner), fixed),
+            (gate, (BLOCK, inner), rowwise),
+            (head, (8, LANES), fixed),
+            (gain, (8, inner), fixed),
+        ],
+        [
+            ((steps * LANES, inner), BF16, (LANES, inner), rowwise),
+            ((tokens, inner), BF16, (BLOCK, inner), rowwise),
+            ((tokens, inner), BF16, (BLOCK, inner), rowwise),
+        ],
+        [((8, LANES), F32), ((BLOCK, inner), F32)],
+        2 * tokens * LANES * inner * 8,
+    )
+
+
+def run_gate(gn, y, gate, conv, xm, head, gain, inner, size):
+    tokens, channels = conv.shape
+    steps = tokens // BLOCK
+    c_at = channels // LANES - 1
+    return call(
+        functools.partial(gate_kernel, inner, size),
+        steps,
+        [
+            (gn, (BLOCK, inner), rowwise),
+            (y, (BLOCK, inner), rowwise),
+            (gate, (BLOCK, inner), rowwise),
+            (conv, (BLOCK, LANES), lambda i: (i, c_at)),
+            (xm, (BLOCK, LANES), lambda i: (i, c_at + 1)),
+            (head, (8, LANES), fixed),
+            (gain, (8, inner), fixed),
+        ],
+        [
+            ((tokens, inner), BF16, (BLOCK, inner), rowwise),
+            ((tokens, inner), BF16, (BLOCK, inner), rowwise),
+            ((8, inner), F32, (8, inner), fixed),
+            ((LANES, inner), BF16, (LANES, inner), fixed),
+        ],
+        [((8, LANES), F32), ((LANES, inner), F32)],
+        2 * tokens * LANES * inner * 4,
+    )
+
+
+def run_back(gy, conv, xm, halo, whole, after, taps, head, heads_map, inner, size):
+    tokens, channels = conv.shape
+    wide = xm.shape[1]
+    steps = tokens // BLOCK
+    per = BLOCK // 16
+    return call(
+        functools.partial(back_kernel, inner, size, steps),
+        steps,
+        [
+            (gy, (BLOCK, inner), rowwise),
+            (conv, (BLOCK, channels), rowwise),
+            (xm, (BLOCK, wide), rowwise),
+            (xm, (16, wide), lambda i: (jnp.maximum(i * per - 1, 0), 0)),
+            (halo, (16, wide), fixed),
+            (whole, (LANES, inner), rowwise),
+            (after, (LANES, inner), fixed),
+            (taps, (8, channels), fixed),
+            (head, (8, LANES), fixed),
+            (heads_map, (inner, LANES), fixed),
+        ],
+        [
+            ((tokens, wide), BF16, (BLOCK, wide), rowwise),
+            ((8, channels), F32, (8, channels), fixed),
+            ((8, LANES), F32, (8, LANES), fixed),
+            ((8, channels), F32, (8, channels), fixed),
+        ],
+        [
+            ((LANES, inner), F32),
+            ((BLOCK, inner), F32),
+            ((BLOCK, inner), BF16),
+            ((8, channels), F32),
+        ],
+        2 * tokens * LANES * inner * 24,
+        turned=True,
+    )
+
+
+def of_sequence(array, seat, whole_run):
+    n_seq, micro = whole_run
+    every = lax.all_gather(array, ("seq", "section"), axis=0)
+    every = every.reshape((n_seq // micro, micro, 2) + array.shape)
+    mine = lax.dynamic_index_in_dim(every, seat % micro, 1, keepdims=False)
+    return mine.reshape((-1,) + array.shape)
+
+
+def neighbour(array, run, seat, whole_run, by):
     n_seq, micro = whole_run
     if n_seq == micro:
-        return lax.ppermute(tail, "section", [(0, 1)])
-    every = lax.all_gather(tail, ("seq", "section"), axis=0)
-    every = every.reshape((n_seq // micro, micro, 2) + tail.shape)
-    mine = lax.dynamic_index_in_dim(every, seat % micro, 1, keepdims=False)
-    mine = mine.reshape((-1,) + tail.shape)
-    past = lax.dynamic_index_in_dim(mine, jnp.maximum(run - 1, 0), 0, keepdims=False)
-    return jnp.where(run > 0, past, 0.0)
-
-
-def carried(state, total, run, seat, whole_run):
+        return lax.ppermute(array, "section", [(0, 1)] if by < 0 else [(1, 0)])
+    every = of_sequence(array, seat, whole_run)
+    count = every.shape[0]
+    found = lax.dynamic_index_in_dim(every, jnp.clip(run + by, 0, count - 1), 0, keepdims=False)
+    return jnp.where((run + by >= 0) & (run + by < count), found, 0)
+
+
+def carried(state, total, run, seat, whole_run, by, size):
     n_seq, micro = whole_run
     if n_seq == micro:
-        return lax.ppermute(state.astype(jnp.bfloat16), "section", [(0, 1)]).astype(jnp.float32)
-    every = lax.all_gather(state, ("seq", "section"), axis=0)
-    totals = lax.all_gather(total, ("seq", "section"), axis=0)
-    every = every.reshape((n_seq // micro, micro, 2) + state.shape)
-    totals = totals.reshape((n_seq // micro, micro, 2) + total.shape)
-    mine = lax.dynamic_index_in_dim(every, seat % micro, 1, keepdims=False)
-    mine = mine.reshape((-1,) + state.shape)
-    gone = lax.dynamic_index_in_dim(totals, seat % micro, 1, keepdims=False)
-    gone = jnp.cumsum(gone.reshape((-1,) + total.shape), axis=0)
-    upto = lax.dynamic_index_in_dim(gone, jnp.maximum(run - 1, 0), 0, keepdims=False)
-    early = (jnp.arange(mine.shape[0]) < run)[:, None]
-    decay = jnp.where(early, jnp.exp(jnp.where(early, upto[None] - gone, 0.0)), 0.0)
-    return jnp.einsum("kh,khnp->hnp", decay, mine, precision=HIGHEST)
+        return neighbour(state, run, seat, whole_run, by)
+    states = of_sequence(state, seat, whole_run).astype(jnp.float32)
+    totals = of_sequence(total[0], seat, whole_run)
+    count = states.shape[0]
+    gone = jnp.cumsum(totals, axis=0)
+    ids = jnp.arange(count)
+    if by < 0:
+        edge = lax.dynamic_index_in_dim(gone, jnp.maximum(run - 1, 0), 0, keepdims=False)
+        between = edge[None] - gone
+        used = (ids < run)[:, None]
+    else:
+        edge = lax.dynamic_index_in_dim(gone, run, 0, keepdims=False)
+        between = gone - totals - edge[None]
+        used = (ids > run)[:, None]
+    decay = jnp.where(used, jnp.exp(jnp.where(used, between, 0.0)), 0.0)
+    heads = state.shape[1] // size
+    decay = jnp.repeat(decay[:, :heads], size, axis=1)
+    return jnp.sum(decay[:, None, :] * states, axis=0).astype(jnp.bfloat16)
 
 
 def local(
@@ -281,7 +707,6 @@
     inner = gated_gain.shape[1]
     heads = dt_bias.shape[1]
     channels = conv_weight.shape[2]
-    state_width = (channels - inner) // 2
     proj = in_weight.shape[2]
     mixed = proj - inner
     padded = -(-mixed // (2 * LANES)) * 2 * LANES
@@ -322,29 +747,42 @@
     positions = run * tokens + jnp.arange(tokens)
     valid = (positions < length).astype(jnp.float32)[:, None]
 
+    size = inner // heads
+    lane_heads = lax.broadcasted_iota(jnp.int32, (inner, LANES), 0) // size
+    heads_map = (lane_heads == lax.broadcasted_iota(jnp.int32, (inner, LANES), 1)).astype(
+        jnp.bfloat16
+    )
+
+    def table(rows, wide):
+        rows = [jnp.pad(row, (0, wide - row.shape[0])) for row in rows]
+        return jnp.concatenate([jnp.stack(rows), jnp.zeros((8 - len(rows), wide), jnp.float32)])
+
+    tables = []
+    for gain_in, kernel, offset, dt_offset, alog, skip, gain_out in params:
+        tables.append(
+            (
+                jnp.concatenate([kernel, offset[None], jnp.zeros((3, channels), jnp.float32)]),
+                table([dt_offset, alog, skip], LANES),
+                table([gain_out], inner),
+            )
+        )
+
     kept = []
     layer_outs = []
     for layer in range(2):
-        gain_in, kernel, offset, dt_offset, alog, skip, gain_out = params[layer]
+        gain_in = params[layer][0]
+        taps, head, gain = tables[layer]
         hidden = hidden_bf.astype(jnp.float32)
         normed_in = norm_rows(hidden, gain_in).astype(jnp.bfloat16)
-        projected = times(normed_in, mix_layers[layer], section).astype(jnp.bfloat16)
-        gate_z = times(normed_in, gate_layers[layer], section)
-        conv_in = projected[:, :channels]
-        dt_raw = projected[:, channels:mixed]
-
-        def run_mixer(*args):
-            return mixer(*args, heads, state_width, seat, run, whole_run)
-
-        mix_args = (
-            conv_in.astype(jnp.float32), dt_raw.astype(jnp.float32), kernel, offset, dt_offset,
-            alog, skip,
-        )
-        scanned = run_mixer(*mix_args).astype(jnp.bfloat16)
-        normed_out = gate_norm(scanned.astype(jnp.float32), gate_z, gain_out).astype(jnp.bfloat16)
-        branch = times(normed_out, out_layers[layer], section)
+        xm = times(normed_in, mix_layers[layer], section, jnp.bfloat16)
+        gate = times(normed_in, gate_layers[layer], section, jnp.bfloat16)
+        halo = neighbour(xm[tokens - 16 :], run, seat, whole_run, -1)
+        conv, enter, state, total = run_states(xm, halo, taps, head, inner, size)
+        into = carried(state, total, run, seat, whole_run, -1, size)
+        whole, y, normed_out = run_scan(conv, xm, enter, into, gate, head, gain, inner, size)
+        branch = times(normed_out, out_layers[layer], section, jnp.float32)
         layer_out = (valid * (hidden + branch)).astype(jnp.bfloat16)
-        kept.append((hidden_bf, normed_in, gate_z, mix_args, run_mixer, scanned, normed_out))
+        kept.append((hidden_bf, normed_in, gate, xm, halo, conv, total, whole, y, normed_out))
         layer_outs.append(layer_out)
         hidden_bf = layer_out
     acts = to_pieces(layer_outs[0], layer_outs[1], section, micro, n_seq)
@@ -353,26 +791,27 @@
     shard_gate, shard_mix, shard_out = [None] * 2, [None] * 2, [None] * 2
     small, grad_outs = [None] * 2, [None] * 2
     for layer in (1, 0):
-        gain_in, kernel, offset, dt_offset, alog, skip, gain_out = params[layer]
-        hid, normed_in, gate_z, mix_args, run_mixer, scanned, normed_out = kept[layer]
+        gain_in = params[layer][0]
+        taps, head, gain = tables[layer]
+        hid, normed_in, gate, xm, halo, conv, total, whole, y, normed_out = kept[layer]
         masked = grad_bf.astype(jnp.float32) * valid
         grad_branch = masked.astype(jnp.bfloat16)
         shard_out[layer] = weight_sum(normed_out, grad_branch, section, False)
-        grad_normed = times_back(grad_branch, out_layers[layer], section)
-        _, pull_gate = jax.vjp(gate_norm, scanned.astype(jnp.float32), gate_z, gain_out)
-        grad_scanned, grad_gate, grad_gain_out = pull_gate(grad_normed)
-        grad_y = grad_scanned.astype(jnp.bfloat16).astype(jnp.float32)
-        _, pull_mixer = jax.vjp(run_mixer, *mix_args)
-        g_conv, g_dt, g_kernel, g_offset, g_dto, g_alog, g_skip = pull_mixer(grad_y)
-        grad_gate = grad_gate.astype(jnp.bfloat16)
+        grad_normed = times_back(grad_branch, out_layers[layer], section).astype(jnp.bfloat16)
+        grad_y, grad_gate, gain_sum, left = run_gate(
+            grad_normed, y, gate, conv, xm, head, gain, inner, size
+        )
+        after = carried(left, total, run, seat, whole_run, 1, size)
         shard_gate[layer] = weight_sum(normed_in, grad_gate, section, True)
-        grad_mix = jnp.concatenate(
-            [
-                g_conv.astype(jnp.bfloat16),
-                g_dt.astype(jnp.bfloat16),
-                jnp.zeros((tokens, padded - mixed), jnp.bfloat16),
-            ],
-            axis=1,
+        grad_mix, tap_sum, head_sum, edge = run_back(
+            grad_y, conv, xm, halo, whole, after, taps, head, heads_map, inner, size
+        )
+        edge = neighbour(edge, run, seat, whole_run, 1)
+        fixed_rows = grad_mix[tokens - 16 :, :channels].astype(jnp.float32) + jnp.pad(
+            edge, ((8, 0), (0, 0))
+        )
+        grad_mix = lax.dynamic_update_slice(
+            grad_mix, fixed_rows.astype(jnp.bfloat16), (tokens - 16, 0)
         )
         grad_normed_in = times_back(grad_gate, gate_layers[layer], section) + times_back(
             grad_mix, mix_layers[layer], section
@@ -383,7 +822,10 @@
         shard_mix[layer] = weight_sum(normed_in, grad_mix, section, False)
         grad_outs[layer] = grad_bf
         small[layer] = jnp.concatenate(
-            [grad_gain_in, g_kernel.reshape(-1), g_offset, g_dto, g_alog, g_skip, grad_gain_out]
+            [
+                grad_gain_in, tap_sum[:4].reshape(-1), tap_sum[4], head_sum[0, :heads],
+                head_sum[1, :heads], head_sum[2, :heads], gain_sum[0],
+            ]
         )
     grads = to_pieces(grad_outs[0], grad_outs[1], section, micro, n_seq)
     mine = jnp.where(section == 0, small[0], small[1])

time: 1270 us -> 937 us (0.74)
  local copies, waits for them, and re-layouts: 237 us -> 40.1 us
  other arithmetic: 185 us -> 38 us
  Pallas kernels: 0 us -> 120 us
  matrix products: 215 us -> 110 us
    pallas_call x0 -> x8, Pallas kernels: none -> 120 us  [call(): pl.pallas_call(kernel, grid=(steps,), in_specs=[spec(block, index) for _,...]
    dot_general x36 -> x12, matrix products: 117 us -> 30.6 us  [the longest x6 21.1 us: times(): jnp.dot(rows, weight.other, preferred_element_type=jnp.float32).astype(kind)]
    reshape x22 -> x4, local copies, waits for them, and re-layouts: 68.1 us -> 0.07 us  [the longest x2 0.04 us: unpack(): parts[1] = parts[1].reshape(conv_weight.shape[1:])]
    reduce_sum x14 -> x0, other arithmetic: 49.2 us -> none  [the longest x2 26.7 us: mixer(): total = total + kernel[tap][None, :] * padded[tap:tap + tokens]]
    convert_element_type x8 -> x0, local copies, waits for them, and re-layouts: 48.9 us -> none  [the longest x4 34 us: local(): scanned.astype(jnp.float32)]
    concatenate x8 -> x6, local copies, waits for them, and re-layouts: 42.8 us -> 0.34 us  [the longest x2 0.17 us: local(): jnp.concatenate([grad_gain_in, tap_sum[:4].reshape(-1), tap_sum[4], head_...]
    mul x13 -> x0, other arithmetic: 39.6 us -> none  [the longest x2 15.4 us: mixer(): total = total + kernel[tap][None, :] * padded[tap:tap + tokens]]
    convert_element_type x11 -> x1, other arithmetic: 27.9 us -> 1.67 us  [local(): (lane_heads == lax.broadcasted_iota(jnp.int32, (inner, LANES), 1)).astype...]
  transfers between devices with their start and end apart: 72 -> 70, of which waited for: 32 -> 30; matrix products, arithmetic and copies ran while one was open for 47% -> 18% of each run, Pallas kernels for 0% -> 10%
where the time goes in v2:
time: 937 us; the launch traced here: 928 us
  waiting for transfers between devices  524 us (56%)
  Pallas kernels  120 us (13%)
  matrix products  110 us (12%)
  starting transfers between devices  80.2 us (9%)
  local copies, waits for them, and re-layouts  40.1 us (4%)
  other arithmetic  38 us (4%)
  between operations  16.3 us (2%)
    all_gather x6, waiting for transfers between devices, fetch(): own = lax.all_gather(piece, BOTH, axis=0, tiled=True)  342 us
    ppermute x28, waiting for transfers between devices, exchanged(): return lax.ppermute(array, axis, pairs)  140 us
    pallas_call x8, Pallas kernels, call(): pl.pallas_call(kernel, grid=(steps,), in_specs=[spec(block, index) for _,...  120 us
    ppermute x28, starting transfers between devices, exchanged(): return lax.ppermute(array, axis, pairs)  42.7 us
    all_to_all x2, waiting for transfers between devices, to_sequences(): lax.all_to_all(mine, 'seq', 0, 0, axis_index_groups=seat_groups(n_seq, mi...  28.1 us
    dot_general x6, matrix products, times_back(): jnp.einsum('tp,dp->td', other, weight.other, preferred_element_type=jnp.f...  23 us
    dot_general x6, matrix products, times(): jnp.dot(rows, weight.other, preferred_element_type=jnp.float32).astype(kind)  21.1 us
    unnamed x169, local copies, waits for them, and re-layouts  19.6 us
  transfers between devices with their start and end apart: 70, of which 30 were waited for; matrix products, arithmetic and copies ran while one was open for 18% of the time, Pallas kernels for 10%

profile of v2, /device:TPU:0, one launch (start us, length us, event | category | flops | bytes accessed | tf_op | source)
XLA Modules:
  0.0 928.1 jit_solution(1954182173423680694)
XLA Ops:
  19.5 6.0 all-to-all-start
  32.8 28.1 %all-to-all-done = bf16[4,128,1024]{2,1,0:T(8,128)(2,1)S(1)} async-done(((bf16[4,128,1024]{2,1,0:T(8,128)(2,1)}), bf16[4,128,1024]{2,1,0:T(8,128)(2,1)S(1)}, u32[]{:S(2)}, u32[]{:S(2)}) %all-to-all-start) | async-done | bytes 1048608 | tf_op jit(solution)/shard_map/all_to_all | solution.py:35
  64.5 36.8 %all-gather.7.cloned.1.call-done = bf16[1024,1280]{1,0:T(8,128)(2,1)} async-done(((bf16[64,1280]{1,0:T(8,128)(2,1)}), bf16[1024,1280]{1,0:T(8,128)(2,1)}) %all-gather.7.cloned.1.call-update) | async-done | bytes 2621456 | tf_op jit(solution)/shard_map/all_gather | solution.py:74
  101.4 63.0 %all-gather.9.cloned.1.call-done = bf16[1024,1024]{1,0:T(8,128)(2,1)} async-done(((bf16[64,1024]{1,0:T(8,128)(2,1)}), bf16[1024,1024]{1,0:T(8,128)(2,1)}) %all-gather.9.cloned.1.call-update) | async-done | bytes 2097168 | tf_op jit(solution)/shard_map/all_gather | solution.py:74
  173.7 52.8 %all-gather.15.cloned.1.call-done = bf16[1024,1024]{1,0:T(8,128)(2,1)} async-done(((bf16[64,1024]{1,0:T(8,128)(2,1)}), bf16[1024,1024]{1,0:T(8,128)(2,1)}) %all-gather.15.cloned.1.call-update) | async-done | bytes 2097168 | tf_op jit(solution)/shard_map/all_gather | solution.py:74
  226.6 62.0 %all-gather.11.cloned.1.call-done = bf16[2048,512]{1,0:T(8,128)(2,1)} async-done(((bf16[128,512]{1,0:T(8,128)(2,1)}), bf16[2048,512]{1,0:T(8,128)(2,1)}) %all-gather.11.cloned.1.call-update) | async-done | bytes 2097168 | tf_op jit(solution)/shard_map/all_gather | solution.py:74
  288.6 62.0 %all-gather.17.cloned.1.call-done = bf16[2048,512]{1,0:T(8,128)(2,1)} async-done(((bf16[128,512]{1,0:T(8,128)(2,1)}), bf16[2048,512]{1,0:T(8,128)(2,1)}) %all-gather.17.cloned.1.call-update) | async-done | bytes 2097168 | tf_op jit(solution)/shard_map/all_gather | solution.py:74
  350.6 65.8 %all-gather.13.cloned.1.call-done = bf16[1024,1280]{1,0:T(8,128)(2,1)} async-done(((bf16[64,1280]{1,0:T(8,128)(2,1)}), bf16[1024,1280]{1,0:T(8,128)(2,1)}) %all-gather.13.cloned.1.call-update) | async-done | bytes 2621456 | tf_op jit(solution)/shard_map/all_gather | solution.py:74
  428.5 8.8 shard_map.203
  441.8 11.1 %shard_map.204 = (bf16[512,2048]{1,0:T(8,128)(2,1)S(1)}, bf16[512,2048]{1,0:T(8,128)(2,1)S(1)}, bf16[512,2048]{1,0:T(8,128)(2,1)}) custom-call(bf16[512,2304]{1,0:T(8,128)(2,1)} %copy-done.2, bf16[512,2560]{1,0:T(8,128)(2,1)} %pad_maximum_fusion.xm_ref.prev_ref.raw_ref, bf16[512,2048]{1,0:T(8,128)(2,1)} %copy-done.6, ...), custom_call_target="tpu_custom_call" | custom-call | flops 2147483648 | bytes 9768960 | tf_op jit(solution)/shard_map/pallas_call | solution.py:508
  452.9 5.0 fusion.141
  478.2 8.7 shard_map.205
  494.6 11.1 %shard_map.206 = (bf16[512,2048]{1,0:T(8,128)(2,1)S(1)}, bf16[512,2048]{1,0:T(8,128)(2,1)S(1)}, bf16[512,2048]{1,0:T(8,128)(2,1)}) custom-call(bf16[512,2304]{1,0:T(8,128)(2,1)} %copy-done.3, bf16[512,2560]{1,0:T(8,128)(2,1)} %pad_maximum_fusion.1.xm_ref.prev_ref.raw_ref, bf16[512,2048]{1,0:T(8,128)(2,1)} %copy-done.7, ...), custom_call_target="tpu_custom_call" | custom-call | flops 2147483648 | bytes 9768960 | tf_op jit(solution)/shard_map/pallas_call | solution.py:508
  507.0 9.7 %shard_map.207 = (bf16[512,2048]{1,0:T(8,128)(2,1)S(1)}, bf16[512,2048]{1,0:T(8,128)(2,1)S(1)}, f32[8,2048]{1,0:T(8,128)S(1)}, bf16[128,2048]{1,0:T(8,128)(2,1)S(1)}) custom-call(bf16[512,2048]{1,0:T(8,128)(2,1)} %add_convert_fusion.7.gn_ref, bf16[512,2048]{1,0:T(8,128)(2,1)} %copy-done.5, bf16[512,2048]{1,0:T(8,128)(2,1)} %pad_maximum_fusion.3.gate_ref, ...), custom_call_target="tpu_custom_call" | custom-call | flops 1073741824 | bytes 11341824 | tf_op jit(solution)/shard_map/pallas_call | solution.py:508
  527.9 4.4 fusion.56
  537.5 29.9 %shard_map.208 = (bf16[512,2560]{1,0:T(8,128)(2,1)}, f32[8,2304]{1,0:T(8,128)S(1)}, f32[8,128]{1,0:T(8,128)S(1)}, f32[8,2304]{1,0:T(8,128)S(1)}) custom-call(bf16[512,2048]{1,0:T(8,128)(2,1)S(1)} %get-tuple-element.49.gy_ref, bf16[512,2304]{1,0:T(8,128)(2,1)} %copy-done.3, bf16[512,2560]{1,0:T(8,128)(2,1)} %pad_maximum_fusion.1.xm_ref.prev_ref.raw_ref, ...), custom_call_target="tpu_custom_call" | custom-call | flops 6442450944 | bytes 13004800 | tf_op jit(solution)/shard_map/pallas_call | solution.py:508
  587.9 10.3 %shard_map.209 = (bf16[512,2048]{1,0:T(8,128)(2,1)S(1)}, bf16[512,2048]{1,0:T(8,128)(2,1)S(1)}, f32[8,2048]{1,0:T(8,128)S(1)}, bf16[128,2048]{1,0:T(8,128)(2,1)}) custom-call(bf16[512,2048]{1,0:T(8,128)(2,1)} %add_convert_fusion.6.gn_ref, bf16[512,2048]{1,0:T(8,128)(2,1)} %copy-done.4, bf16[512,2048]{1,0:T(8,128)(2,1)} %pad_maximum_fusion.2.gate_ref, ...), custom_call_target="tpu_custom_call" | custom-call | flops 1073741824 | bytes 11341824 | tf_op jit(solution)/shard_map/pallas_call | solution.py:508
  602.7 4.7 fusion.47
  612.8 30.1 %shard_map.210 = (bf16[512,2560]{1,0:T(8,128)(2,1)}, f32[8,2304]{1,0:T(8,128)S(1)}, f32[8,128]{1,0:T(8,128)S(1)}, f32[8,2304]{1,0:T(8,128)S(1)}) custom-call(bf16[512,2048]{1,0:T(8,128)(2,1)S(1)} %copy-done.15, bf16[512,2304]{1,0:T(8,128)(2,1)} %copy-done.2, bf16[512,2560]{1,0:T(8,128)(2,1)} %pad_maximum_fusion.xm_ref.prev_ref.raw_ref, ...), custom_call_target="tpu_custom_call" | custom-call | flops 6442450944 | bytes 13004800 | tf_op jit(solution)/shard_map/pallas_call | solution.py:508
  652.9 4.7 fusion.24
  657.9 5.0 convolution_convert_fusion
  699.4 5.0 all-to-all-start.3
  719.1 11.7 %collective-permute-done.33 = bf16[2,2,2,64,1024]{4,3,0,1,2:T(8,128)(2,1)S(1)} collective-permute-done((bf16[2,2,2,64,1024]{4,3,0,1,2:T(8,128)(2,1)}, bf16[2,2,2,64,1024]{4,3,0,1,2:T(8,128)(2,1)S(1)}, u32[]{:S(2)}, u32[]{:S(2)}) %collective-permute-start.33) | collective-permute-done | bytes 1048608 | tf_op jit(solution)/shard_map/ppermute | solution.py:120
  742.2 25.7 %collective-permute-done.34 = bf16[2,2,64,1024]{3,2,0,1:T(8,128)(2,1)S(1)} collective-permute-done((bf16[2,2,64,1024]{3,2,0,1:T(8,128)(2,1)S(1)}, bf16[2,2,64,1024]{3,2,0,1:T(8,128)(2,1)S(1)}, u32[]{:S(2)}, u32[]{:S(2)}) %collective-permute-start.34) | collective-permute-done | bytes 524320 | tf_op jit(solution)/shard_map/ppermute | solution.py:120
  783.9 26.9 %collective-permute-done.29 = bf16[2,2,64,1024]{3,2,0,1:T(8,128)(2,1)S(1)} collective-permute-done((bf16[2,2,64,1024]{3,2,0,1:T(8,128)(2,1)S(1)}, bf16[2,2,64,1024]{3,2,0,1:T(8,128)(2,1)S(1)}, u32[]{:S(2)}, u32[]{:S(2)}) %collective-permute-start.29) | collective-permute-done | bytes 524320 | tf_op jit(solution)/shard_map/ppermute | solution.py:120
  815.5 7.2 collective-permute-done.30
  824.2 7.3 collective-permute-done.52
  849.6 4.5 all-to-all-start.1
  854.1 6.4 collective-permute-done.40
  866.6 29.4 %collective-permute-done.41 = bf16[2,64,1280]{2,1,0:T(8,128)(2,1)S(1)} collective-permute-done((bf16[2,64,1280]{2,1,0:T(8,128)(2,1)S(1)}, bf16[2,64,1280]{2,1,0:T(8,128)(2,1)S(1)}, u32[]{:S(2)}, u32[]{:S(2)}) %collective-permute-start.41) | collective-permute-done | bytes 327712 | tf_op jit(solution)/shard_map/ppermute | solution.py:120
  896.1 5.1 collective-permute-start.42
  902.1 9.7 %collective-permute-done.47 = bf16[64,1280]{1,0:T(8,128)(2,1)S(1)} collective-permute-done((bf16[64,1280]{1,0:T(8,128)(2,1)S(1)}, bf16[64,1280]{1,0:T(8,128)(2,1)S(1)}, u32[]{:S(2)}, u32[]{:S(2)}) %collective-permute-start.47) | collective-permute-done | bytes 163872 | tf_op jit(solution)/shard_map/ppermute | solution.py:120
  (480 shorter events, 252.9 us)
Async XLA Ops:
  7.2 94.1 %all-gather.7.cloned.1.call-start = ((), (), s32[]{:S(2)}) async-start(), calls=%async_computation.4 | async-start | bytes 2785280 | tf_op jit(solution)/shard_map/all_gather | solution.py:74
  10.9 153.5 %all-gather.9.cloned.1.call-start = ((), (), s32[]{:S(2)}) async-start(), calls=%async_computation.5 | async-start | bytes 2228224 | tf_op jit(solution)/shard_map/all_gather | solution.py:74
  14.2 212.4 %all-gather.15.cloned.1.call-start = ((), (), s32[]{:S(2)}) async-start(), calls=%async_computation.8 | async-start | bytes 2228224 | tf_op jit(solution)/shard_map/all_gather | solution.py:74
  14.9 273.7 %all-gather.11.cloned.1.call-start = ((), (), s32[]{:S(2)}) async-start(), calls=%async_computation.6 | async-start | bytes 2228224 | tf_op jit(solution)/shard_map/all_gather | solution.py:74
  17.2 333.4 %all-gather.17.cloned.1.call-start = ((), (), s32[]{:S(2)}) async-start(), calls=%async_computation.9 | async-start | bytes 2228224 | tf_op jit(solution)/shard_map/all_gather | solution.py:74
  19.5 41.3 %all-to-all-start = ((bf16[4,128,1024]{2,1,0:T(8,128)(2,1)}), bf16[4,128,1024]{2,1,0:T(8,128)(2,1)S(1)}, u32[]{:S(2)}, u32[]{:S(2)}) async-start(bf16[4,128,1024]{2,1,0:T(8,128)(2,1)} %dynamic-slice_bitcast_fusion.1), calls=%async_computation | async-start | bytes 2097152 | tf_op jit(solution)/shard_map/all_to_all | solution.py:35
  25.6 390.8 %all-gather.13.cloned.1.call-start = ((), (), s32[]{:S(2)}) async-start(), calls=%async_computation.7 | async-start | bytes 2785280 | tf_op jit(solution)/shard_map/all_gather | solution.py:74
  60.9 104.4 %all-to-all-start.2 = ((bf16[4,128,1024]{2,1,0:T(8,128)(2,1)}), bf16[4,128,1024]{2,1,0:T(8,128)(2,1)S(1)}, u32[]{:S(2)}, u32[]{:S(2)}) async-start(bf16[4,128,1024]{2,1,0:T(8,128)(2,1)} %dynamic-slice_bitcast_fusion), calls=%async_computation.2 | async-start | bytes 2097152 | tf_op jit(solution)/shard_map/all_to_all | solution.py:35
  101.3 317.9 %collective-permute-start.3 = (bf16[1024,1280]{1,0:T(8,128)(2,1)}, bf16[1024,1280]{1,0:T(8,128)(2,1)}, u32[]{:S(2)}, u32[]{:S(2)}) collective-permute-start(bf16[1024,1280]{1,0:T(8,128)(2,1)} %all-gather.7.cloned.1.call-done), channel_id=1, source_target_pairs={{0,16},{16,0},{1,17},{17,1},{2,18},{18,2},{3,19},{19,3},{4,20},{20... | collective-permute-start | bytes 7864328 | tf_op jit(solution)/shard_map/ppermute | solution.py:18
  164.4 252.0 %collective-permute-start.7 = (bf16[1024,1024]{1,0:T(8,128)(2,1)}, bf16[1024,1024]{1,0:T(8,128)(2,1)}, u32[]{:S(2)}, u32[]{:S(2)}) collective-permute-start(bf16[1024,1024]{1,0:T(8,128)(2,1)} %all-gather.9.cloned.1.call-done), channel_id=1, source_target_pairs={{0,16},{16,0},{1,17},{17,1},{2,18},{18,2},{3,19},{19,3},{4,20},{20... | collective-permute-start | bytes 6291464 | tf_op jit(solution)/shard_map/ppermute | solution.py:18
  226.6 242.0 %collective-permute-start.13 = (bf16[1024,1024]{1,0:T(8,128)(2,1)}, bf16[1024,1024]{1,0:T(8,128)(2,1)}, u32[]{:S(2)}, u32[]{:S(2)}) collective-permute-start(bf16[1024,1024]{1,0:T(8,128)(2,1)} %all-gather.15.cloned.1.call-done), channel_id=1, source_target_pairs={{0,16},{16,0},{1,17},{17,1},{2,18},{18,2},{3,19},{19,3},{4,20},{20... | collective-permute-start | bytes 6291464 | tf_op jit(solution)/shard_map/ppermute | solution.py:18
  288.6 164.3 %collective-permute-start.9 = (bf16[2048,512]{1,0:T(8,128)(2,1)}, bf16[2048,512]{1,0:T(8,128)(2,1)}, u32[]{:S(2)}, u32[]{:S(2)}) collective-permute-start(bf16[2048,512]{1,0:T(8,128)(2,1)} %all-gather.11.cloned.1.call-done), channel_id=1, source_target_pairs={{0,16},{16,0},{1,17},{17,1},{2,18},{18,2},{3,19},{19,3},{4,20},{20... | collective-permute-start | bytes 6291464 | tf_op jit(solution)/shard_map/ppermute | solution.py:18
  350.6 124.7 %collective-permute-start.14 = (bf16[2048,512]{1,0:T(8,128)(2,1)}, bf16[2048,512]{1,0:T(8,128)(2,1)}, u32[]{:S(2)}, u32[]{:S(2)}) collective-permute-start(bf16[2048,512]{1,0:T(8,128)(2,1)} %all-gather.17.cloned.1.call-done), channel_id=1, source_target_pairs={{0,16},{16,0},{1,17},{17,1},{2,18},{18,2},{3,19},{19,3},{4,20},{20... | collective-permute-start | bytes 6291464 | tf_op jit(solution)/shard_map/ppermute | solution.py:18
  416.4 44.9 %collective-permute-start.10 = (bf16[1024,1280]{1,0:T(8,128)(2,1)}, bf16[1024,1280]{1,0:T(8,128)(2,1)}, u32[]{:S(2)}, u32[]{:S(2)}) collective-permute-start(bf16[1024,1280]{1,0:T(8,128)(2,1)} %all-gather.13.cloned.1.call-done), channel_id=1, source_target_pairs={{0,16},{16,0},{1,17},{17,1},{2,18},{18,2},{3,19},{19,3},{4,20},{20... | collective-permute-start | bytes 7864328 | tf_op jit(solution)/shard_map/ppermute | solution.py:18
  523.9 161.0 %collective-permute-start.32 = (bf16[1024,1024]{1,0:T(8,128)(2,1)}, bf16[1024,1024]{1,0:T(8,128)(2,1)}, u32[]{:S(2)}, u32[]{:S(2)}) collective-permute-start(bf16[1024,1024]{1,0:T(8,128)(2,1)} %convolution_convert_fusion.8), channel_id=1, source_target_pairs={{0,16},{16,0},{1,17},{17,1},{2,18},{18,2},{3,19},{19,3},{4,20},{20... | collective-permute-start | bytes 6291464 | tf_op jit(solution)/shard_map/ppermute | solution.py:18
  525.0 165.9 %collective-permute-start.54 = (bf16[2048,512]{1,0:T(8,128)(2,1)}, bf16[2048,512]{1,0:T(8,128)(2,1)}, u32[]{:S(2)}, u32[]{:S(2)}) collective-permute-start(bf16[2048,512]{1,0:T(8,128)(2,1)} %convolution_convert_fusion.2), channel_id=1, source_target_pairs={{0,16},{16,0},{1,17},{17,1},{2,18},{18,2},{3,19},{19,3},{4,20},{20... | collective-permute-start | bytes 6291464 | tf_op jit(solution)/shard_map/ppermute | solution.py:18
  668.0 41.6 %collective-permute-start.27 = (bf16[1024,1024]{1,0:T(8,128)(2,1)}, bf16[1024,1024]{1,0:T(8,128)(2,1)}, u32[]{:S(2)}, u32[]{:S(2)}) collective-permute-start(bf16[1024,1024]{1,0:T(8,128)(2,1)} %convolution_convert_fusion.9), channel_id=1, source_target_pairs={{0,16},{16,0},{1,17},{17,1},{2,18},{18,2},{3,19},{19,3},{4,20},{20... | collective-permute-start | bytes 6291464 | tf_op jit(solution)/shard_map/ppermute | solution.py:18
  668.2 46.2 %collective-permute-start.49 = (bf16[2048,512]{1,0:T(8,128)(2,1)}, bf16[2048,512]{1,0:T(8,128)(2,1)}, u32[]{:S(2)}, u32[]{:S(2)}) collective-permute-start(bf16[2048,512]{1,0:T(8,128)(2,1)} %convolution_convert_fusion.3), channel_id=1, source_target_pairs={{0,16},{16,0},{1,17},{17,1},{2,18},{18,2},{3,19},{19,3},{4,20},{20... | collective-permute-start | bytes 6291464 | tf_op jit(solution)/shard_map/ppermute | solution.py:18
  681.7 55.3 %collective-permute-start.43 = (bf16[1024,1280]{1,0:T(8,128)(2,1)}, bf16[1024,1280]{1,0:T(8,128)(2,1)}, u32[]{:S(2)}, u32[]{:S(2)}) collective-permute-start(bf16[1024,1280]{1,0:T(8,128)(2,1)} %convolution_convert_fusion), channel_id=1, source_target_pairs={{0,16},{16,0},{1,17},{17,1},{2,18},{18,2},{3,19},{19,3},{4,20},{20... | collective-permute-start | bytes 7864328 | tf_op jit(solution)/shard_map/ppermute | solution.py:18
  696.9 76.6 %collective-permute-start.38 = (bf16[1024,1280]{1,0:T(8,128)(2,1)}, bf16[1024,1280]{1,0:T(8,128)(2,1)}, u32[]{:S(2)}, u32[]{:S(2)}) collective-permute-start(bf16[1024,1280]{1,0:T(8,128)(2,1)} %convolution_convert_fusion.1), channel_id=1, source_target_pairs={{0,16},{16,0},{1,17},{17,1},{2,18},{18,2},{3,19},{19,3},{4,20},{20... | collective-permute-start | bytes 7864328 | tf_op jit(solution)/shard_map/ppermute | solution.py:18
  699.4 148.9 %all-to-all-start.3 = ((bf16[4,256,1024]{2,1,0:T(8,128)(2,1)}), bf16[4,256,1024]{2,1,0:T(8,128)(2,1)S(1)}, u32[]{:S(2)}, u32[]{:S(2)}) async-start(bf16[4,256,1024]{2,1,0:T(8,128)(2,1)} %bitcast.331), calls=%async_computation.3 | async-start | bytes 4194304 | tf_op jit(solution)/shard_map/all_to_all | solution.py:55
  714.4 56.7 %collective-permute-start.28 = (bf16[2,2,2,64,1024]{4,3,0,1,2:T(8,128)(2,1)S(1)}, bf16[2,2,2,64,1024]{4,3,0,1,2:T(8,128)(2,1)S(1)}, u32[]{:S(2)}, u32[]{:S(2)}) collective-permute-start(bf16[2,2,2,64,1024]{4,3,0,1,2:T(8,128)(2,1)S(1)} %bitcast.348), channel_id=1, source_target_pairs={{0,2},{1,3},{2,0},{3,1},{4,6},{5,7},{6,4},{7,5},{8,10},{9,11},{10,... | collective-permute-start | bytes 3145736 | tf_op jit(solution)/shard_map/ppermute | solution.py:120
  730.7 41.1 %collective-permute-start.50 = (bf16[2,2,2,128,512]{4,3,0,1,2:T(8,128)(2,1)S(1)}, bf16[2,2,2,128,512]{4,3,0,1,2:T(8,128)(2,1)S(1)}, u32[]{:S(2)}, u32[]{:S(2)}) collective-permute-start(bf16[2,2,2,128,512]{4,3,0,1,2:T(8,128)(2,1)S(1)} %bitcast.349), channel_id=1, source_target_pairs={{0,1},{1,0},{2,3},{3,2},{4,5},{5,4},{6,7},{7,6},{8,9},{9,8},{10,11... | collective-permute-start | bytes 3145736 | tf_op jit(solution)/shard_map/ppermute | solution.py:120
  767.9 65.2 %collective-permute-start.44 = (bf16[2,2,2,64,1280]{4,3,0,1,2:T(8,128)(2,1)S(1)}, bf16[2,2,2,64,1280]{4,3,0,1,2:T(8,128)(2,1)S(1)}, u32[]{:S(2)}, u32[]{:S(2)}) collective-permute-start(bf16[2,2,2,64,1280]{4,3,0,1,2:T(8,128)(2,1)S(1)} %bitcast.344), channel_id=1, source_target_pairs={{0,1},{1,0},{2,3},{3,2},{4,5},{5,4},{6,7},{7,6},{8,9},{9,8},{10,11... | collective-permute-start | bytes 3932168 | tf_op jit(solution)/shard_map/ppermute | solution.py:120
  771.9 39.0 %collective-permute-start.29 = (bf16[2,2,64,1024]{3,2,0,1:T(8,128)(2,1)S(1)}, bf16[2,2,64,1024]{3,2,0,1:T(8,128)(2,1)S(1)}, u32[]{:S(2)}, u32[]{:S(2)}) collective-permute-start(bf16[2,2,64,1024]{3,2,0,1:T(8,128)(2,1)S(1)} %dynamic-slice_bitcast_fusion.7), channel_id=1, source_target_pairs={{0,1},{1,0},{2,3},{3,2},{4,5},{5,4},{6,7},{7,6},{8,9},{9,8},{10,11... | collective-permute-start | bytes 1572872 | tf_op jit(solution)/shard_map/ppermute | solution.py:120
  773.5 40.2 %collective-permute-start.51 = (bf16[2,2,128,512]{3,2,0,1:T(8,128)(2,1)S(1)}, bf16[2,2,128,512]{3,2,0,1:T(8,128)(2,1)S(1)}, u32[]{:S(2)}, u32[]{:S(2)}) collective-permute-start(bf16[2,2,128,512]{3,2,0,1:T(8,128)(2,1)S(1)} %dynamic-slice_bitcast_fusion.5), channel_id=1, source_target_pairs={{0,2},{1,3},{2,0},{3,1},{4,6},{5,7},{6,4},{7,5},{8,10},{9,11},{10,... | collective-permute-start | bytes 1572872 | tf_op jit(solution)/shard_map/ppermute | solution.py:120
  778.5 63.2 %collective-permute-start.39 = (bf16[2,2,2,64,1280]{4,3,0,1,2:T(8,128)(2,1)S(1)}, bf16[2,2,2,64,1280]{4,3,0,1,2:T(8,128)(2,1)S(1)}, u32[]{:S(2)}, u32[]{:S(2)}) collective-permute-start(bf16[2,2,2,64,1280]{4,3,0,1,2:T(8,128)(2,1)S(1)} %bitcast.345), channel_id=1, source_target_pairs={{0,1},{1,0},{2,3},{3,2},{4,5},{5,4},{6,7},{7,6},{8,9},{9,8},{10,11... | collective-permute-start | bytes 3932168 | tf_op jit(solution)/shard_map/ppermute | solution.py:120
  781.2 54.0 %collective-permute-start.36 = (bf16[64,1024]{1,0:T(8,128)(2,1)S(1)}, bf16[64,1024]{1,0:T(8,128)(2,1)S(1)}, u32[]{:S(2)}, u32[]{:S(2)}) collective-permute-start(bf16[64,1024]{1,0:T(8,128)(2,1)S(1)} %dynamic-slice_bitcast_fusion.20), channel_id=1, source_target_pairs={{0,8},{4,12},{8,0},{12,4},{1,9},{5,13},{9,1},{13,5},{2,10},{6,14},... | collective-permute-start | bytes 393224 | tf_op jit(solution)/shard_map/ppermute | solution.py:120
  839.5 61.7 %collective-permute-start.37 = (bf16[64,1024]{1,0:T(8,128)(2,1)}, bf16[64,1024]{1,0:T(8,128)(2,1)}, u32[]{:S(2)}, u32[]{:S(2)}) collective-permute-start(bf16[64,1024]{1,0:T(8,128)(2,1)} %get-tuple-element.74), channel_id=1, source_target_pairs={{0,16},{16,0},{1,17},{17,1},{2,18},{18,2},{3,19},{19,3},{4,20},{20... | collective-permute-start | bytes 393224 | tf_op jit(solution)/shard_map/ppermute | solution.py:18
  841.6 72.2 %collective-permute-start.59 = (bf16[128,512]{1,0:T(8,128)(2,1)S(1)}, bf16[128,512]{1,0:T(8,128)(2,1)S(1)}, u32[]{:S(2)}, u32[]{:S(2)}) collective-permute-start(bf16[128,512]{1,0:T(8,128)(2,1)S(1)} %get-tuple-element.71), channel_id=1, source_target_pairs={{0,16},{16,0},{1,17},{17,1},{2,18},{18,2},{3,19},{19,3},{4,20},{20... | collective-permute-start | bytes 393224 | tf_op jit(solution)/shard_map/ppermute | solution.py:18
  849.6 65.0 %all-to-all-start.1 = ((bf16[4,256,1024]{2,1,0:T(8,128)(2,1)}), bf16[4,256,1024]{2,1,0:T(8,128)(2,1)}, u32[]{:S(2)}, u32[]{:S(2)}) async-start(bf16[4,256,1024]{2,1,0:T(8,128)(2,1)} %bitcast.330), calls=%async_computation.1 | async-start | bytes 4194304 | tf_op jit(solution)/shard_map/all_to_all | solution.py:55
  863.7 48.2 %collective-permute-start.47 = (bf16[64,1280]{1,0:T(8,128)(2,1)S(1)}, bf16[64,1280]{1,0:T(8,128)(2,1)S(1)}, u32[]{:S(2)}, u32[]{:S(2)}) collective-permute-start(bf16[64,1280]{1,0:T(8,128)(2,1)S(1)} %dynamic-slice_bitcast_fusion.16), channel_id=1, source_target_pairs={{0,8},{4,12},{8,0},{12,4},{1,9},{5,13},{9,1},{13,5},{2,10},{6,14},... | collective-permute-start | bytes 491528 | tf_op jit(solution)/shard_map/ppermute | solution.py:120
  (121 other events, 1765.2 us)
Sparse Core Ops, SparseCore 0:
  11.3 89.9 all-gather.6
  104.1 60.2 all-gather.8
  167.2 59.3 all-gather.14
  229.2 59.3 all-gather.10
  291.2 59.3 all-gather.16
  353.7 62.6 all-gather.12

commit v3 on v2

--- a/solution.py
+++ b/solution.py
@@ -28,14 +28,14 @@
     return [list(range(start, start + micro)) for start in range(0, n_seq, micro)]
 
 
-def to_sequences(rows, section, micro, n_seq):
+def to_sequences(rows, section, micro, n_seq, use=()):
     _, t, d = rows.shape
     half = t // 2
     mine = lax.dynamic_slice_in_dim(rows, section * half, half, 1)
     got = lax.all_to_all(
         mine, "seq", 0, 0, axis_index_groups=seat_groups(n_seq, micro), tiled=True
     )
-    pairs = got.reshape(2, micro // 2, half, d)
+    pairs = later(got, use).reshape(2, micro // 2, half, d)
     keep = lax.dynamic_index_in_dim(pairs, section, 0, keepdims=False)
     give = lax.dynamic_index_in_dim(pairs, 1 - section, 0, keepdims=False)
     other = swapped(give)
@@ -44,17 +44,30 @@
     return jnp.stack([first, second], axis=1).reshape(micro * half, d)
 
 
-def to_pieces(first_rows, second_rows, section, micro, n_seq):
-    rows, d = first_rows.shape
-    keep = jnp.where(section == 0, first_rows, second_rows)
-    give = jnp.where(section == 0, second_rows, first_rows)
+def half_pieces(rows, section, micro):
+    count, d = rows.shape
+    half = count // micro
+    chunks = rows.reshape(micro // 2, 2, half, d)
+    keep = lax.dynamic_index_in_dim(chunks, section, 1, keepdims=False)
+    give = lax.dynamic_index_in_dim(chunks, 1 - section, 1, keepdims=False)
     other = swapped(give)
     lo = jnp.where(section == 0, keep, other)
     hi = jnp.where(section == 0, other, keep)
-    whole = jnp.concatenate([lo, hi]).reshape(micro, 2 * rows // micro, d)
+    return jnp.concatenate([lo, hi])
+
+
+def sent_pieces(pieces, micro, n_seq):
     return lax.all_to_all(
-        whole, "seq", 0, 0, axis_index_groups=seat_groups(n_seq, micro), tiled=True
-    )
+        pieces, "seq", 0, 0, axis_index_groups=seat_groups(n_seq, micro), tiled=True
+    )
+
+
+def whole_pieces(first, second, section):
+    keep = jnp.where(section == 0, first, second)
+    other = swapped(jnp.where(section == 0, second, first))
+    lo = jnp.where(section == 0, keep, other)
+    hi = jnp.where(section == 0, other, keep)
+    return jnp.concatenate([lo, hi], axis=1)
 
 
 class Halves:
@@ -63,17 +76,78 @@
         self.other = other
 
 
-def fetch(weight, section):
-    width = weight.shape[1] // 2
-    keep = lax.dynamic_slice_in_dim(weight, section * width, width, 1)
-    give = lax.dynamic_slice_in_dim(weight, (1 - section) * width, width, 1)
-    got = swapped(give)
-    layers = []
-    for layer in range(2):
-        piece = jnp.where(section == layer, keep, got)
-        own = lax.all_gather(piece, BOTH, axis=0, tiled=True)
-        layers.append(Halves(own, swapped(own)))
-    return layers
+class Gather:
+    def __init__(self, array, order):
+        self.hops = hop_list()
+        self.array = array
+        self.order = order
+
+    def step(self, use=(), meet=None):
+        if not self.order:
+            return meet
+        dim = self.order.pop(0)
+        axis, distance = self.hops[dim]
+        side = side_of(axis, distance)
+        got = later(exchanged(self.array, axis, distance), use)
+        if meet is not None:
+            got, meet = lax.optimization_barrier((got, meet))
+        lo = jnp.where(side == 0, self.array, got)
+        hi = jnp.where(side == 0, got, self.array)
+        self.array = jnp.concatenate([lo, hi], axis=dim)
+        return meet
+
+    def part(self, start, end, turned):
+        order = self.order[::-1] if turned else list(self.order)
+        return Gather(self.array[..., start:end], order)
+
+    def whole(self):
+        while self.order:
+            self.step()
+        return self.array.reshape(-1, self.array.shape[-1])
+
+
+def by_side(array, rows):
+    blocks = array.shape[0] // (2 * rows)
+    pair = array.reshape(blocks, 2, rows, array.shape[1])
+    return jnp.concatenate([pair[:, 0], pair[:, 1]], axis=2).reshape(
+        blocks * rows, 2 * array.shape[1]
+    )
+
+
+def by_rows(array, rows):
+    blocks = array.shape[0] // rows
+    width = array.shape[1] // 2
+    sides = array.reshape(blocks, rows, 2 * width)
+    return jnp.stack([sides[..., :width], sides[..., width:]], axis=1).reshape(-1, width)
+
+
+seen = []
+
+
+def later(array, others):
+    if not len(others):
+        return array
+    out = lax.optimization_barrier((array,) + tuple(others))
+    seen.extend(out[1:])
+    return out[0]
+
+
+def nothing_of(tables):
+    total = jnp.zeros((8, LANES), jnp.float32)
+    for values in tables:
+        total = total + jnp.clip(values[:, :LANES], -1.0, 1.0)
+    return total[0] * 0.0
+
+
+def stage(jobs, *arrays):
+    out = lax.optimization_barrier(tuple(arrays_of(jobs)) + arrays)
+    for job, array in zip(jobs, out):
+        job.array = array
+    return out[len(jobs) :]
+
+
+def arrays_of(jobs):
+    return [job.array for job in jobs]
 
 
 def in_order(own, other, section, axis):
@@ -128,44 +202,49 @@
     return (one.astype(jnp.float32) + two.astype(jnp.float32)).astype(jnp.bfloat16)
 
 
-def scatter_sum(array, turned):
-    hops = hop_list()
-    seat_bits = bits_of(lax.axis_size("seq"))
-    order = list(range(seat_bits, len(hops)))
-    order = (order if turned else order[::-1]) + list(range(seat_bits))[::-1]
-    rows = array.shape[0] >> len(hops)
-    array = array.reshape((2,) * len(hops) + (rows, array.shape[1]))
-    left = list(range(len(hops)))
-    for dim in order:
-        axis, distance = hops[dim]
-        at = left.index(dim)
+class Scatter:
+    def __init__(self, array, turned):
+        hops = hop_list()
+        seat_bits = bits_of(lax.axis_size("seq"))
+        order = list(range(seat_bits, len(hops)))
+        self.order = (order if turned else order[::-1]) + list(range(seat_bits))[::-1]
+        self.hops = hops
+        self.left = list(range(len(hops)))
+        self.array = array.reshape(
+            (2,) * len(hops) + (array.shape[0] >> len(hops), array.shape[1])
+        )
+
+    def step(self, start=(), use=()):
+        if not self.order:
+            return
+        dim = self.order.pop(0)
+        axis, distance = self.hops[dim]
+        at = self.left.index(dim)
         side = side_of(axis, distance)
+        array = later(self.array, start)
         give = lax.dynamic_index_in_dim(array, 1 - side, at, keepdims=False)
         keep = lax.dynamic_index_in_dim(array, side, at, keepdims=False)
-        array = add_low(keep, exchanged(give, axis, distance))
-        left.remove(dim)
-    return array
-
-
-def sum_everywhere(array):
-    for axis, distance in hop_list():
-        array = array + exchanged(array, axis, distance)
-    return array
-
-
-def weight_sum(rows, grad, section, turned):
+        self.array = add_low(keep, later(exchanged(give, axis, distance), use))
+        self.left.remove(dim)
+
+    def joined(self, other):
+        out = Scatter.__new__(Scatter)
+        out.hops, out.left, out.order = self.hops, self.left, self.order
+        out.array = jnp.concatenate([self.array, other.array], axis=-1)
+        return out
+
+    def shard(self):
+        while self.order:
+            self.step()
+        return self.array
+
+
+def weight_sum(rows, grad, section):
     own, other = halves_of(grad, section)
     give = jnp.einsum("td,te->de", rows, other, preferred_element_type=jnp.float32)
     got = swapped(give.astype(jnp.bfloat16))
     keep = jnp.einsum("td,te->de", rows, own, preferred_element_type=jnp.float32)
-    return scatter_sum(add_low(keep, got), turned)
-
-
-def place(first, second, section):
-    keep = jnp.where(section == 0, first, second)
-    give = jnp.where(section == 0, second, first)
-    other = swapped(give)
-    return in_order(keep, other, section, 1).astype(jnp.float32)
+    return add_low(keep, got)
 
 
 BLOCK = 128
@@ -498,17 +577,23 @@
             edge_ref[:, lanes] = out
 
 
-def call(kernel, steps, operands, outs, scratch, flops, turned=False):
+def call(kernel, steps, operands, outs, scratch, flops, waits, turned=False):
+    count = len(operands)
+
+    def body(*refs):
+        kernel(*refs[:count], *refs[count + len(waits) :])
+
     at = (lambda i: steps - 1 - i) if turned else (lambda i: i)
 
     def spec(block, index):
         return pl.BlockSpec(block, lambda i: index(at(i)))
 
-    moved = sum(a.size * a.dtype.itemsize for a, _, _ in operands)
+    moved = sum(a.size * a.dtype.itemsize for a, _, _ in operands) // 8
     return pl.pallas_call(
-        kernel,
+        body,
         grid=(steps,),
-        in_specs=[spec(block, index) for _, block, index in operands],
+        in_specs=[spec(block, index) for _, block, index in operands]
+        + [pl.BlockSpec(memory_space=pl.ANY)] * len(waits),
         out_specs=[spec(block, index) for _, _, block, index in outs],
         out_shape=[jax.ShapeDtypeStruct(shape, kind) for shape, kind, _, _ in outs],
         scratch_shapes=[pltpu.VMEM(shape, kind) for shape, kind in scratch],
@@ -516,7 +601,7 @@
             vmem_limit_bytes=LIMIT, dimension_semantics=("arbitrary",)
         ),
         cost_estimate=pl.CostEstimate(flops=flops, bytes_accessed=moved, transcendentals=0),
-    )(*[a for a, _, _ in operands])
+    )(*[a for a, _, _ in operands], *waits)
 
 
 def rowwise(i):
@@ -527,7 +612,7 @@
     return (0, 0)
 
 
-def run_states(xm, halo, taps, head, inner, size):
+def run_states(xm, halo, taps, head, inner, size, waits=()):
     tokens, wide = xm.shape
     channels = taps.shape[1]
     steps = tokens // BLOCK
@@ -549,11 +634,12 @@
             ((8, LANES), F32, (8, LANES), fixed),
         ],
         [((LANES, inner), F32)],
-        2 * tokens * LANES * inner * 4,
-    )
-
-
-def run_scan(conv, xm, enter, into, gate, head, gain, inner, size):
+        tokens * inner * 900,
+        waits,
+    )
+
+
+def run_scan(conv, xm, enter, into, gate, head, gain, inner, size, waits=()):
     tokens, channels = conv.shape
     steps = tokens // BLOCK
     at = channels // LANES
@@ -573,13 +659,15 @@
             ((steps * LANES, inner), BF16, (LANES, inner), rowwise),
             ((tokens, inner), BF16, (BLOCK, inner), rowwise),
             ((tokens, inner), BF16, (BLOCK, inner), rowwise),
+            ((8, LANES), F32, (8, LANES), fixed),
         ],
-        [((8, LANES), F32), ((BLOCK, inner), F32)],
-        2 * tokens * LANES * inner * 8,
-    )
-
-
-def run_gate(gn, y, gate, conv, xm, head, gain, inner, size):
+        [((BLOCK, inner), F32)],
+        tokens * inner * 1100,
+        waits,
+    )
+
+
+def run_gate(gn, y, gate, conv, xm, head, gain, inner, size, waits=()):
     tokens, channels = conv.shape
     steps = tokens // BLOCK
     c_at = channels // LANES - 1
@@ -602,11 +690,12 @@
             ((LANES, inner), BF16, (LANES, inner), fixed),
         ],
         [((8, LANES), F32), ((LANES, inner), F32)],
-        2 * tokens * LANES * inner * 4,
-    )
-
-
-def run_back(gy, conv, xm, halo, whole, after, taps, head, heads_map, inner, size):
+        tokens * inner * 1000,
+        waits,
+    )
+
+
+def run_back(gy, conv, xm, halo, whole, after, taps, head, heads_map, inner, size, waits=()):
     tokens, channels = conv.shape
     wide = xm.shape[1]
     steps = tokens // BLOCK
@@ -638,7 +727,8 @@
             ((BLOCK, inner), BF16),
             ((8, channels), F32),
         ],
-        2 * tokens * LANES * inner * 24,
+        tokens * inner * 3000,
+        waits,
         turned=True,
     )
 
@@ -698,6 +788,7 @@
     gated_gain,
     out_weight,
 ):
+    seen.clear()
     section = lax.axis_index("section")
     seat = lax.axis_index("seq")
     lane = lax.axis_index("wshard")
@@ -713,13 +804,51 @@
     run = (seat // micro) * 2 + section
     whole_run = (n_seq, micro)
 
-    mix_layers = fetch(
-        jnp.pad(in_weight[0, :, inner:], ((0, 0), (0, padded - mixed))), section
-    )
-    gate_layers = fetch(in_weight[0, :, :inner], section)
-    out_layers = fetch(out_weight[0], section)
-    hidden_bf = to_sequences(inputs[:, 0], section, micro, n_seq)
-    cot = to_sequences(cotangent[:, 0], section, micro, n_seq)
+    rows_in = in_weight.shape[1]
+    mix_shard = jnp.pad(in_weight[0, :, inner:], ((0, 0), (0, padded - mixed)))
+    gate_shard = in_weight[0, :, :inner]
+    mix_half, gate_half = padded // 2, inner // 2
+    out_half = out_weight.shape[2] // 2
+
+    def packed(side):
+        return jnp.concatenate(
+            [
+                mix_shard[:, side * mix_half : (side + 1) * mix_half],
+                gate_shard[:, side * gate_half : (side + 1) * gate_half],
+                by_side(out_weight[0, :, side * out_half : (side + 1) * out_half], rows_in),
+            ],
+            axis=1,
+        )
+
+    lo, hi = packed(0), packed(1)
+    keep = jnp.where(section == 0, lo, hi)
+    got = swapped(jnp.where(section == 0, hi, lo))
+    hops = hop_list()
+    seat_bits = bits_of(n_seq)
+    first, second = [
+        Gather(
+            jnp.where(section == layer, keep, got)[(None,) * len(hops)], list(range(len(hops)))
+        )
+        for layer in range(2)
+    ]
+    total_width = lo.shape[1]
+    for bit in range(seat_bits):
+        first.step()
+    (inputs,) = stage([first, second], inputs[:, 0])
+    hidden_bf = to_sequences(inputs, section, micro, n_seq)
+
+    def three(job):
+        end = mix_half + gate_half
+        return [
+            job.part(0, mix_half, False), job.part(mix_half, end, True),
+            job.part(end, total_width, False),
+        ]
+
+    first_mix, first_gate, first_out = three(first)
+    for job in (first_mix, first_gate, first_out):
+        job.step()
+    for bit in range(seat_bits // 2):
+        second.step()
 
     def both_layers(array):
         other = swapped(array)
@@ -768,44 +897,106 @@
         )
 
     kept = []
+    wholes = []
     layer_outs = []
     for layer in range(2):
         gain_in = params[layer][0]
         taps, head, gain = tables[layer]
         hidden = hidden_bf.astype(jnp.float32)
         normed_in = norm_rows(hidden, gain_in).astype(jnp.bfloat16)
-        xm = times(normed_in, mix_layers[layer], section, jnp.bfloat16)
-        gate = times(normed_in, gate_layers[layer], section, jnp.bfloat16)
+        mix_job, gate_job, out_job = layer_jobs = (
+            [first_mix, first_gate, first_out] if layer == 0 else second_jobs
+        )
+        own = mix_job.whole()
+        mix_whole = Halves(own, swapped(own))
+        xm = times(normed_in, mix_whole, section, jnp.bfloat16)
         halo = neighbour(xm[tokens - 16 :], run, seat, whole_run, -1)
-        conv, enter, state, total = run_states(xm, halo, taps, head, inner, size)
+        waits = []
+        if layer == 0:
+            for bit in range(seat_bits - seat_bits // 2):
+                second.step()
+            (xm,) = stage([second], xm)
+            second_jobs = three(second)
+        conv, enter, state, total = run_states(xm, halo, taps, head, inner, size, waits)
         into = carried(state, total, run, seat, whole_run, -1, size)
-        whole, y, normed_out = run_scan(conv, xm, enter, into, gate, head, gain, inner, size)
-        branch = times(normed_out, out_layers[layer], section, jnp.float32)
+        if layer == 1:
+            gate_job.step([total])
+        own = gate_job.whole()
+        gate_whole = Halves(own, swapped(own))
+        out_job.step([total])
+        own = by_rows(out_job.whole(), rows_in)
+        out_whole = Halves(own, swapped(own))
+        wholes.append((mix_whole, gate_whole, out_whole))
+        gate = times(normed_in, gate_whole, section, jnp.bfloat16)
+        if layer == 0:
+            second_jobs[0].step()
+            second_jobs[1].step()
+            waits = arrays_of(second_jobs[:2])
+        else:
+            cot = to_sequences(
+                later(cotangent, [first_flag])[:, 0], section, micro, n_seq, [total]
+            )
+            waits = [cot]
+        whole, y, normed_out, flag = run_scan(
+            conv, xm, enter, into, gate, head, gain, inner, size, waits
+        )
+        branch = times(normed_out, out_whole, section, jnp.float32)
         layer_out = (valid * (hidden + branch)).astype(jnp.bfloat16)
+        if layer == 0:
+            first_flag = flag
+            second_jobs[2].step([flag])
+            layer_out = second_jobs[0].step((), layer_out)
         kept.append((hidden_bf, normed_in, gate, xm, halo, conv, total, whole, y, normed_out))
         layer_outs.append(layer_out)
         hidden_bf = layer_out
-    acts = to_pieces(layer_outs[0], layer_outs[1], section, micro, n_seq)
+    act_one = sent_pieces(half_pieces(layer_outs[0], section, micro), micro, n_seq)
+    act_two = sent_pieces(half_pieces(layer_outs[1], section, micro), micro, n_seq)
 
     grad_bf = cot
-    shard_gate, shard_mix, shard_out = [None] * 2, [None] * 2, [None] * 2
-    small, grad_outs = [None] * 2, [None] * 2
+    small = [None] * 2
     for layer in (1, 0):
         gain_in = params[layer][0]
         taps, head, gain = tables[layer]
         hid, normed_in, gate, xm, halo, conv, total, whole, y, normed_out = kept[layer]
+        mix_whole, gate_whole, out_whole = wholes[layer]
         masked = grad_bf.astype(jnp.float32) * valid
         grad_branch = masked.astype(jnp.bfloat16)
-        shard_out[layer] = weight_sum(normed_out, grad_branch, section, False)
-        grad_normed = times_back(grad_branch, out_layers[layer], section).astype(jnp.bfloat16)
+        sum_out = Scatter(
+            by_side(weight_sum(normed_out, grad_branch, section), rows_in), False
+        )
+        grad_normed = times_back(grad_branch, out_whole, section).astype(jnp.bfloat16)
+        waits = []
+        if layer == 0:
+            two_gate.step()
+            two_out.step()
+            two_both = two_gate.joined(two_out)
+            two_both.step()
+            waits = [two_both.array, two_one.array, two_two.array]
         grad_y, grad_gate, gain_sum, left = run_gate(
-            grad_normed, y, gate, conv, xm, head, gain, inner, size
+            grad_normed, y, gate, conv, xm, head, gain, inner, size, waits
         )
         after = carried(left, total, run, seat, whole_run, 1, size)
-        shard_gate[layer] = weight_sum(normed_in, grad_gate, section, True)
+        sum_gate = Scatter(weight_sum(normed_in, grad_gate, section), True)
+        gate_part = times_back(grad_gate, gate_whole, section)
+        waits = [sum_out.array, sum_gate.array, gate_part[:16, :LANES]]
+        if layer == 0:
+            two_both.step((), [gain_sum])
+            two_one.step((), [gain_sum])
+            two_two.step((), [gain_sum])
+            waits = waits + [two_both.array, two_one.array, two_two.array]
         grad_mix, tap_sum, head_sum, edge = run_back(
-            grad_y, conv, xm, halo, whole, after, taps, head, heads_map, inner, size
-        )
+            grad_y, conv, xm, halo, whole, after, taps, head, heads_map, inner, size, waits
+        )
+        sum_out.step((), [head_sum])
+        sum_gate.step((), [head_sum])
+        if layer == 0:
+            two_one.step((), [head_sum])
+            two_two.step((), [head_sum])
+            edge, pieces_two = stage(
+                [two_one, two_two, sum_out, sum_gate, two_both], edge, pieces_two
+            )
+        else:
+            edge, act_one, act_two = stage([sum_out, sum_gate], edge, act_one, act_two)
         edge = neighbour(edge, run, seat, whole_run, 1)
         fixed_rows = grad_mix[tokens - 16 :, :channels].astype(jnp.float32) + jnp.pad(
             edge, ((8, 0), (0, 0))
@@ -813,31 +1004,76 @@
         grad_mix = lax.dynamic_update_slice(
             grad_mix, fixed_rows.astype(jnp.bfloat16), (tokens - 16, 0)
         )
-        grad_normed_in = times_back(grad_gate, gate_layers[layer], section) + times_back(
-            grad_mix, mix_layers[layer], section
-        )
+
+        def mix_sums():
+            half = weight_sum(normed_in, grad_mix, section)
+            middle = half.shape[1] // 2
+            return Scatter(half[:, :middle], False), Scatter(half[:, middle:], True)
+
+        if layer == 0:
+            sum_one, sum_two = mix_sums()
+            (grad_mix,) = stage([sum_one, sum_two], grad_mix)
+            two_mix = two_one.joined(two_two)
+            for job in (sum_gate, sum_out, two_mix):
+                job.step()
+            one_both = sum_gate.joined(sum_out)
+            for job in (sum_one, sum_two, one_both, two_mix):
+                job.step()
+        grad_normed_in = gate_part + times_back(grad_mix, mix_whole, section)
+        if layer == 1:
+            sum_one, sum_two = mix_sums()
         _, pull_norm = jax.vjp(norm_rows, hid.astype(jnp.float32), gain_in)
         grad_hidden, grad_gain_in = pull_norm(grad_normed_in)
         grad_bf = (masked + grad_hidden).astype(jnp.bfloat16)
-        shard_mix[layer] = weight_sum(normed_in, grad_mix, section, False)
-        grad_outs[layer] = grad_bf
+        if layer == 0:
+            (grad_bf,) = stage([sum_one, sum_two, one_both, two_mix], grad_bf)
         small[layer] = jnp.concatenate(
             [
                 grad_gain_in, tap_sum[:4].reshape(-1), tap_sum[4], head_sum[0, :heads],
                 head_sum[1, :heads], head_sum[2, :heads], gain_sum[0],
             ]
         )
-    grads = to_pieces(grad_outs[0], grad_outs[1], section, micro, n_seq)
+        pieces = half_pieces(grad_bf, section, micro)
+        if layer == 1:
+            pieces_two = sent_pieces(pieces, micro, n_seq)
+            two_gate, two_out, two_one, two_two = sum_gate, sum_out, sum_one, sum_two
+    pieces_one = sent_pieces(pieces, micro, n_seq)
     mine = jnp.where(section == 0, small[0], small[1])
     others = jnp.where(section == 0, small[1], small[0])
-    g = unpack(sum_everywhere(mine + swapped(others)))
+    small_sum = mine + swapped(others)
+    small_hops = hop_list()[::-1]
+    for job in (sum_one, sum_two, one_both, two_mix):
+        job.step()
+    one_mix = sum_one.joined(sum_two)
+    (small_sum,) = stage([one_mix, one_both, two_mix], small_sum)
+    while one_mix.order:
+        one_mix.step()
+        one_both.step()
+        for axis, distance in small_hops[:2]:
+            small_sum = small_sum + exchanged(small_sum, axis, distance)
+        small_hops = small_hops[2:]
+        if len(one_mix.order) == 1:
+            small_sum, pieces_one = stage([one_mix], small_sum, pieces_one)
+    for axis, distance in small_hops:
+        small_sum = small_sum + exchanged(small_sum, axis, distance)
+    one = jnp.concatenate([one_both.shard(), one_mix.shard()], axis=1)
+    two = jnp.concatenate([two_both.shard(), two_mix.shard()], axis=1)
+    keep = jnp.where(section == 0, one, two)
+    other = swapped(jnp.where(section == 0, two, one))
+    lo = jnp.where(section == 0, keep, other).astype(jnp.float32)
+    hi = jnp.where(section == 0, other, keep).astype(jnp.float32)
+    ends = [gate_half, gate_half + 2 * out_half]
     grad_in_weight = jnp.concatenate(
-        [
-            place(shard_gate[0], shard_gate[1], section),
-            place(shard_mix[0], shard_mix[1], section)[:, :mixed],
-        ],
+        [lo[:, : ends[0]], hi[:, : ends[0]], lo[:, ends[1] :], hi[:, ends[1] :]], axis=1
+    )[:, :proj]
+    grad_out_weight = jnp.concatenate(
+        [by_rows(lo[:, ends[0] : ends[1]], rows_in), by_rows(hi[:, ends[0] : ends[1]], rows_in)],
         axis=1,
     )
+    acts = whole_pieces(act_one, act_two, section)
+    grads = whole_pieces(pieces_one, pieces_two, section)
+    g = unpack(small_sum)
+    g[3] = g[3] + nothing_of(seen)[:heads]
     return (
         acts[None, :, None],
         grads[None, :, None],
@@ -849,7 +1085,7 @@
         g[4][None],
         g[5][None],
         g[6][None],
-        place(shard_out[0], shard_out[1], section)[None],
+        grad_out_weight[None],
     )
 
 

time: 937 us -> 690 us (0.74)
  waiting for transfers between devices: 524 us -> 207 us
  other arithmetic: 38 us -> 96.7 us
  starting transfers between devices: 80.2 us -> 97.5 us
  between operations: 16.3 us -> 3.82 us
    all_gather x6 -> x0, waiting for transfers between devices: 342 us -> none  [fetch(): own = lax.all_gather(piece, BOTH, axis=0, tiled=True)]
    ppermute x28 -> x44, waiting for transfers between devices: 140 us -> 203 us  [exchanged(): return lax.ppermute(array, axis, pairs)]
    all_to_all x2, waiting for transfers between devices: 28.1 us -> 0.01 us  [to_sequences(): lax.all_to_all(mine, 'seq', 0, 0, axis_index_groups=seat_groups(n_seq, mi...]
    concatenate x2 -> x25, other arithmetic: 3 us -> 20.1 us  [the longest x16 10 us: step(): self.array = jnp.concatenate([lo, hi], axis=dim)]
    select_n x11 -> x25, other arithmetic: 9.46 us -> 23.8 us  [the longest x15 13.5 us: step(): lo = jnp.where(side == 0, self.array, got)]
    convert_element_type x18 -> x24, other arithmetic: 6.11 us -> 20.3 us  [add_low(): (one.astype(jnp.float32) + two.astype(jnp.float32)).astype(jnp.bfloat16)]
    ppermute x28 -> x44, starting transfers between devices: 42.7 us -> 52.5 us  [exchanged(): return lax.ppermute(array, axis, pairs)]
    unnamed x169 -> x225, local copies, waits for them, and re-layouts: 19.6 us -> 13.1 us
  transfers between devices with their start and end apart: 70 -> 82, of which waited for: 30 -> 27; matrix products, arithmetic and copies ran while one was open for 18% -> 29% of each run, Pallas kernels for 10% -> 16%
where the time goes in v3:
time: 690 us; the launch traced here: 680 us
  waiting for transfers between devices  207 us (30%)
  Pallas kernels  119 us (17%)
  matrix products  113 us (16%)
  starting transfers between devices  97.5 us (14%)
  other arithmetic  96.7 us (14%)
  local copies, waits for them, and re-layouts  42.4 us (6%)
    ppermute x44, waiting for transfers between devices, exchanged(): return lax.ppermute(array, axis, pairs)  203 us
    pallas_call x8, Pallas kernels, call(): pl.pallas_call(body, grid=(steps,), in_specs=[spec(block, index) for _, b...  119 us
    ppermute x44, starting transfers between devices, exchanged(): return lax.ppermute(array, axis, pairs)  52.5 us
    dot_general x6, matrix products, times(): jnp.dot(rows, weight.other, preferred_element_type=jnp.float32).astype(kind)  22.1 us
    dot_general x6, matrix products, times_back(): jnp.einsum('tp,dp->td', other, weight.other, preferred_element_type=jnp.f...  21.4 us
    dot_general x6, matrix products, times_back(): jnp.einsum('tp,dp->td', own, weight.own, preferred_element_type=jnp.float32)  21.3 us
    convert_element_type x24, other arithmetic, add_low(): (one.astype(jnp.float32) + two.astype(jnp.float32)).astype(jnp.bfloat16)  20.3 us
    dot_general x6, matrix products, weight_sum(): jnp.einsum('td,te->de', rows, other, preferred_element_type=jnp.float32)  16.7 us
  transfers between devices with their start and end apart: 82, of which 27 were waited for; matrix products, arithmetic and copies ran while one was open for 29% of the time, Pallas kernels for 16%

profile of v3, /device:TPU:0, one launch (start us, length us, event | category | flops | bytes accessed | tf_op | source)
XLA Modules:
  0.0 680.1 jit_solution(7939060045060696984)
XLA Ops:
  14.0 19.1 %collective-permute-done.1 = bf16[1,1,1,1,64,3328]{5,4,3,2,1,0:T(8,128)(2,1)} collective-permute-done((bf16[1,1,1,1,64,3328]{5,4,3,2,1,0:T(8,128)(2,1)S(1)}, bf16[1,1,1,1,64,3328]{5,4,3,2,1,0:T(8,128)(2,1)}, u32[]{:S(2)}, u32[]{:S(2)}) %collective-permute-start.1) | collective-permute-done | bytes 426016 | tf_op jit(solution)/shard_map/ppermute | solution.py:194
  35.0 19.8 %collective-permute-done.2 = bf16[2,1,1,1,64,3328]{5,4,3,2,1,0:T(8,128)(2,1)S(1)} collective-permute-done((bf16[2,1,1,1,64,3328]{5,4,3,2,1,0:T(8,128)(2,1)S(1)}, bf16[2,1,1,1,64,3328]{5,4,3,2,1,0:T(8,128)(2,1)S(1)}, u32[]{:S(2)}, u32[]{:S(2)}) %collective-permute-start.2) | collective-permute-done | bytes 852000 | tf_op jit(solution)/shard_map/ppermute | solution.py:194
  59.1 5.6 all-to-all-start
  74.0 33.8 %collective-permute-done.3 = bf16[1,1,1,1,64,3328]{5,4,3,2,1,0:T(8,128)(2,1)S(1)} collective-permute-done((bf16[1,1,1,1,64,3328]{5,4,3,2,1,0:T(8,128)(2,1)S(1)}, bf16[1,1,1,1,64,3328]{5,4,3,2,1,0:T(8,128)(2,1)S(1)}, u32[]{:S(2)}, u32[]{:S(2)}) %collective-permute-start.3) | collective-permute-done | bytes 426016 | tf_op jit(solution)/shard_map/ppermute | solution.py:194
  114.4 13.5 %collective-permute-done.4 = bf16[2,1,1,1,64,3328]{5,4,3,2,1,0:T(8,128)(2,1)S(1)} collective-permute-done((bf16[2,1,1,1,64,3328]{5,4,3,2,1,0:T(8,128)(2,1)S(1)}, bf16[2,1,1,1,64,3328]{5,4,3,2,1,0:T(8,128)(2,1)S(1)}, u32[]{:S(2)}, u32[]{:S(2)}) %collective-permute-start.4) | collective-permute-done | bytes 852000 | tf_op jit(solution)/shard_map/ppermute | solution.py:194
  148.9 8.3 %shard_map.203 = (bf16[512,2304]{1,0:T(8,128)(2,1)S(1)}, bf16[512,2048]{1,0:T(8,128)(2,1)S(1)}, bf16[128,2048]{1,0:T(8,128)(2,1)S(1)}, f32[8,128]{1,0:T(8,128)S(1)}) custom-call(bf16[512,2560]{1,0:T(8,128)(2,1)} %pad_maximum_fusion.refs_0_.refs_1_.refs_4_.refs_2_.refs_3_, bf16[512,2560]{1,0:T(8,128)(2,1)} %pad_maximum_fusion.refs_0_.refs_1_.refs_4_.refs_2_.refs_3_, ...), custom_call_target="tpu_custom_call" | custom-call | flops 943718400 | bytes 675328 | tf_op jit(solution)/shard_map/pallas_call | solution.py:592
  172.4 7.7 %collective-permute-done.17 = bf16[2,2,1,1,64,1024]{5,4,3,2,1,0:T(8,128)(2,1)S(1)} collective-permute-done((bf16[2,2,1,1,64,1024]{5,4,3,2,1,0:T(8,128)(2,1)S(1)}, bf16[2,2,1,1,64,1024]{5,4,3,2,1,0:T(8,128)(2,1)S(1)}, u32[]{:S(2)}, u32[]{:S(2)}) %collective-permute-start.17) | collective-permute-done | bytes 524320 | tf_op jit(solution)/shard_map/ppermute | solution.py:194
  185.0 11.1 %shard_map.204 = (bf16[512,2048]{1,0:T(8,128)(2,1)S(1)}, bf16[512,2048]{1,0:T(8,128)(2,1)}, bf16[512,2048]{1,0:T(8,128)(2,1)}, f32[8,128]{1,0:T(8,128)S(1)}) custom-call(bf16[512,2304]{1,0:T(8,128)(2,1)} %copy-done.3, bf16[512,2560]{1,0:T(8,128)(2,1)} %pad_maximum_fusion.refs_0_.refs_1_.refs_4_.refs_2_.refs_3_, bf16[512,2048]{1,0:T(8,128)(2,1)} %copy-done.11, ...), custom_call_target="tpu_custom_call" | custom-call | flops 1153433600 | bytes 1221120 | tf_op jit(solution)/shard_map/pallas_call | solution.py:592
  196.1 4.4 fusion.154
  203.7 10.7 %collective-permute-done.11 = bf16[2,2,2,1,64,1280]{5,4,3,2,1,0:T(8,128)(2,1)S(1)} collective-permute-done((bf16[2,2,2,1,64,1280]{5,4,3,2,1,0:T(8,128)(2,1)S(1)}, bf16[2,2,2,1,64,1280]{5,4,3,2,1,0:T(8,128)(2,1)S(1)}, u32[]{:S(2)}, u32[]{:S(2)}) %collective-permute-start.11) | collective-permute-done | bytes 1310752 | tf_op jit(solution)/shard_map/ppermute | solution.py:194
  220.2 4.6 all-to-all-start.1
  224.9 6.4 collective-permute-done.29
  244.0 8.4 %shard_map.205 = (bf16[512,2304]{1,0:T(8,128)(2,1)S(1)}, bf16[512,2048]{1,0:T(8,128)(2,1)S(1)}, bf16[128,2048]{1,0:T(8,128)(2,1)S(1)}, f32[8,128]{1,0:T(8,128)S(1)}) custom-call(bf16[512,2560]{1,0:T(8,128)(2,1)} %pad_maximum_fusion.1.refs_0_.refs_1_.refs_4_.refs_2_.refs_3_, bf16[512,2560]{1,0:T(8,128)(2,1)} %pad_maximum_fusion.1.refs_0_.refs_1_.refs_4_.refs_2_.refs_3_, ...), custom_call_target="tpu_custom_call" | custom-call | flops 943718400 | bytes 675328 | tf_op jit(solution)/shard_map/pallas_call | solution.py:592
  275.7 11.4 %shard_map.206 = (bf16[512,2048]{1,0:T(8,128)(2,1)S(1)}, bf16[512,2048]{1,0:T(8,128)(2,1)S(1)}, bf16[512,2048]{1,0:T(8,128)(2,1)}, f32[8,128]{1,0:T(8,128)}) custom-call(bf16[512,2304]{1,0:T(8,128)(2,1)} %copy-done.2, bf16[512,2560]{1,0:T(8,128)(2,1)} %pad_maximum_fusion.1.refs_0_.refs_1_.refs_4_.refs_2_.refs_3_, bf16[512,2048]{1,0:T(8,128)(2,1)} %copy-done.5, ...), custom_call_target="tpu_custom_call" | custom-call | flops 1153433600 | bytes 1221120 | tf_op jit(solution)/shard_map/pallas_call | solution.py:592
  287.1 5.0 fusion.155
  299.2 4.3 add_convert_fusion.6.refs_0_
  303.4 9.6 %shard_map.207 = (bf16[512,2048]{1,0:T(8,128)(2,1)S(1)}, bf16[512,2048]{1,0:T(8,128)(2,1)S(1)}, f32[8,2048]{1,0:T(8,128)S(1)}, bf16[128,2048]{1,0:T(8,128)(2,1)S(1)}) custom-call(bf16[512,2048]{1,0:T(8,128)(2,1)} %add_convert_fusion.6.refs_0_, bf16[512,2048]{1,0:T(8,128)(2,1)} %copy-done.10, bf16[512,2048]{1,0:T(8,128)(2,1)} %pad_maximum_fusion.11.refs_4_.refs_2_, ...), custom_call_target="tpu_custom_call" | custom-call | flops 1048576000 | bytes 1417728 | tf_op jit(solution)/shard_map/pallas_call | solution.py:592
  329.2 4.5 fusion.64
  365.8 30.2 %shard_map.208 = (bf16[512,2560]{1,0:T(8,128)(2,1)}, f32[8,2304]{1,0:T(8,128)S(1)}, f32[8,128]{1,0:T(8,128)S(1)}, f32[8,2304]{1,0:T(8,128)S(1)}) custom-call(bf16[512,2048]{1,0:T(8,128)(2,1)S(1)} %copy-done.9, bf16[512,2304]{1,0:T(8,128)(2,1)} %copy-done.2, bf16[512,2560]{1,0:T(8,128)(2,1)} %pad_maximum_fusion.1.refs_0_.refs_1_.refs_4_.refs_2_.refs_3_, ...), custom_call_target="tpu_custom_call" | custom-call | flops 3145728000 | bytes 1625600 | tf_op jit(solution)/shard_map/pallas_call | solution.py:592
  439.3 4.4 all-to-all-start.4
  467.7 10.4 %shard_map.209 = (bf16[512,2048]{1,0:T(8,128)(2,1)S(1)}, bf16[512,2048]{1,0:T(8,128)(2,1)}, f32[8,2048]{1,0:T(8,128)S(1)}, bf16[128,2048]{1,0:T(8,128)(2,1)S(1)}) custom-call(bf16[512,2048]{1,0:T(8,128)(2,1)} %add_convert_fusion.4.refs_0_, bf16[512,2048]{1,0:T(8,128)(2,1)} %get-tuple-element.143.refs_1_, ...), custom_call_target="tpu_custom_call" | custom-call | flops 1048576000 | bytes 1417728 | tf_op jit(solution)/shard_map/pallas_call | solution.py:592
  488.3 10.1 %collective-permute-done.47 = bf16[2,2,2,64,640]{4,3,1,0,2:T(8,128)(2,1)S(1)} collective-permute-done((bf16[2,2,2,64,640]{4,3,1,0,2:T(8,128)(2,1)S(1)}, bf16[2,2,2,64,640]{4,3,1,0,2:T(8,128)(2,1)S(1)}, u32[]{:S(2)}, u32[]{:S(2)}) %collective-permute-start.47) | collective-permute-done | bytes 655392 | tf_op jit(solution)/shard_map/ppermute | solution.py:194
  506.4 30.2 %shard_map.210 = (bf16[512,2560]{1,0:T(8,128)(2,1)}, f32[8,2304]{1,0:T(8,128)S(1)}, f32[8,128]{1,0:T(8,128)S(1)}, f32[8,2304]{1,0:T(8,128)S(1)}) custom-call(bf16[512,2048]{1,0:T(8,128)(2,1)S(1)} %get-tuple-element.146.refs_0_, bf16[512,2304]{1,0:T(8,128)(2,1)} %copy-done.3, bf16[512,2560]{1,0:T(8,128)(2,1)} %pad_maximum_fusion.refs_0_.refs_1_.refs_4_.refs_2_.refs_3_, ...), custom_call_target="tpu_custom_call" | custom-call | flops 3145728000 | bytes 1625600 | tf_op jit(solution)/shard_map/pallas_call | solution.py:592
  556.6 5.6 collective-permute-done.59
  562.4 5.0 collective-permute-done.58
  569.1 11.7 %collective-permute-done.60 = bf16[2,64,2048]{2,1,0:T(8,128)(2,1)S(1)} collective-permute-done((bf16[2,64,2048]{2,1,0:T(8,128)(2,1)S(1)}, bf16[2,64,2048]{2,1,0:T(8,128)(2,1)S(1)}, u32[]{:S(2)}, u32[]{:S(2)}) %collective-permute-start.60) | collective-permute-done | bytes 524320 | tf_op jit(solution)/shard_map/ppermute | solution.py:194
  583.7 4.3 fusion.32
  588.0 5.1 fusion.21
  599.8 9.5 %collective-permute-done.57 = bf16[2,2,2,64,640]{4,3,0,1,2:T(8,128)(2,1)} collective-permute-done((bf16[2,2,2,64,640]{4,3,0,1,2:T(8,128)(2,1)}, bf16[2,2,2,64,640]{4,3,0,1,2:T(8,128)(2,1)}, u32[]{:S(2)}, u32[]{:S(2)}) %collective-permute-start.57) | collective-permute-done | bytes 655392 | tf_op jit(solution)/shard_map/ppermute | solution.py:194
  616.3 8.0 %collective-permute-done.65 = bf16[64,2048]{1,0:T(8,128)(2,1)S(1)} collective-permute-done((bf16[64,2048]{1,0:T(8,128)(2,1)S(1)}, bf16[64,2048]{1,0:T(8,128)(2,1)S(1)}, u32[]{:S(2)}, u32[]{:S(2)}) %collective-permute-start.65) | collective-permute-done | bytes 262176 | tf_op jit(solution)/shard_map/ppermute | solution.py:194
  638.9 15.8 %collective-permute-done.67 = bf16[2,64,1280]{2,1,0:T(8,128)(2,1)S(1)} collective-permute-done((bf16[2,64,1280]{2,1,0:T(8,128)(2,1)S(1)}, bf16[2,64,1280]{2,1,0:T(8,128)(2,1)S(1)}, u32[]{:S(2)}, u32[]{:S(2)}) %collective-permute-start.67) | collective-permute-done | bytes 327712 | tf_op jit(solution)/shard_map/ppermute | solution.py:194
  657.8 6.4 collective-permute-done.72
  (630 shorter events, 331.7 us)
Async XLA Ops:
  59.1 69.9 %all-to-all-start = ((bf16[4,128,1024]{2,1,0:T(8,128)(2,1)}), bf16[4,128,1024]{2,1,0:T(8,128)(2,1)}, u32[]{:S(2)}, u32[]{:S(2)}) async-start(bf16[4,128,1024]{2,1,0:T(8,128)(2,1)} %constant_dynamic-slice_fusion.8), calls=%async_computation | async-start | bytes 2097152 | tf_op jit(solution)/shard_map/all_to_all | solution.py:35
  64.7 43.1 %collective-permute-start.3 = (bf16[1,1,1,1,64,3328]{5,4,3,2,1,0:T(8,128)(2,1)S(1)}, bf16[1,1,1,1,64,3328]{5,4,3,2,1,0:T(8,128)(2,1)S(1)}, u32[]{:S(2)}, u32[]{:S(2)}) collective-permute-start(bf16[1,1,1,1,64,3328]{5,4,3,2,1,0:T(8,128)(2,1)S(1)} %get-tuple-element.106), channel_id=1, source_target_pairs={{0,8},{4,12},{8,0},{12,4},{1,9},{5,13},{9,1},{13,5},{2,10},{6,14},... | collective-permute-start | bytes 1277960 | tf_op jit(solution)/shard_map/ppermute | solution.py:194
  67.8 40.2 %collective-permute-start.14 = (bf16[2,2,1,1,64,1024]{5,4,3,2,1,0:T(8,128)(2,1)S(1)}, bf16[2,2,1,1,64,1024]{5,4,3,2,1,0:T(8,128)(2,1)S(1)}, u32[]{:S(2)}, u32[]{:S(2)}) collective-permute-start(bf16[2,2,1,1,64,1024]{5,4,3,2,1,0:T(8,128)(2,1)S(1)} %get-tuple-element.282), channel_id=1, source_target_pairs={{0,1},{1,0},{2,3},{3,2},{4,5},{5,4},{6,7},{7,6},{8,9},{9,8},{10,11... | collective-permute-start | bytes 1572872 | tf_op jit(solution)/shard_map/ppermute | solution.py:194
  69.3 38.7 %collective-permute-start.18 = (bf16[2,2,1,1,64,1024]{5,4,3,2,1,0:T(8,128)(2,1)S(1)}, bf16[2,2,1,1,64,1024]{5,4,3,2,1,0:T(8,128)(2,1)S(1)}, u32[]{:S(2)}, u32[]{:S(2)}) collective-permute-start(bf16[2,2,1,1,64,1024]{5,4,3,2,1,0:T(8,128)(2,1)S(1)} %get-tuple-element.281), channel_id=1, source_target_pairs={{0,2},{1,3},{2,0},{3,1},{4,6},{5,7},{6,4},{7,5},{8,10},{9,11},{10,... | collective-permute-start | bytes 1572872 | tf_op jit(solution)/shard_map/ppermute | solution.py:194
  72.7 39.8 %collective-permute-start.8 = (bf16[2,2,2,1,64,1280]{5,4,3,2,1,0:T(8,128)(2,1)S(1)}, bf16[2,2,2,1,64,1280]{5,4,3,2,1,0:T(8,128)(2,1)S(1)}, u32[]{:S(2)}, u32[]{:S(2)}) collective-permute-start(bf16[2,2,2,1,64,1280]{5,4,3,2,1,0:T(8,128)(2,1)S(1)} %pad_maximum_fusion.16), channel_id=1, source_target_pairs={{0,1},{1,0},{2,3},{3,2},{4,5},{5,4},{6,7},{7,6},{8,9},{9,8},{10,11... | collective-permute-start | bytes 3932168 | tf_op jit(solution)/shard_map/ppermute | solution.py:194
  109.4 24.4 %collective-permute-start.15 = (bf16[2,2,1,2,64,1024]{5,4,3,2,1,0:T(8,128)(2,1)}, bf16[2,2,1,2,64,1024]{5,4,3,2,1,0:T(8,128)(2,1)}, u32[]{:S(2)}, u32[]{:S(2)}) collective-permute-start(bf16[2,2,1,2,64,1024]{5,4,3,2,1,0:T(8,128)(2,1)} %pad_maximum_fusion.22), channel_id=1, source_target_pairs={{0,2},{1,3},{2,0},{3,1},{4,6},{5,7},{6,4},{7,5},{8,10},{9,11},{10,... | collective-permute-start | bytes 3145736 | tf_op jit(solution)/shard_map/ppermute | solution.py:194
  111.0 47.6 %collective-permute-start.19 = (bf16[2,2,2,1,64,1024]{5,4,3,2,1,0:T(8,128)(2,1)}, bf16[2,2,2,1,64,1024]{5,4,3,2,1,0:T(8,128)(2,1)}, u32[]{:S(2)}, u32[]{:S(2)}) collective-permute-start(bf16[2,2,2,1,64,1024]{5,4,3,2,1,0:T(8,128)(2,1)} %pad_maximum_fusion.24), channel_id=1, source_target_pairs={{0,1},{1,0},{2,3},{3,2},{4,5},{5,4},{6,7},{7,6},{8,9},{9,8},{10,11... | collective-permute-start | bytes 3145736 | tf_op jit(solution)/shard_map/ppermute | solution.py:194
  114.4 23.6 %collective-permute-start.9 = (bf16[1024,1280]{1,0:T(8,128)(2,1)}, bf16[1024,1280]{1,0:T(8,128)(2,1)}, u32[]{:S(2)}, u32[]{:S(2)}) collective-permute-start(bf16[1024,1280]{1,0:T(8,128)(2,1)} %bitcast.21), channel_id=1, source_target_pairs={{0,16},{16,0},{1,17},{17,1},{2,18},{18,2},{3,19},{19,3},{4,20},{20... | collective-permute-start | bytes 7864328 | tf_op jit(solution)/shard_map/ppermute | solution.py:18
  135.4 27.3 %collective-permute-start.16 = (bf16[1024,1024]{1,0:T(8,128)(2,1)S(1)}, bf16[1024,1024]{1,0:T(8,128)(2,1)}, u32[]{:S(2)}, u32[]{:S(2)}) collective-permute-start(bf16[1024,1024]{1,0:T(8,128)(2,1)S(1)} %bitcast.435), channel_id=1, source_target_pairs={{0,16},{16,0},{1,17},{17,1},{2,18},{18,2},{3,19},{19,3},{4,20},{20... | collective-permute-start | bytes 6291464 | tf_op jit(solution)/shard_map/ppermute | solution.py:18
  162.6 33.4 %collective-permute-start.20 = (bf16[2048,512]{1,0:T(8,128)(2,1)}, bf16[2048,512]{1,0:T(8,128)(2,1)S(1)}, u32[]{:S(2)}, u32[]{:S(2)}) collective-permute-start(bf16[2048,512]{1,0:T(8,128)(2,1)} %bitcast.36), channel_id=1, source_target_pairs={{0,16},{16,0},{1,17},{17,1},{2,18},{18,2},{3,19},{19,3},{4,20},{20... | collective-permute-start | bytes 6291464 | tf_op jit(solution)/shard_map/ppermute | solution.py:18
  184.3 30.1 %collective-permute-start.11 = (bf16[2,2,2,1,64,1280]{5,4,3,2,1,0:T(8,128)(2,1)S(1)}, bf16[2,2,2,1,64,1280]{5,4,3,2,1,0:T(8,128)(2,1)S(1)}, u32[]{:S(2)}, u32[]{:S(2)}) collective-permute-start(bf16[2,2,2,1,64,1280]{5,4,3,2,1,0:T(8,128)(2,1)S(1)} %pad_maximum_fusion.17.refs_7_), channel_id=1, source_target_pairs={{0,1},{1,0},{2,3},{3,2},{4,5},{5,4},{6,7},{7,6},{8,9},{9,8},{10,11... | collective-permute-start | bytes 3932168 | tf_op jit(solution)/shard_map/ppermute | solution.py:194
  217.7 36.1 %collective-permute-start.24 = (bf16[2,2,1,2,64,1024]{5,4,3,2,1,0:T(8,128)(2,1)S(1)}, bf16[2,2,1,2,64,1024]{5,4,3,2,1,0:T(8,128)(2,1)}, u32[]{:S(2)}, u32[]{:S(2)}) collective-permute-start(bf16[2,2,1,2,64,1024]{5,4,3,2,1,0:T(8,128)(2,1)S(1)} %pad_maximum_fusion.23.refs_8_), channel_id=1, source_target_pairs={{0,2},{1,3},{2,0},{3,1},{4,6},{5,7},{6,4},{7,5},{8,10},{9,11},{10,... | collective-permute-start | bytes 3145736 | tf_op jit(solution)/shard_map/ppermute | solution.py:194
  220.2 37.8 %all-to-all-start.1 = ((bf16[4,128,1024]{2,1,0:T(8,128)(2,1)}), bf16[4,128,1024]{2,1,0:T(8,128)(2,1)}, u32[]{:S(2)}, u32[]{:S(2)}) async-start(bf16[4,128,1024]{2,1,0:T(8,128)(2,1)} %dynamic-slice_bitcast_fusion), calls=%async_computation.1 | async-start | bytes 2097152 | tf_op jit(solution)/shard_map/all_to_all | solution.py:35
  233.4 24.6 %collective-permute-start.30 = (bf16[2,2,2,1,64,1024]{5,4,3,2,1,0:T(8,128)(2,1)S(1)}, bf16[2,2,2,1,64,1024]{5,4,3,2,1,0:T(8,128)(2,1)}, u32[]{:S(2)}, u32[]{:S(2)}) collective-permute-start(bf16[2,2,2,1,64,1024]{5,4,3,2,1,0:T(8,128)(2,1)S(1)} %pad_maximum_fusion.26), channel_id=1, source_target_pairs={{0,1},{1,0},{2,3},{3,2},{4,5},{5,4},{6,7},{7,6},{8,9},{9,8},{10,11... | collective-permute-start | bytes 3145736 | tf_op jit(solution)/shard_map/ppermute | solution.py:194
  262.6 24.5 %collective-permute-start.31 = (bf16[2048,512]{1,0:T(8,128)(2,1)}, bf16[2048,512]{1,0:T(8,128)(2,1)}, u32[]{:S(2)}, u32[]{:S(2)}) collective-permute-start(bf16[2048,512]{1,0:T(8,128)(2,1)} %bitcast.62), channel_id=1, source_target_pairs={{0,16},{16,0},{1,17},{17,1},{2,18},{18,2},{3,19},{19,3},{4,20},{20... | collective-permute-start | bytes 6291464 | tf_op jit(solution)/shard_map/ppermute | solution.py:18
  323.3 30.5 %all-to-all-start.2 = ((bf16[4,128,1024]{2,1,0:T(8,128)(2,1)}), bf16[4,128,1024]{2,1,0:T(8,128)(2,1)}, u32[]{:S(2)}, u32[]{:S(2)}) async-start(bf16[4,128,1024]{2,1,0:T(8,128)(2,1)} %pad_maximum_fusion.27), calls=%async_computation.2 | async-start | bytes 2097152 | tf_op jit(solution)/shard_map/all_to_all | solution.py:60
  327.5 36.6 %collective-permute-start.32 = (bf16[128,2048]{1,0:T(8,128)(2,1)S(1)}, bf16[128,2048]{1,0:T(8,128)(2,1)S(1)}, u32[]{:S(2)}, u32[]{:S(2)}) collective-permute-start(bf16[128,2048]{1,0:T(8,128)(2,1)S(1)} %get-tuple-element.133), channel_id=1, source_target_pairs={{16,0},{17,1},{18,2},{19,3},{20,4},{21,5},{22,6},{23,7},{24,8},{25... | collective-permute-start | bytes 1572872 | tf_op jit(solution)/shard_map/ppermute | solution.py:747
  341.8 54.2 %collective-permute-start.34 = (bf16[2,2,2,64,1024]{4,3,0,1,2:T(8,128)(2,1)}, bf16[2,2,2,64,1024]{4,3,0,1,2:T(8,128)(2,1)}, u32[]{:S(2)}, u32[]{:S(2)}) collective-permute-start(bf16[2,2,2,64,1024]{4,3,0,1,2:T(8,128)(2,1)} %bitcast.400), channel_id=1, source_target_pairs={{0,2},{1,3},{2,0},{3,1},{4,6},{5,7},{6,4},{7,5},{8,10},{9,11},{10,... | collective-permute-start | bytes 3145736 | tf_op jit(solution)/shard_map/ppermute | solution.py:194
  348.5 47.6 %collective-permute-start.28 = (bf16[2,2,2,64,1024]{4,3,0,1,2:T(8,128)(2,1)}, bf16[2,2,2,64,1024]{4,3,0,1,2:T(8,128)(2,1)}, u32[]{:S(2)}, u32[]{:S(2)}) collective-permute-start(bf16[2,2,2,64,1024]{4,3,0,1,2:T(8,128)(2,1)} %bitcast.398), channel_id=1, source_target_pairs={{0,1},{1,0},{2,3},{3,2},{4,5},{5,4},{6,7},{7,6},{8,9},{9,8},{10,11... | collective-permute-start | bytes 3145736 | tf_op jit(solution)/shard_map/ppermute | solution.py:194
  353.8 47.9 %all-to-all-start.3 = ((bf16[4,128,1024]{2,1,0:T(8,128)(2,1)}), bf16[4,128,1024]{2,1,0:T(8,128)(2,1)}, u32[]{:S(2)}, u32[]{:S(2)}) async-start(bf16[4,128,1024]{2,1,0:T(8,128)(2,1)} %pad_maximum_fusion.28), calls=%async_computation.3 | async-start | bytes 2097152 | tf_op jit(solution)/shard_map/all_to_all | solution.py:60
  404.5 24.8 %collective-permute-start.40 = (bf16[2,2,64,1024]{3,2,0,1:T(8,128)(2,1)S(1)}, bf16[2,2,64,1024]{3,2,0,1:T(8,128)(2,1)S(1)}, u32[]{:S(2)}, u32[]{:S(2)}) collective-permute-start(bf16[2,2,64,1024]{3,2,0,1:T(8,128)(2,1)S(1)} %dynamic-slice_bitcast_fusion.6), channel_id=1, source_target_pairs={{0,2},{1,3},{2,0},{3,1},{4,6},{5,7},{6,4},{7,5},{8,10},{9,11},{10,... | collective-permute-start | bytes 1572872 | tf_op jit(solution)/shard_map/ppermute | solution.py:194
  410.4 41.4 %collective-permute-start.37 = (bf16[4,128,1024]{2,1,0:T(8,128)(2,1)}, bf16[4,128,1024]{2,1,0:T(8,128)(2,1)}, u32[]{:S(2)}, u32[]{:S(2)}) collective-permute-start(bf16[4,128,1024]{2,1,0:T(8,128)(2,1)} %broadcast_select_fusion.26), channel_id=1, source_target_pairs={{0,16},{16,0},{1,17},{17,1},{2,18},{18,2},{3,19},{19,3},{4,20},{20... | collective-permute-start | bytes 3145736 | tf_op jit(solution)/shard_map/ppermute | solution.py:18
  423.2 39.6 %collective-permute-start.42 = (bf16[1024,1280]{1,0:T(8,128)(2,1)}, bf16[1024,1280]{1,0:T(8,128)(2,1)}, u32[]{:S(2)}, u32[]{:S(2)}) collective-permute-start(bf16[1024,1280]{1,0:T(8,128)(2,1)} %convolution_convert_fusion.1), channel_id=1, source_target_pairs={{0,16},{16,0},{1,17},{17,1},{2,18},{18,2},{3,19},{19,3},{4,20},{20... | collective-permute-start | bytes 7864328 | tf_op jit(solution)/shard_map/ppermute | solution.py:18
  429.3 25.6 %collective-permute-start.44 = (bf16[2048,512]{1,0:T(8,128)(2,1)}, bf16[2048,512]{1,0:T(8,128)(2,1)}, u32[]{:S(2)}, u32[]{:S(2)}) collective-permute-start(bf16[2048,512]{1,0:T(8,128)(2,1)} %convolution_convert_fusion.2), channel_id=1, source_target_pairs={{0,16},{16,0},{1,17},{17,1},{2,18},{18,2},{3,19},{19,3},{4,20},{20... | collective-permute-start | bytes 6291464 | tf_op jit(solution)/shard_map/ppermute | solution.py:18
  439.3 103.8 %all-to-all-start.4 = ((bf16[4,128,1024]{2,1,0:T(8,128)(2,1)}), bf16[4,128,1024]{2,1,0:T(8,128)(2,1)}, u32[]{:S(2)}, u32[]{:S(2)}) async-start(bf16[4,128,1024]{2,1,0:T(8,128)(2,1)} %pad_maximum_fusion.29), calls=%async_computation.4 | async-start | bytes 2097152 | tf_op jit(solution)/shard_map/all_to_all | solution.py:60
  448.9 37.8 %collective-permute-start.46 = (bf16[64,2048]{1,0:T(8,128)(2,1)S(1)}, bf16[64,2048]{1,0:T(8,128)(2,1)S(1)}, u32[]{:S(2)}, u32[]{:S(2)}) collective-permute-start(bf16[64,2048]{1,0:T(8,128)(2,1)S(1)} %dynamic-slice_bitcast_fusion.19), channel_id=1, source_target_pairs={{0,8},{4,12},{8,0},{12,4},{1,9},{5,13},{9,1},{13,5},{2,10},{6,14},... | collective-permute-start | bytes 786440 | tf_op jit(solution)/shard_map/ppermute | solution.py:194
  460.4 76.2 %collective-permute-start.51 = (bf16[2,2,2,64,1024]{4,3,0,1,2:T(8,128)(2,1)S(1)}, bf16[2,2,2,64,1024]{4,3,0,1,2:T(8,128)(2,1)}, u32[]{:S(2)}, u32[]{:S(2)}) collective-permute-start(bf16[2,2,2,64,1024]{4,3,0,1,2:T(8,128)(2,1)S(1)} %bitcast.442), channel_id=1, source_target_pairs={{0,1},{1,0},{2,3},{3,2},{4,5},{5,4},{6,7},{7,6},{8,9},{9,8},{10,11... | collective-permute-start | bytes 3145736 | tf_op jit(solution)/shard_map/ppermute | solution.py:194
  498.9 37.7 %collective-permute-start.50 = (bf16[2,2,64,640]{3,2,1,0:T(8,128)(2,1)S(1)}, bf16[2,2,64,640]{3,2,1,0:T(8,128)(2,1)S(1)}, u32[]{:S(2)}, u32[]{:S(2)}) collective-permute-start(bf16[2,2,64,640]{3,2,1,0:T(8,128)(2,1)S(1)} %dynamic-slice_bitcast_fusion.16), channel_id=1, source_target_pairs={{0,1},{1,0},{2,3},{3,2},{4,5},{5,4},{6,7},{7,6},{8,9},{9,8},{10,11... | collective-permute-start | bytes 983048 | tf_op jit(solution)/shard_map/ppermute | solution.py:194
  500.1 36.5 %collective-permute-start.49 = (bf16[2,2,64,640]{3,2,1,0:T(8,128)(2,1)S(1)}, bf16[2,2,64,640]{3,2,1,0:T(8,128)(2,1)}, u32[]{:S(2)}, u32[]{:S(2)}) collective-permute-start(bf16[2,2,64,640]{3,2,1,0:T(8,128)(2,1)S(1)} %dynamic-slice_bitcast_fusion.17), channel_id=1, source_target_pairs={{0,2},{1,3},{2,0},{3,1},{4,6},{5,7},{6,4},{7,5},{8,10},{9,11},{10,... | collective-permute-start | bytes 983048 | tf_op jit(solution)/shard_map/ppermute | solution.py:194
  505.1 35.5 %collective-permute-start.52 = (bf16[2,2,2,64,1024]{4,3,0,1,2:T(8,128)(2,1)}, bf16[2,2,2,64,1024]{4,3,0,1,2:T(8,128)(2,1)}, u32[]{:S(2)}, u32[]{:S(2)}) collective-permute-start(bf16[2,2,2,64,1024]{4,3,0,1,2:T(8,128)(2,1)} %bitcast.399), channel_id=1, source_target_pairs={{0,2},{1,3},{2,0},{3,1},{4,6},{5,7},{6,4},{7,5},{8,10},{9,11},{10,... | collective-permute-start | bytes 3145736 | tf_op jit(solution)/shard_map/ppermute | solution.py:194
  552.8 28.9 %collective-permute-start.55 = (bf16[1024,1280]{1,0:T(8,128)(2,1)S(1)}, bf16[1024,1280]{1,0:T(8,128)(2,1)S(1)}, u32[]{:S(2)}, u32[]{:S(2)}) collective-permute-start(bf16[1024,1280]{1,0:T(8,128)(2,1)S(1)} %convolution_convert_fusion), channel_id=1, source_target_pairs={{0,16},{16,0},{1,17},{17,1},{2,18},{18,2},{3,19},{19,3},{4,20},{20... | collective-permute-start | bytes 7864328 | tf_op jit(solution)/shard_map/ppermute | solution.py:18
  625.6 29.2 %all-to-all-start.5 = ((bf16[4,128,1024]{2,1,0:T(8,128)(2,1)}), bf16[4,128,1024]{2,1,0:T(8,128)(2,1)S(1)}, u32[]{:S(2)}, u32[]{:S(2)}) async-start(bf16[4,128,1024]{2,1,0:T(8,128)(2,1)} %pad_maximum_fusion.30), calls=%async_computation.5 | async-start | bytes 2097152 | tf_op jit(solution)/shard_map/all_to_all | solution.py:60
  (160 other events, 1526.5 us)
